TPU v7x, 32 devices: a whole 2x2x4 slice. The times are simulated.
32 devices in a mesh: gx: 4 (over y, x), gy: 8 (over z, core).
Axes of the slice: x: 2, y: 2, z: 4, core: 2. Of those that a mesh axis runs over, the one named last changes fastest.
Arguments:
- prev_block: float32 [3, 8, 32, 64, 128], P(None, None, 'gx', 'gy'), may hold values from -20 to 20
- block: float32 [3, 8, 32, 64, 128], P(None, None, 'gx', 'gy'), may hold values from -20 to 20
- hop_seed: int32 [3, 32, 64, 128], P(None, 'gx', 'gy'), may hold values from 0 to 15
- levels: int32 [32, 64, 128], P('gx', 'gy'), may hold values from 0 to 15
- hop_table: float32 [3, 16, 3, 3], replicated, may hold values from -3 to 3
- onsite_table: float32 [16, 3], replicated, may hold values from -2 to 2
Outputs:
- next_block: float32 [3, 8, 32, 64, 128], P(None, None, 'gx', 'gy')
- alpha: float32 [8, 8], replicated
- beta: float32 [8, 8], replicated
All inputs are finite; a program needn't handle non-finite values.
Results may differ from a plain program's by a relative error of at most 0.0003.
Values sent between devices are 32-bit elements; how exact they have to be, the bound alone decides.
No kernel may reach another device: no remote copies, remote signals or barrier semaphores. Data moves between devices by JAX's collectives and lax.ppermute only.
A program may use at most 64 MiB of HBM per device.

v0:
```python
import jax
import jax.numpy as jnp
from jax import lax
from jax.sharding import PartitionSpec as P

HIGH = lax.Precision.HIGHEST


def extended(value, sides, width):
    for axis, dim in sides:
        count, length = (lax.axis_size(axis), value.shape[dim])
        up = [(i, (i + 1) % count) for i in range(count)]
        down = [(j, i) for i, j in up]
        last = lax.slice_in_dim(value, length - width, length, axis=dim)
        leading = lax.slice_in_dim(value, 0, width, axis=dim)
        before = lax.ppermute(last, axis, up)
        after = lax.ppermute(leading, axis, down)
        value = jnp.concatenate([before, value, after], axis=dim)
    return value


def passed_along(value, axis, steps):
    count = lax.axis_size(axis)
    pairs = [(source, (source + steps) % count) for source in range(count)]
    return lax.ppermute(value, axis, pairs)


def table_rows(table_flat, indices):
    entries = table_flat.shape[0]
    flat = indices.reshape(-1)
    onehot = (flat[None, :] == jnp.arange(entries, dtype=jnp.int32)[:, None]).astype(jnp.float32)
    picked = lax.dot_general(table_flat, onehot, (((0,), (0,)), ((), ())), precision=HIGH)
    return picked.reshape((table_flat.shape[1],) + indices.shape)


def hop_blocks(table_dir, seeds):
    orbs = table_dir.shape[1]
    picked = table_rows(table_dir.reshape(table_dir.shape[0], orbs * orbs), seeds)
    return picked.reshape((orbs, orbs) + seeds.shape)


def forward(bonds, field):
    orbs = field.shape[0]
    rows = []
    for left in range(orbs):
        acc = bonds[left, 0][None] * field[0]
        for right in range(1, orbs):
            acc = acc + bonds[left, right][None] * field[right]
        rows.append(acc)
    return jnp.stack(rows, axis=0)


def backward(bonds, field):
    orbs = field.shape[0]
    rows = []
    for right in range(orbs):
        acc = bonds[0, right][None] * field[0]
        for left in range(1, orbs):
            acc = acc + bonds[left, right][None] * field[left]
        rows.append(acc)
    return jnp.stack(rows, axis=0)


def onsite_image(block, levels, onsite_table):
    energy = table_rows(onsite_table, levels)
    return energy[:, None] * block


def apply_values(block, hop_seed, levels, hop_table, onsite_table):
    padded = extended(block, (("gx", 2), ("gy", 3)), 1)
    ahead = [padded[:, :, 2:, 1:-1], padded[:, :, 1:-1, 2:], jnp.roll(block, -1, axis=4)]
    behind = [padded[:, :, :-2, 1:-1], padded[:, :, 1:-1, :-2], jnp.roll(block, 1, axis=4)]
    edge_x = passed_along(hop_seed[0, -1:], "gx", 1)
    edge_y = passed_along(hop_seed[1, :, -1:], "gy", 1)
    seeds_behind = [
        jnp.concatenate([edge_x, hop_seed[0, :-1]], axis=0),
        jnp.concatenate([edge_y, hop_seed[1, :, :-1]], axis=1),
        jnp.roll(hop_seed[2], 1, axis=2),
    ]
    image = onsite_image(block, levels, onsite_table)
    for direction in range(3):
        image = image + forward(
            hop_blocks(hop_table[direction], hop_seed[direction]), ahead[direction]
        )
        image = image + backward(
            hop_blocks(hop_table[direction], seeds_behind[direction]), behind[direction]
        )
    return image


def local_inner(left, right):
    total = None
    for orbit in range(left.shape[0]):
        flat_left = left[orbit].reshape(left.shape[1], -1)
        flat_right = right[orbit].reshape(right.shape[1], -1)
        part_sum = lax.dot_general(flat_left, flat_right, (((1,), (1,)), ((), ())), precision=HIGH)
        total = part_sum if total is None else total + part_sum
    return total


def apply_left(matrix, field):
    rows = []
    for orbit in range(field.shape[0]):
        flat = field[orbit].reshape(field.shape[1], -1)
        mixed = jnp.dot(matrix, flat, precision=HIGH)
        rows.append(mixed.reshape((matrix.shape[0],) + field.shape[2:]))
    return jnp.stack(rows, axis=0)


def combine(basis, coeffs):
    return apply_left(coeffs.T, basis)


def per_device(prev_block, block, hop_seed, levels, hop_table, onsite_table):
    count = (
        block.shape[0]
        * block.shape[2]
        * block.shape[3]
        * block.shape[4]
        * lax.axis_size("gx")
        * lax.axis_size("gy")
    )
    product = apply_values(block, hop_seed, levels, hop_table, onsite_table)
    basis = jnp.concatenate([prev_block, block], axis=1)
    width = block.shape[1]
    first = lax.psum(local_inner(basis, product), ("gx", "gy")) / count
    residual_one = product - combine(basis, first)
    second = lax.psum(local_inner(basis, residual_one), ("gx", "gy")) / count
    residual_two = residual_one - combine(basis, second)
    gram = lax.psum(local_inner(residual_two, residual_two), ("gx", "gy")) / count
    alpha = first[width:]
    lower = jnp.linalg.cholesky(gram)
    lower_inv = jax.scipy.linalg.solve_triangular(
        lower, jnp.eye(width, dtype=jnp.float32), lower=True
    )
    next_block = apply_left(lower_inv, residual_two)
    return (next_block, alpha, lower.T)


def solution(mesh):
    in_specs = (
        P(None, None, "gx", "gy", None),
        P(None, None, "gx", "gy", None),
        P(None, "gx", "gy", None),
        P("gx", "gy", None),
        P(),
        P(),
    )
    out_specs = (P(None, None, "gx", "gy", None), P(), P())
    return jax.shard_map(
        per_device, mesh=mesh, in_specs=in_specs, out_specs=out_specs, check_vma=False
    )
```

profile of v0, /device:TPU:0, one launch (start us, length us, event | category | flops | bytes accessed | tf_op | source)
XLA Modules:
  0.0 202.0 jit_solution(14701415599863294657)
XLA Ops:
  0.7 1.0 fusion.80
  2.3 2.9 %collective-permute-start.2 = (f32[3,8,1,8,128]{4,1,3,2,0:T(8,128)}, f32[3,8,1,8,128]{4,1,3,2,0:T(8,128)}, u32[]{:S(2)}, u32[]{:S(2)}) collective-permute-start(f32[3,8,1,8,128]{4,1,3,2,0:T(8,128)} %copy.105), channel_id=1, source_target_pairs={{0,8},{8,16},{16,24},{24,0},{1,9},{9,17},{17,25},{25,1},{2,10},{10... | collective-permute-start | bytes 294920 | tf_op jit(solution)/shard_map/ppermute | solution.py:16
  5.9 1.0 collective-permute-start
  6.9 1.4 slice.453
  8.3 1.3 slice_bitcast_fusion.72
  9.5 1.1 collective-permute-start.1
  11.4 1.1 fusion.79
  12.6 1.2 fusion.78
  16.4 1.6 copy.108
  18.0 1.3 copy.109
  20.5 1.4 copy.106
  21.9 1.3 copy.107
  26.1 1.8 multiply_add_fusion.2
  28.0 1.4 multiply_add_fusion.1
  29.5 1.1 multiply_add_fusion.4
  36.6 3.3 %collective-permute-start.3 = (f32[3,8,10,1,128]{4,1,3,2,0:T(8,128)}, f32[3,8,10,1,128]{4,1,3,2,0:T(8,128)}, u32[]{:S(2)}, u32[]{:S(2)}) collective-permute-start(f32[3,8,10,1,128]{4,1,3,2,0:T(8,128)} %get-tuple-element.33), channel_id=1, source_target_pairs={{1,0},{2,1},{3,2},{4,3},{5,4},{6,5},{7,6},{0,7},{9,8},{10,9},{11,1... | collective-permute-start | bytes 368648 | tf_op jit(solution)/shard_map/ppermute | solution.py:17
  39.8 1.1 fusion.76
  41.0 1.1 multiply_add_fusion.17
  42.0 1.0 multiply_add_fusion.14
  43.4 1.2 copy.45
  45.5 1.1 copy.83
  46.7 2.0 copy.47
  48.7 1.9 reshape_squeeze.23
  50.6 2.0 %copy.84 = f32[2,8,64,128]{3,2,1,0:T(8,128)} copy(f32[2,8,64,128]{3,1,2,0:T(8,128)} %bitcast.380) | data formatting | bytes 1048576
  52.8 1.2 multiply_add_fusion.8
  59.6 39.8 %psum.21 = f32[16,8]{0,1:T(8,128)S(1)} all-reduce(f32[16,8]{0,1:T(8,128)S(1)} %fusion.2), channel_id=1, replica_groups=mesh['gx'=4,'gy'=8] {'gx','gy'}, use_global_device_ids=true, to_apply=%region_0.1 | all-reduce | flops 128 | bytes 1024 | tf_op jit(solution)/shard_map/psum | solution.py:126
  101.5 2.7 %maximum_subtract_fusion = f32[3,8,8,8,128]{4,1,3,2,0:T(8,128)S(1)} fusion(f32[1,8,8,8,128]{4,1,3,2,0:T(8,128)S(1)} %convolution_bitcast_fusion.3, f32[1,8,8,8,128]{4,1,3,2,0:T(8,128)S(1)} %convolution_bitcast_fusion.4, f32[1,8,8,8,128]{4,1,3,2,0:T(8,128)S(1)} %convolution_bitcast_fusion.5, f32[1,8,8,8,128]{4,1,3,2,0:T(8,128)S(1)} %copy-done.13, ...), kind=kLoop, calls=%fused_computation.32 | loop fusion | flops 4325376 | bytes 7176192 | tf_op jit(solution)/shard_map/sub | solution.py:127
  106.6 40.6 %psum.22 = f32[16,8]{0,1:T(8,128)S(1)} all-reduce(f32[16,8]{0,1:T(8,128)S(1)} %fusion), channel_id=1, replica_groups=mesh['gx'=4,'gy'=8] {'gx','gy'}, use_global_device_ids=true, to_apply=%region_1.2 | all-reduce | flops 128 | bytes 1024 | tf_op jit(solution)/shard_map/psum | solution.py:128
  148.6 1.7 convolution_bitcast_fusion
  150.3 3.5 %maximum_subtract_fusion.1 = f32[3,8,8,8,128]{4,1,3,2,0:T(8,128)S(1)} fusion(f32[1,8,8,8,128]{4,1,3,2,0:T(8,128)S(1)} %convolution_bitcast_fusion, f32[1,8,8,8,128]{4,1,3,2,0:T(8,128)S(1)} %convolution_bitcast_fusion.1, f32[1,8,8,8,128]{4,1,3,2,0:T(8,128)S(1)} %convolution_bitcast_fusion.2, f32[1,8,8,8,128]{4,1,3,2,0:T(8,128)} %copy-done.37, ...), kind=kLoop, calls=%fused_computation.33 | loop fusion | flops 4915200 | bytes 7962624 | tf_op jit(solution)/shard_map/sub | solution.py:129
  155.8 39.7 %psum.23 = f32[8,8]{0,1:T(8,128)S(1)} all-reduce(f32[8,8]{0,1:T(8,128)S(1)} %fusion.5), channel_id=1, replica_groups=mesh['gx'=4,'gy'=8] {'gx','gy'}, use_global_device_ids=true, to_apply=%region_2.3 | all-reduce | flops 64 | bytes 512 | tf_op jit(solution)/shard_map/psum | solution.py:130
  199.6 1.0 copy.57
  (233 shorter events, 34.1 us)
Async XLA Ops:
  0.6 30.0 %copy-start = (f32[16,3]{0,1:T(4,128)S(1)}, f32[16,3]{0,1:T(4,128)}, u32[]{:S(2)}) copy-start(f32[16,3]{0,1:T(4,128)} %param.11) | copy-start | bytes 580
  0.6 10.8 %copy-start.1 = (f32[3,8,8,8,128]{4,3,2,1,0:T(8,128)S(1)}, f32[3,8,8,8,128]{4,3,2,1,0:T(8,128)}, u32[]{:S(2)}) copy-start(f32[3,8,8,8,128]{4,3,2,1,0:T(8,128)} %param.7) | copy-start | bytes 2359300
  2.3 31.1 %collective-permute-start.2 = (f32[3,8,1,8,128]{4,1,3,2,0:T(8,128)}, f32[3,8,1,8,128]{4,1,3,2,0:T(8,128)}, u32[]{:S(2)}, u32[]{:S(2)}) collective-permute-start(f32[3,8,1,8,128]{4,1,3,2,0:T(8,128)} %copy.105), channel_id=1, source_target_pairs={{0,8},{8,16},{16,24},{24,0},{1,9},{9,17},{17,25},{25,1},{2,10},{10... | collective-permute-start | bytes 294920 | tf_op jit(solution)/shard_map/ppermute | solution.py:16
  5.9 29.0 %collective-permute-start = (f32[3,8,1,8,128]{4,1,3,2,0:T(8,128)}, f32[3,8,1,8,128]{4,1,3,2,0:T(8,128)}, u32[]{:S(2)}, u32[]{:S(2)}) collective-permute-start(f32[3,8,1,8,128]{4,1,3,2,0:T(8,128)} %copy.104), channel_id=1, source_target_pairs={{8,0},{16,8},{24,16},{0,24},{9,1},{17,9},{25,17},{1,25},{10,2},{18... | collective-permute-start | bytes 294920 | tf_op jit(solution)/shard_map/ppermute | solution.py:17
  8.3 22.7 %collective-permute-start.4 = (s32[8,1,128]{2,0,1:T(8,128)}, s32[8,1,128]{2,0,1:T(8,128)}, u32[]{:S(2)}, u32[]{:S(2)}) collective-permute-start(s32[8,1,128]{2,0,1:T(8,128)} %bitcast.37), channel_id=1, source_target_pairs={{0,1},{1,2},{2,3},{3,4},{4,5},{5,6},{6,7},{7,0},{8,9},{9,10},{10,1... | collective-permute-start | bytes 12296 | tf_op jit(solution)/shard_map/ppermute | solution.py:25
  9.5 23.3 %collective-permute-start.1 = (s32[1,8,128]{2,1,0:T(8,128)}, s32[1,8,128]{2,1,0:T(8,128)S(1)}, u32[]{:S(2)}, u32[]{:S(2)}) collective-permute-start(s32[1,8,128]{2,1,0:T(8,128)} %slice_bitcast_fusion.72), channel_id=1, source_target_pairs={{0,8},{8,16},{16,24},{24,0},{1,9},{9,17},{17,25},{25,1},{2,10},{10... | collective-permute-start | bytes 12296 | tf_op jit(solution)/shard_map/ppermute | solution.py:25
  12.6 2.5 %copy-start.71 = (f32[3,16,3,3]{1,3,2,0:T(4,128)S(1)}, f32[3,16,3,3]{1,3,2,0:T(4,128)}, u32[]{:S(2)}) copy-start(f32[3,16,3,3]{1,3,2,0:T(4,128)} %param.10) | copy-start | bytes 5188
  15.6 2.3 %copy-start.34 = (f32[3,8,8,8,1]{4,3,2,1,0:T(8,128)S(1)}, f32[3,8,8,8,1]{4,3,2,1,0:T(8,128)}, u32[]{:S(2)}) copy-start(f32[3,8,8,8,1]{4,3,2,1,0:T(8,128)} %get-tuple-element.44) | copy-start | bytes 18436
  20.5 2.7 %copy-start.40 = (f32[3,8,8,8,128]{4,3,2,1,0:T(8,128)S(1)}, f32[3,8,8,8,128]{4,3,2,1,0:T(8,128)}, u32[]{:S(2)}) copy-start(f32[3,8,8,8,128]{4,3,2,1,0:T(8,128)} %param.6) | copy-start | bytes 2359300
  25.4 2.5 %copy-start.3 = (f32[3,8,8,8,1]{4,1,3,2,0:T(8,128)S(1)}, f32[3,8,8,8,1]{4,1,3,2,0:T(8,128)}, u32[]{:S(2)}) copy-start(f32[3,8,8,8,1]{4,1,3,2,0:T(8,128)} %copy.106) | copy-start | bytes 18436
  25.4 2.4 %copy-start.4 = (f32[3,8,8,8,127]{4,1,3,2,0:T(8,128)S(1)}, f32[3,8,8,8,127]{4,1,3,2,0:T(8,128)}, u32[]{:S(2)}) copy-start(f32[3,8,8,8,127]{4,1,3,2,0:T(8,128)} %copy.107) | copy-start | bytes 2340868
  25.4 2.4 %copy-start.54 = (f32[8,8,128]{2,1,0:T(8,128)S(1)}, f32[8,8,128]{2,1,0:T(8,128)}, u32[]{:S(2)}) copy-start(f32[8,8,128]{2,1,0:T(8,128)} %get-tuple-element.57) | copy-start | bytes 98308
  25.5 2.4 %copy-start.55 = (f32[8,8,128]{2,1,0:T(8,128)S(1)}, f32[8,8,128]{2,1,0:T(8,128)}, u32[]{:S(2)}) copy-start(f32[8,8,128]{2,1,0:T(8,128)} %get-tuple-element.58) | copy-start | bytes 98308
  25.5 2.4 %copy-start.56 = (f32[8,8,128]{2,1,0:T(8,128)S(1)}, f32[8,8,128]{2,1,0:T(8,128)}, u32[]{:S(2)}) copy-start(f32[8,8,128]{2,1,0:T(8,128)} %get-tuple-element.59) | copy-start | bytes 98308
  25.5 2.4 %copy-start.63 = (f32[8,8,128]{2,1,0:T(8,128)S(1)}, f32[8,8,128]{2,1,0:T(8,128)}, u32[]{:S(2)}) copy-start(f32[8,8,128]{2,1,0:T(8,128)} %get-tuple-element.69) | copy-start | bytes 98308
  25.5 2.4 %copy-start.64 = (f32[8,8,128]{2,1,0:T(8,128)S(1)}, f32[8,8,128]{2,1,0:T(8,128)}, u32[]{:S(2)}) copy-start(f32[8,8,128]{2,1,0:T(8,128)} %get-tuple-element.70) | copy-start | bytes 98308
  25.5 2.4 %copy-start.65 = (f32[8,8,128]{2,1,0:T(8,128)S(1)}, f32[8,8,128]{2,1,0:T(8,128)}, u32[]{:S(2)}) copy-start(f32[8,8,128]{2,1,0:T(8,128)} %get-tuple-element.71) | copy-start | bytes 98308
  35.8 5.1 %copy-start.38 = (f32[3,8,10,8,128]{4,1,3,2,0:T(8,128)}, f32[3,8,10,8,128]{4,1,3,2,0:T(8,128)S(1)}, u32[]{:S(2)}) copy-start(f32[3,8,10,8,128]{4,1,3,2,0:T(8,128)S(1)} %get-tuple-element.112) | copy-start | bytes 2949124
  36.6 16.1 %collective-permute-start.3 = (f32[3,8,10,1,128]{4,1,3,2,0:T(8,128)}, f32[3,8,10,1,128]{4,1,3,2,0:T(8,128)}, u32[]{:S(2)}, u32[]{:S(2)}) collective-permute-start(f32[3,8,10,1,128]{4,1,3,2,0:T(8,128)} %get-tuple-element.33), channel_id=1, source_target_pairs={{1,0},{2,1},{3,2},{4,3},{5,4},{6,5},{7,6},{0,7},{9,8},{10,9},{11,1... | collective-permute-start | bytes 368648 | tf_op jit(solution)/shard_map/ppermute | solution.py:17
  39.8 12.8 %collective-permute-start.5 = (f32[3,8,10,1,128]{4,1,3,2,0:T(8,128)}, f32[3,8,10,1,128]{4,1,3,2,0:T(8,128)}, u32[]{:S(2)}, u32[]{:S(2)}) collective-permute-start(f32[3,8,10,1,128]{4,1,3,2,0:T(8,128)} %get-tuple-element.32), channel_id=1, source_target_pairs={{0,1},{1,2},{2,3},{3,4},{4,5},{5,6},{6,7},{7,0},{8,9},{9,10},{10,1... | collective-permute-start | bytes 368648 | tf_op jit(solution)/shard_map/ppermute | solution.py:16
  54.0 3.3 %copy-start.28 = (f32[1,8,8,8,128]{4,1,3,2,0:T(8,128)}, f32[1,8,8,8,128]{4,1,3,2,0:T(8,128)S(1)}, u32[]{:S(2)}) copy-start(f32[1,8,8,8,128]{4,1,3,2,0:T(8,128)S(1)} %get-tuple-element.13) | copy-start | bytes 786436
  54.0 3.3 %copy-start.29 = (f32[1,8,8,8,128]{4,1,3,2,0:T(8,128)}, f32[1,8,8,8,128]{4,1,3,2,0:T(8,128)S(1)}, u32[]{:S(2)}) copy-start(f32[1,8,8,8,128]{4,1,3,2,0:T(8,128)S(1)} %get-tuple-element.28) | copy-start | bytes 786436
  54.6 2.7 %copy-start.30 = (f32[1,8,8,8,128]{4,1,3,2,0:T(8,128)}, f32[1,8,8,8,128]{4,1,3,2,0:T(8,128)S(1)}, u32[]{:S(2)}) copy-start(f32[1,8,8,8,128]{4,1,3,2,0:T(8,128)S(1)} %get-tuple-element.48) | copy-start | bytes 786436
  54.6 2.7 %copy-start.31 = (f32[1,8,8,8,128]{4,1,3,2,0:T(8,128)}, f32[1,8,8,8,128]{4,1,3,2,0:T(8,128)S(1)}, u32[]{:S(2)}) copy-start(f32[1,8,8,8,128]{4,1,3,2,0:T(8,128)S(1)} %get-tuple-element.49) | copy-start | bytes 786436
  54.6 2.7 %copy-start.32 = (f32[1,8,8,8,128]{4,1,3,2,0:T(8,128)}, f32[1,8,8,8,128]{4,1,3,2,0:T(8,128)S(1)}, u32[]{:S(2)}) copy-start(f32[1,8,8,8,128]{4,1,3,2,0:T(8,128)S(1)} %get-tuple-element.121) | copy-start | bytes 786436
  54.6 2.7 %copy-start.33 = (f32[1,8,8,8,128]{4,1,3,2,0:T(8,128)}, f32[1,8,8,8,128]{4,1,3,2,0:T(8,128)S(1)}, u32[]{:S(2)}) copy-start(f32[1,8,8,8,128]{4,1,3,2,0:T(8,128)S(1)} %get-tuple-element.122) | copy-start | bytes 786436
  100.1 4.2 %copy-start.35 = (f32[1,8,8,8,128]{4,1,3,2,0:T(8,128)}, f32[1,8,8,8,128]{4,1,3,2,0:T(8,128)S(1)}, u32[]{:S(2)}) copy-start(f32[1,8,8,8,128]{4,1,3,2,0:T(8,128)S(1)} %convolution_bitcast_fusion.5) | copy-start | bytes 786436
  100.8 3.5 %copy-start.36 = (f32[1,8,8,8,128]{4,1,3,2,0:T(8,128)}, f32[1,8,8,8,128]{4,1,3,2,0:T(8,128)S(1)}, u32[]{:S(2)}) copy-start(f32[1,8,8,8,128]{4,1,3,2,0:T(8,128)S(1)} %convolution_bitcast_fusion.4) | copy-start | bytes 786436
  101.5 2.8 %copy-start.37 = (f32[1,8,8,8,128]{4,1,3,2,0:T(8,128)}, f32[1,8,8,8,128]{4,1,3,2,0:T(8,128)S(1)}, u32[]{:S(2)}) copy-start(f32[1,8,8,8,128]{4,1,3,2,0:T(8,128)S(1)} %convolution_bitcast_fusion.3) | copy-start | bytes 786436
  106.6 43.7 %copy-start.8 = (f32[1,8,8,8,128]{4,1,3,2,0:T(8,128)S(1)}, f32[1,8,8,8,128]{4,1,3,2,0:T(8,128)}, u32[]{:S(2)}) copy-start(f32[1,8,8,8,128]{4,1,3,2,0:T(8,128)} %get-tuple-element.9) | copy-start | bytes 786436
  106.6 43.7 %copy-start.11 = (f32[1,8,8,8,128]{4,1,3,2,0:T(8,128)S(1)}, f32[1,8,8,8,128]{4,1,3,2,0:T(8,128)}, u32[]{:S(2)}) copy-start(f32[1,8,8,8,128]{4,1,3,2,0:T(8,128)} %get-tuple-element.21) | copy-start | bytes 786436
  106.6 43.7 %copy-start.14 = (f32[1,8,8,8,128]{4,1,3,2,0:T(8,128)S(1)}, f32[1,8,8,8,128]{4,1,3,2,0:T(8,128)}, u32[]{:S(2)}) copy-start(f32[1,8,8,8,128]{4,1,3,2,0:T(8,128)} %get-tuple-element.22) | copy-start | bytes 786436
  (46 other events, 75.9 us)
where the time goes:
time: 203 us; the launch traced here: 202 us
  blocking collectives  120 us (59%)
  local copies, waits for them, and re-layouts  38 us (19%)
  other arithmetic  18.6 us (9%)
  matrix products  15.1 us (7%)
  starting transfers between devices  8.23 us (4%)
    psum x1, blocking collectives, per_device(): second = lax.psum(local_inner(basis, residual_one), ('gx', 'gy')) / count  40.6 us
    psum x1, blocking collectives, per_device(): first = lax.psum(local_inner(basis, product), ('gx', 'gy')) / count  39.8 us
    psum x1, blocking collectives, per_device(): lax.psum(local_inner(residual_two, residual_two), ('gx', 'gy')) / count  39.7 us
    unnamed x171, local copies, waits for them, and re-layouts  17.2 us
    dot_general x9, matrix products, local_inner(): lax.dot_general(flat_left, flat_right, (((1,), (1,)), ((), ())), precisio...  6.55 us
    dot_general x9, matrix products, apply_left(): mixed = jnp.dot(matrix, flat, precision=HIGH)  6.01 us
    add x5, other arithmetic, backward(): acc = acc + bonds[left, right][None] * field[left]  5.72 us
    slice x4, local copies, waits for them, and re-layouts, local_inner(): flat_left = left[orbit].reshape(left.shape[1], -1)  4.51 us
  transfers between devices with their start and end apart: 6, of which 0 were waited for; matrix products, arithmetic and copies ran while one was open for 19% of the time, Pallas kernels for 0%

commit v1 on v0

v1 whole, which is shorter than its diff:
```python
import jax
import jax.numpy as jnp
from jax import lax
from jax.experimental import pallas as pl
from jax.experimental.pallas import tpu as pltpu
from jax.sharding import PartitionSpec as P

HIGH = lax.Precision.HIGHEST
F32 = jnp.float32
BF16 = jnp.bfloat16
LANES = 128
ROWS = 8
PARAMS = dict(vmem_limit_bytes=32 * 1024 * 1024)


def split(value):
    high = value.astype(BF16)
    low = (value - high.astype(F32)).astype(BF16)
    return high, low


def iota(shape, dim):
    return lax.broadcasted_iota(jnp.int32, shape, dim)


def dot(left, right, dims, precision=None):
    return lax.dot_general(
        left, right, (dims, ((), ())), precision=precision, preferred_element_type=F32
    )


def pick(table_ref, row, index):
    entries = jnp.broadcast_to(table_ref[row : row + 1, :], index.shape)
    return jnp.take_along_axis(entries, index, axis=1)


def bonds_of(table_ref, direction, index, orbs):
    base = direction * orbs * orbs
    return [
        [pick(table_ref, base + a * orbs + b, index) for b in range(orbs)] for a in range(orbs)
    ]


def times(bonds, field):
    return [sum(bonds[a][b] * field[b] for b in range(len(field))) for a in range(len(field))]


def times_transposed(bonds, field):
    return [sum(bonds[a][b] * field[a] for a in range(len(field))) for b in range(len(field))]


def pack_kernel(block_ref, seed_ref, xup_ref, xdown_ref, yup_ref, ydown_ref):
    orbs, width, nx, ny, _ = block_ref.shape
    for o in range(orbs):
        for n in range(width):
            spot = o * width + n
            xup_ref[spot] = block_ref[o, n, nx - 1]
            xdown_ref[spot] = block_ref[o, n, 0]
            yup_ref[spot] = block_ref[o, n, :, ny - 1, :]
            ydown_ref[spot] = block_ref[o, n, :, 0, :]
    xup_ref[orbs * width] = seed_ref[0, nx - 1].astype(F32)
    yup_ref[orbs * width] = seed_ref[1, :, ny - 1, :].astype(F32)


def small_sums(total, copies):
    rows, columns = total.shape
    same = (iota((rows, columns), 0) % ROWS) == (iota((rows, columns), 1) % ROWS)
    kept = jnp.where(same, total, 0.0)
    return kept.reshape(rows // ROWS, ROWS, columns).sum(axis=1)


def interior_kernel(
    prev_ref, block_ref, seed_ref, level_ref, table_ref, part_ref, high_ref, low_ref, gram_ref
):
    orbs, width, nx, ny, nz = block_ref.shape
    row = iota((ny, nz), 0)
    side = width * ny
    gram_ref[...] = jnp.zeros(gram_ref.shape, F32)

    def onsite(x, carry):
        index = [seed_ref[d, x] for d in range(3)]
        energy = [pick(table_ref, 3 * orbs * orbs + o, level_ref[x]) for o in range(orbs)]
        bond_y = bonds_of(table_ref, 1, index[1], orbs)
        bond_z = bonds_of(table_ref, 2, index[2], orbs)
        for n in range(width):
            here = [block_ref[o, n, x] for o in range(orbs)]
            image = [energy[o] * here[o] for o in range(orbs)]
            ahead = [jnp.where(row == ny - 1, 0.0, pltpu.roll(v, ny - 1, 0)) for v in here]
            image = [a + b for a, b in zip(image, times(bond_y, ahead))]
            carried = times_transposed(bond_y, here)
            image = [
                a + jnp.where(row == 0, 0.0, pltpu.roll(b, 1, 0)) for a, b in zip(image, carried)
            ]
            ahead = [pltpu.roll(v, nz - 1, 1) for v in here]
            image = [a + b for a, b in zip(image, times(bond_z, ahead))]
            carried = times_transposed(bond_z, here)
            image = [a + pltpu.roll(b, 1, 1) for a, b in zip(image, carried)]
            for o in range(orbs):
                part_ref[o, n, x] = image[o]
        return carry

    lax.fori_loop(0, nx, onsite, 0)

    def along_x(x, carry):
        bonds = bonds_of(table_ref, 0, seed_ref[0, x], orbs)
        for n in range(width):
            here = [block_ref[o, n, x] for o in range(orbs)]
            ahead = [block_ref[o, n, x + 1] for o in range(orbs)]
            forward = times(bonds, ahead)
            back = times_transposed(bonds, here)
            for o in range(orbs):
                part_ref[o, n, x] += forward[o]
                part_ref[o, n, x + 1] += back[o]
        return carry

    lax.fori_loop(0, nx - 1, along_x, 0)

    def products(pair, carry):
        for o in range(orbs):
            highs, lows = [], []
            for half in range(2):
                x = 2 * pair + half
                basis = jnp.concatenate(
                    [prev_ref[o, :, x].reshape(side, nz), block_ref[o, :, x].reshape(side, nz)], 0
                )
                high, low = split(basis)
                high_ref[o, x] = high
                low_ref[o, x] = low
                highs.append(high)
                lows.append(low)
            high = jnp.concatenate(highs, 1)
            low = jnp.concatenate(lows, 1)
            gram_ref[...] += (
                dot(high, high, ((1,), (1,)))
                + dot(high, low, ((1,), (1,)))
                + dot(low, high, ((1,), (1,)))
            )
        return carry

    lax.fori_loop(0, nx // 2, products, 0)


def halo_kernel(
    part_ref,
    seed_ref,
    table_ref,
    xlow_ref,
    xhigh_ref,
    ylow_ref,
    yhigh_ref,
    high_ref,
    low_ref,
    gram_ref,
    phigh_ref,
    plow_ref,
    sums_ref,
    image_ref,
    total_ref,
):
    orbs, width, nx, ny, nz = part_ref.shape
    side = width * ny
    last = orbs * width
    image_ref[...] = part_ref[...]

    bond_x = bonds_of(table_ref, 0, seed_ref[0, nx - 1], orbs)
    bond_xlow = bonds_of(table_ref, 0, xlow_ref[last].astype(jnp.int32), orbs)
    for n in range(width):
        forward = times(bond_x, [xhigh_ref[o * width + n] for o in range(orbs)])
        back = times_transposed(bond_xlow, [xlow_ref[o * width + n] for o in range(orbs)])
        for o in range(orbs):
            image_ref[o, n, nx - 1] += forward[o]
            image_ref[o, n, 0] += back[o]
    bond_y = bonds_of(table_ref, 1, seed_ref[1, :, ny - 1, :], orbs)
    bond_ylow = bonds_of(table_ref, 1, ylow_ref[last].astype(jnp.int32), orbs)
    for n in range(width):
        forward = times(bond_y, [yhigh_ref[o * width + n] for o in range(orbs)])
        back = times_transposed(bond_ylow, [ylow_ref[o * width + n] for o in range(orbs)])
        for o in range(orbs):
            image_ref[o, n, :, ny - 1, :] += forward[o]
            image_ref[o, n, :, 0, :] += back[o]

    total_ref[...] = jnp.zeros(total_ref.shape, F32)

    def products(pair, carry):
        for o in range(orbs):
            ins = [[], [], [], []]
            for half in range(2):
                x = 2 * pair + half
                high, low = split(image_ref[o, :, x].reshape(side, nz))
                phigh_ref[o, x] = high
                plow_ref[o, x] = low
                for group, value in zip(ins, (high, low, high_ref[o, x], low_ref[o, x])):
                    group.append(value)
            high, low, bhigh, blow = (jnp.concatenate(group, 1) for group in ins)
            both = jnp.concatenate([high, low], 0)
            total_ref[...] += dot(jnp.concatenate([bhigh, high], 0), both, ((1,), (1,))) + dot(
                jnp.concatenate([blow, low], 0), both, ((1,), (1,))
            )
        return carry

    lax.fori_loop(0, nx // 2, products, 0)

    first = small_sums(total_ref[...], 3)
    second = small_sums(gram_ref[...], 2)
    parts = [first[i * width : (i + 1) * width] for i in range(3)]
    parts += [second[i * width : (i + 1) * width] for i in range(2)]
    stacked = jnp.concatenate(parts, 1)
    spots = iota((LANES, LANES), 0)
    lanes = iota((LANES, LANES), 1)
    maps = []
    for i in range(3):
        maps.append(jnp.where(lanes == width * i + (spots // ny) % width, 1.0, 0.0))
    for i in range(2):
        maps.append(jnp.where(lanes == width * (3 + 2 * i) + spots // ny, 1.0, 0.0))
    sums = dot(stacked, jnp.concatenate(maps, 0), ((1,), (0,)), HIGH)
    half = width // 2
    folded = sums[:half] + pltpu.roll(sums, LANES // 2, 1)[half:]
    sums_ref[...] = jnp.broadcast_to(folded[None], sums_ref.shape)


def final_kernel(count, sums_ref, high_ref, low_ref, phigh_ref, plow_ref, next_ref, alpha_ref, beta_ref):
    orbs, nx, side, nz = phigh_ref.shape
    width = side // ROWS
    folded = jnp.sum(sums_ref[...], axis=0) / count
    sums = jnp.concatenate([folded, pltpu.roll(folded, LANES // 2, 1)], 0)
    first = jnp.concatenate([sums[:, 0:width], sums[:, width : 2 * width]], 0)
    norms = sums[:, 2 * width : 3 * width]
    metric = jnp.concatenate([sums[:, 3 * width : 5 * width], sums[:, 5 * width : 7 * width]], 0)
    alpha_ref[...] = first[width:]
    eye = jnp.where(iota((width, width), 0) == iota((width, width), 1), 1.0, 0.0)
    turned = dot(eye, first, ((1,), (1,)), HIGH)
    coeffs = 2.0 * turned - dot(turned, metric, ((1,), (0,)), HIGH)
    rest = turned - dot(coeffs, metric, ((1,), (0,)), HIGH)
    gram = norms - dot(
        jnp.concatenate([turned, coeffs], 1),
        jnp.concatenate([coeffs, rest], 1),
        ((1,), (1,)),
        HIGH,
    )
    pad = jnp.zeros((width, LANES - 4 * width), F32)
    table = jnp.concatenate([gram, eye, -coeffs, pad], 1)
    rows = iota((width, LANES), 0)
    scale = jnp.ones((width, LANES), F32)
    for k in range(width):
        pivot = jnp.broadcast_to(table[k : k + 1, k : k + 1], (width, LANES))
        column = jnp.broadcast_to(table[:, k : k + 1], (width, LANES))
        line = jnp.broadcast_to(table[k : k + 1, :], (width, LANES))
        table = jnp.where(rows > k, table - column / pivot * line, table)
        scale = jnp.where(rows == k, lax.rsqrt(pivot), scale)
    table = table * scale
    keep = iota((width, width), 0) <= iota((width, width), 1)
    beta_ref[...] = jnp.where(keep, table[:, :width], 0.0)
    lanes = iota((width, LANES), 1)
    basis_part = jnp.take_along_axis(table, 2 * width + lanes // ROWS, axis=1)
    product_part = jnp.take_along_axis(table, width + (lanes // ROWS) % width, axis=1)

    def spread(value, columns):
        grown = jnp.broadcast_to(value[:, None, :], (width, ROWS, LANES)).reshape(side, LANES)
        same = iota((side, LANES), 0) % ROWS == iota((side, LANES), 1) % ROWS
        return jnp.where(same, grown, 0.0)[:, :columns]

    mixed = jnp.concatenate([spread(basis_part, LANES), spread(product_part, side)], 1)
    mixed_high, mixed_low = split(mixed)

    def combine(pair, carry):
        for o in range(orbs):
            highs, lows = [], []
            for half in range(2):
                x = 2 * pair + half
                highs.append(jnp.concatenate([high_ref[o, x], phigh_ref[o, x]], 0))
                lows.append(jnp.concatenate([low_ref[o, x], plow_ref[o, x]], 0))
            high = jnp.concatenate(highs, 1)
            low = jnp.concatenate(lows, 1)
            dims = ((1,), (0,))
            out = dot(mixed_high, high, dims) + dot(mixed_low, high, dims) + dot(mixed_high, low, dims)
            for half in range(2):
                x = 2 * pair + half
                next_ref[o, :, x] = out[:, half * nz : (half + 1) * nz].reshape(width, ROWS, nz)
        return carry

    lax.fori_loop(0, nx // 2, combine, 0)


def shifted(value, axis, steps):
    count = lax.axis_size(axis)
    return lax.ppermute(value, axis, [(i, (i + steps) % count) for i in range(count)])


def per_device(prev_block, block, hop_seed, levels, hop_table, onsite_table):
    orbs, width, nx, ny, nz = block.shape
    devices = lax.axis_size("gx") * lax.axis_size("gy")
    count = orbs * nx * ny * nz * devices
    fields = orbs * width
    table = jnp.concatenate(
        [jnp.transpose(hop_table, (0, 2, 3, 1)).reshape(-1, hop_table.shape[1]), onsite_table.T], 0
    )
    table = jnp.pad(table, ((0, 0), (0, LANES - table.shape[1])))
    params = pltpu.CompilerParams(**PARAMS)

    xup, xdown, yup, ydown = pl.pallas_call(
        pack_kernel,
        out_shape=[
            pltpu.VMEM((fields + 1, ny, nz), F32),
            pltpu.VMEM((fields, ny, nz), F32),
            pltpu.VMEM((fields + 1, nx, nz), F32),
            pltpu.VMEM((fields, nx, nz), F32),
        ],
        compiler_params=params,
        name="pack",
    )(block, hop_seed)
    xlow = shifted(xup, "gx", 1)
    ylow = shifted(yup, "gy", 1)
    xhigh = shifted(xdown, "gx", -1)
    yhigh = shifted(ydown, "gy", -1)

    side = width * ny
    part, high, low, gram = pl.pallas_call(
        interior_kernel,
        out_shape=[
            pltpu.VMEM(block.shape, F32),
            pltpu.VMEM((orbs, nx, 2 * side, nz), BF16),
            pltpu.VMEM((orbs, nx, 2 * side, nz), BF16),
            pltpu.VMEM((2 * side, 2 * side), F32),
        ],
        compiler_params=params,
        cost_estimate=pl.CostEstimate(flops=10**8, bytes_accessed=4 * 10**6, transcendentals=0),
        name="interior",
    )(prev_block, block, hop_seed, levels, table)

    phigh, plow, sums = pl.pallas_call(
        halo_kernel,
        out_shape=[
            pltpu.VMEM((orbs, nx, side, nz), BF16),
            pltpu.VMEM((orbs, nx, side, nz), BF16),
            pltpu.VMEM((devices, width // 2, LANES), F32),
        ],
        scratch_shapes=[pltpu.VMEM(block.shape, F32), pltpu.VMEM((3 * side, 2 * side), F32)],
        compiler_params=params,
        name="halo",
    )(part, hop_seed, table, xlow, xhigh, ylow, yhigh, high, low, gram)

    sums = lax.all_to_all(sums, ("gx", "gy"), 0, 0)

    next_block, alpha, beta = pl.pallas_call(
        lambda *refs: final_kernel(count, *refs),
        out_shape=[
            jax.ShapeDtypeStruct(block.shape, F32),
            jax.ShapeDtypeStruct((width, width), F32),
            jax.ShapeDtypeStruct((width, width), F32),
        ],
        compiler_params=params,
        name="final",
    )(sums, high, low, phigh, plow)
    return next_block, alpha, beta


def solution(mesh):
    in_specs = (
        P(None, None, "gx", "gy", None),
        P(None, None, "gx", "gy", None),
        P(None, "gx", "gy", None),
        P("gx", "gy", None),
        P(),
        P(),
    )
    out_specs = (P(None, None, "gx", "gy", None), P(), P())
    return jax.shard_map(
        per_device, mesh=mesh, in_specs=in_specs, out_specs=out_specs, check_vma=False
    )
```

time: 203 us -> 35 us (0.17)
  blocking collectives: 120 us -> 13.4 us
  local copies, waits for them, and re-layouts: 38 us -> 3.91 us
  other arithmetic: 18.6 us -> 0.01 us
  matrix products: 15.1 us -> 0 us
  Pallas kernels: 0 us -> 9.89 us
    psum x3 -> x0, blocking collectives: 120 us -> none  [the longest x1 40.6 us: per_device(): second = lax.psum(local_inner(basis, residual_one), ('gx', 'gy')) / count]
    dot_general x25 -> x0, matrix products: 15 us -> none  [the longest x9 6.55 us: local_inner(): lax.dot_general(flat_left, flat_right, (((1,), (1,)), ((), ())), precisio...]
    unnamed x171 -> x14, local copies, waits for them, and re-layouts: 17.2 us -> 3.16 us
    all_to_all x0 -> x1, blocking collectives: none -> 13.4 us  [per_device(): sums = lax.all_to_all(sums, ('gx', 'gy'), 0, 0)]
    slice x12 -> x0, local copies, waits for them, and re-layouts: 10.1 us -> none  [the longest x4 4.51 us: local_inner(): flat_left = left[orbit].reshape(left.shape[1], -1)]
    pallas_call x0 -> x4, Pallas kernels: none -> 9.89 us  [the longest x1 3.9 us: per_device(): pl.pallas_call(lambda *refs: final_kernel(count, *refs), out_shape=[jax.S...]
    add x8 -> x0, other arithmetic: 8.87 us -> none  [the longest x5 5.72 us: backward(): acc = acc + bonds[left, right][None] * field[left]]
    sub x2 -> x0, other arithmetic: 6.21 us -> none  [the longest x1 3.47 us: per_device(): residual_two = residual_one - combine(basis, second)]
  transfers between devices with their start and end apart: 6 -> 4, of which waited for: 0 -> 1; matrix products, arithmetic and copies ran while one was open for 19% -> 2% of each run, Pallas kernels for 0% -> 11%
where the time goes in v1:
time: 35 us; the launch traced here: 34.7 us
  blocking collectives  13.4 us (38%)
  Pallas kernels  9.89 us (28%)
  starting transfers between devices  6.71 us (19%)
  local copies, waits for them, and re-layouts  3.91 us (11%)
  between operations  0.74 us (2%)
    all_to_all x1, blocking collectives, per_device(): sums = lax.all_to_all(sums, ('gx', 'gy'), 0, 0)  13.4 us
    ppermute x4, starting transfers between devices, shifted(): lax.ppermute(value, axis, [(i, (i + steps) % count) for i in range(count)])  6.71 us
    pallas_call x1, Pallas kernels, per_device(): pl.pallas_call(lambda *refs: final_kernel(count, *refs), out_shape=[jax.S...  3.9 us
    pallas_call x1, Pallas kernels, per_device(): pl.pallas_call(interior_kernel, out_shape=[pltpu.VMEM(block.shape, F32),...  3.8 us
    unnamed x14, local copies, waits for them, and re-layouts  3.16 us
    pallas_call x1, Pallas kernels, per_device(): pl.pallas_call(halo_kernel, out_shape=[pltpu.VMEM((orbs, nx, side, nz), B...  2.07 us
    reshape x1, local copies, waits for them, and re-layouts, per_device(): jnp.transpose(hop_table, (0, 2, 3, 1)).reshape(-1, hop_table.shape[1])  0.74 us
  transfers between devices with their start and end apart: 4, of which 1 were waited for; matrix products, arithmetic and copies ran while one was open for 2% of the time, Pallas kernels for 11%

profile of v1, /device:TPU:0, one launch (start us, length us, event | category | flops | bytes accessed | tf_op | source)
XLA Modules:
  0.0 34.7 jit_solution(1531401902411862515)
XLA Ops:
  0.6 0.0 copy-start
  0.6 1.1 %copy-done = f32[3,8,8,8,128]{4,3,2,1,0:T(8,128)S(1)} copy-done((f32[3,8,8,8,128]{4,3,2,1,0:T(8,128)S(1)}, f32[3,8,8,8,128]{4,3,2,1,0:T(8,128)}, u32[]{:S(2)}) %copy-start) | copy-done | bytes 786456
  1.8 0.0 copy-start.2
  1.8 0.9 %copy-done.2 = s32[3,8,8,128]{3,2,1,0:T(8,128)S(1)} copy-done((s32[3,8,8,128]{3,2,1,0:T(8,128)S(1)}, s32[3,8,8,128]{3,2,1,0:T(8,128)}, u32[]{:S(2)}) %copy-start.2) | copy-done | bytes 98328
  2.7 0.0 copy-start.1
  2.7 0.0 copy-start.3
  2.7 0.1 pack.1
  2.8 3.9 %collective-permute-start.1 = (f32[24,8,128]{2,1,0:T(8,128)S(1)}, f32[24,8,128]{2,1,0:T(8,128)S(1)}, u32[]{:S(2)}, u32[]{:S(2)}) collective-permute-start(f32[24,8,128]{2,1,0:T(8,128)S(1)} %get-tuple-element.16), channel_id=1, source_target_pairs={{0,24},{8,0},{16,8},{24,16},{1,25},{9,1},{17,9},{25,17},{2,26},{10... | collective-permute-start | bytes 294920 | tf_op jit(solution)/shard_map/ppermute | solution.py:286
  6.7 2.8 %collective-permute-start.3 = (f32[24,8,128]{2,1,0:T(8,128)S(1)}, f32[24,8,128]{2,1,0:T(8,128)S(1)}, u32[]{:S(2)}, u32[]{:S(2)}) collective-permute-start(f32[24,8,128]{2,1,0:T(8,128)S(1)} %get-tuple-element.18), channel_id=1, source_target_pairs={{0,7},{1,0},{2,1},{3,2},{4,3},{5,4},{6,5},{7,6},{8,15},{9,8},{10,9... | collective-permute-start | bytes 294920 | tf_op jit(solution)/shard_map/ppermute | solution.py:286
  9.5 0.0 collective-permute-start
  9.5 0.0 collective-permute-start.2
  9.5 0.0 copy-start.6
  9.5 0.0 copy-start.5
  9.5 0.7 %reshape.9 = f32[27,16]{1,0:T(8,128)S(1)} reshape(f32[3,3,3,16]{3,2,1,0:T(4,128)} %bitcast.2) | data formatting | bytes 3456 | tf_op jit(solution)/shard_map/reshape | solution.py:295
  10.3 0.0 copy-done.6
  10.3 0.0 copy-done.1
  10.3 0.0 copy-done.3
  10.3 0.0 copy-done.5
  10.3 0.0 copy-start.4
  10.3 1.1 %copy-done.4 = f32[3,8,8,8,128]{4,3,2,1,0:T(8,128)S(1)} copy-done((f32[3,8,8,8,128]{4,3,2,1,0:T(8,128)S(1)}, f32[3,8,8,8,128]{4,3,2,1,0:T(8,128)}, u32[]{:S(2)}) %copy-start.4) | copy-done | bytes 786456
  11.4 3.8 %interior.1 = (f32[3,8,8,8,128]{4,3,2,1,0:T(8,128)S(1)}, bf16[3,8,128,128]{3,2,1,0:T(8,128)(2,1)S(1)}, bf16[3,8,128,128]{3,2,1,0:T(8,128)(2,1)S(1)}, f32[128,128]{1,0:T(8,128)S(1)}) custom-call(f32[3,8,8,8,128]{4,3,2,1,0:T(8,128)S(1)} %copy-done.4, f32[3,8,8,8,128]{4,3,2,1,0:T(8,128)S(1)} %copy-done.1, s32[3,8,8,128]{3,2,1,0:T(8,128)S(1)} %copy-done.3, ...), custom_call_target="tpu_custom_call" | custom-call | flops 100000000 | bytes 4000000 | tf_op jit(solution)/shard_map/interior/pallas_call | solution.py:317
  15.2 0.0 collective-permute-done.1.xhigh_ref
  15.3 0.0 collective-permute-done.3.yhigh_ref
  15.3 0.0 collective-permute-done.xlow_ref
  15.3 0.1 collective-permute-done.2.ylow_ref
  15.4 2.1 %halo.1 = (bf16[3,8,64,128]{3,2,1,0:T(8,128)(2,1)S(1)}, bf16[3,8,64,128]{3,2,1,0:T(8,128)(2,1)S(1)}, f32[32,4,128]{2,1,0:T(4,128)S(1)}) custom-call(f32[3,8,8,8,128]{4,3,2,1,0:T(8,128)S(1)} %get-tuple-element.14.part_ref, s32[3,8,8,128]{3,2,1,0:T(8,128)S(1)} %copy-done.3, f32[30,128]{1,0:T(8,128)S(1)} %select_maximum_fusion.table_ref, ...), custom_call_target="tpu_custom_call" | custom-call | tf_op jit(solution)/shard_map/halo/pallas_call | solution.py:330
  17.5 13.4 %all_to_all.5.refs_0_ = f32[32,4,128]{2,1,0:T(4,128)S(1)} all-to-all(f32[32,4,128]{2,1,0:T(4,128)S(1)} %get-tuple-element.22), channel_id=1, replica_groups=mesh['gx'=4,'gy'=8] {'gx','gy'}, dimensions={0} | all-to-all | bytes 131072 | tf_op jit(solution)/shard_map/all_to_all | solution.py:342
  30.8 3.9 %final.1 = (f32[3,8,8,8,128]{4,3,2,1,0:T(8,128)}, f32[8,8]{1,0:T(8,128)}, f32[8,8]{1,0:T(8,128)}) custom-call(f32[32,4,128]{2,1,0:T(4,128)S(1)} %all_to_all.5.refs_0_, bf16[3,8,128,128]{3,2,1,0:T(8,128)(2,1)S(1)} %get-tuple-element.19.high_ref.refs_1_, bf16[3,8,128,128]{3,2,1,0:T(8,128)(2,1)S(1)} %get-tuple-element.20.low_ref.refs_2_, ...), custom_call_target="tpu_custom_call" | custom-call | tf_op jit(solution)/shard_map/final/pallas_call | solution.py:344
  (1 shorter events, 0.0 us)
Async XLA Ops:
  0.6 1.1 %copy-start = (f32[3,8,8,8,128]{4,3,2,1,0:T(8,128)S(1)}, f32[3,8,8,8,128]{4,3,2,1,0:T(8,128)}, u32[]{:S(2)}) copy-start(f32[3,8,8,8,128]{4,3,2,1,0:T(8,128)} %block_ref.3) | copy-start | bytes 2359300
  1.8 0.9 %copy-start.2 = (s32[3,8,8,128]{3,2,1,0:T(8,128)S(1)}, s32[3,8,8,128]{3,2,1,0:T(8,128)}, u32[]{:S(2)}) copy-start(s32[3,8,8,128]{3,2,1,0:T(8,128)} %seed_ref.5) | copy-start | bytes 294916
  2.7 7.6 %copy-start.1 = (f32[3,8,8,8,128]{4,3,2,1,0:T(8,128)S(1)}, f32[3,8,8,8,128]{4,3,2,1,0:T(8,128)}, u32[]{:S(2)}) copy-start(f32[3,8,8,8,128]{4,3,2,1,0:T(8,128)} %block_ref.3) | copy-start | bytes 2359300
  2.7 7.6 %copy-start.3 = (s32[3,8,8,128]{3,2,1,0:T(8,128)S(1)}, s32[3,8,8,128]{3,2,1,0:T(8,128)}, u32[]{:S(2)}) copy-start(s32[3,8,8,128]{3,2,1,0:T(8,128)} %seed_ref.5) | copy-start | bytes 294916
  2.8 12.5 %collective-permute-start.1 = (f32[24,8,128]{2,1,0:T(8,128)S(1)}, f32[24,8,128]{2,1,0:T(8,128)S(1)}, u32[]{:S(2)}, u32[]{:S(2)}) collective-permute-start(f32[24,8,128]{2,1,0:T(8,128)S(1)} %get-tuple-element.16), channel_id=1, source_target_pairs={{0,24},{8,0},{16,8},{24,16},{1,25},{9,1},{17,9},{25,17},{2,26},{10... | collective-permute-start | bytes 294920 | tf_op jit(solution)/shard_map/ppermute | solution.py:286
  6.7 8.5 %collective-permute-start.3 = (f32[24,8,128]{2,1,0:T(8,128)S(1)}, f32[24,8,128]{2,1,0:T(8,128)S(1)}, u32[]{:S(2)}, u32[]{:S(2)}) collective-permute-start(f32[24,8,128]{2,1,0:T(8,128)S(1)} %get-tuple-element.18), channel_id=1, source_target_pairs={{0,7},{1,0},{2,1},{3,2},{4,3},{5,4},{6,5},{7,6},{8,15},{9,8},{10,9... | collective-permute-start | bytes 294920 | tf_op jit(solution)/shard_map/ppermute | solution.py:286
  9.5 5.8 %collective-permute-start = (f32[25,8,128]{2,1,0:T(8,128)S(1)}, f32[25,8,128]{2,1,0:T(8,128)S(1)}, u32[]{:S(2)}, u32[]{:S(2)}) collective-permute-start(f32[25,8,128]{2,1,0:T(8,128)S(1)} %get-tuple-element.15), channel_id=1, source_target_pairs={{0,8},{8,16},{16,24},{24,0},{1,9},{9,17},{17,25},{25,1},{2,10},{10... | collective-permute-start | bytes 307208 | tf_op jit(solution)/shard_map/ppermute | solution.py:286
  9.5 5.9 %collective-permute-start.2 = (f32[25,8,128]{2,1,0:T(8,128)S(1)}, f32[25,8,128]{2,1,0:T(8,128)S(1)}, u32[]{:S(2)}, u32[]{:S(2)}) collective-permute-start(f32[25,8,128]{2,1,0:T(8,128)S(1)} %get-tuple-element.17), channel_id=1, source_target_pairs={{0,1},{1,2},{2,3},{3,4},{4,5},{5,6},{6,7},{7,0},{8,9},{9,10},{10,1... | collective-permute-start | bytes 307208 | tf_op jit(solution)/shard_map/ppermute | solution.py:286
  9.5 0.8 %copy-start.6 = (f32[16,3]{0,1:T(4,128)S(1)}, f32[16,3]{0,1:T(4,128)}, u32[]{:S(2)}) copy-start(f32[16,3]{0,1:T(4,128)} %param.11) | copy-start | bytes 580
  9.5 0.8 %copy-start.5 = (s32[8,8,128]{2,1,0:T(8,128)S(1)}, s32[8,8,128]{2,1,0:T(8,128)}, u32[]{:S(2)}) copy-start(s32[8,8,128]{2,1,0:T(8,128)} %level_ref.1) | copy-start | bytes 98308
  10.3 1.1 %copy-start.4 = (f32[3,8,8,8,128]{4,3,2,1,0:T(8,128)S(1)}, f32[3,8,8,8,128]{4,3,2,1,0:T(8,128)}, u32[]{:S(2)}) copy-start(f32[3,8,8,8,128]{4,3,2,1,0:T(8,128)} %prev_ref.1) | copy-start | bytes 2359300

commit v2 on v1

--- a/solution.py
+++ b/solution.py
@@ -41,6 +41,16 @@
     ]
 
 
+def fill_table(table_ref, hop_ref, onsite_ref):
+    orbs, kinds = hop_ref.shape[1], hop_ref.shape[3]
+    for d in range(3):
+        for a in range(orbs):
+            base = (d * orbs + a) * orbs
+            table_ref[base : base + orbs, :kinds] = hop_ref[d, a]
+    base = 3 * orbs * orbs
+    table_ref[base : base + orbs, : onsite_ref.shape[1]] = onsite_ref[...]
+
+
 def times(bonds, field):
     return [sum(bonds[a][b] * field[b] for b in range(len(field))) for a in range(len(field))]
 
@@ -49,17 +59,42 @@
     return [sum(bonds[a][b] * field[a] for a in range(len(field))) for b in range(len(field))]
 
 
-def pack_kernel(block_ref, seed_ref, xup_ref, xdown_ref, yup_ref, ydown_ref):
+def pack_kernel(
+    block_in,
+    seed_in,
+    level_in,
+    hop_in,
+    onsite_in,
+    block_ref,
+    seed_ref,
+    level_ref,
+    hop_ref,
+    onsite_ref,
+    xup_ref,
+    xdown_ref,
+    yup_ref,
+    ydown_ref,
+    sems,
+):
     orbs, width, nx, ny, _ = block_ref.shape
+    pairs = [(block_in.at[o], block_ref.at[o]) for o in range(orbs)]
+    pairs += [(seed_in, seed_ref), (level_in, level_ref), (hop_in, hop_ref), (onsite_in, onsite_ref)]
+    loads = [pltpu.make_async_copy(*pair, sems.at[i]) for i, pair in enumerate(pairs)]
+    for load in loads:
+        load.start()
     for o in range(orbs):
+        loads[o].wait()
         for n in range(width):
             spot = o * width + n
             xup_ref[spot] = block_ref[o, n, nx - 1]
             xdown_ref[spot] = block_ref[o, n, 0]
             yup_ref[spot] = block_ref[o, n, :, ny - 1, :]
             ydown_ref[spot] = block_ref[o, n, :, 0, :]
+    loads[orbs].wait()
     xup_ref[orbs * width] = seed_ref[0, nx - 1].astype(F32)
     yup_ref[orbs * width] = seed_ref[1, :, ny - 1, :].astype(F32)
+    for load in loads[orbs + 1 :]:
+        load.wait()
 
 
 def small_sums(total, copies):
@@ -70,9 +105,20 @@
 
 
 def interior_kernel(
-    prev_ref, block_ref, seed_ref, level_ref, table_ref, part_ref, high_ref, low_ref, gram_ref
+    prev_ref,
+    block_ref,
+    seed_ref,
+    level_ref,
+    hop_ref,
+    onsite_ref,
+    part_ref,
+    high_ref,
+    low_ref,
+    gram_ref,
+    table_ref,
 ):
     orbs, width, nx, ny, nz = block_ref.shape
+    fill_table(table_ref, hop_ref, onsite_ref)
     row = iota((ny, nz), 0)
     side = width * ny
     gram_ref[...] = jnp.zeros(gram_ref.shape, F32)
@@ -291,41 +337,53 @@
     devices = lax.axis_size("gx") * lax.axis_size("gy")
     count = orbs * nx * ny * nz * devices
     fields = orbs * width
-    table = jnp.concatenate(
-        [jnp.transpose(hop_table, (0, 2, 3, 1)).reshape(-1, hop_table.shape[1]), onsite_table.T], 0
-    )
-    table = jnp.pad(table, ((0, 0), (0, LANES - table.shape[1])))
+    hops = jnp.transpose(hop_table, (0, 2, 3, 1))
+    onsite = onsite_table.T
+    table_rows = 3 * orbs * orbs + ROWS
+    outside = pl.BlockSpec(memory_space=pltpu.HBM)
+
+    def stay(value):
+        return pltpu.with_memory_space_constraint(value, pltpu.HBM)
+
     params = pltpu.CompilerParams(**PARAMS)
 
-    xup, xdown, yup, ydown = pl.pallas_call(
+    block_here, seed_here, levels_here, hops_here, onsite_here, xup, xdown, yup, ydown = pl.pallas_call(
         pack_kernel,
+        in_specs=[outside] * 5,
         out_shape=[
+            pltpu.VMEM(block.shape, F32),
+            pltpu.VMEM(hop_seed.shape, jnp.int32),
+            pltpu.VMEM(levels.shape, jnp.int32),
+            pltpu.VMEM(hops.shape, F32),
+            pltpu.VMEM(onsite.shape, F32),
             pltpu.VMEM((fields + 1, ny, nz), F32),
             pltpu.VMEM((fields, ny, nz), F32),
             pltpu.VMEM((fields + 1, nx, nz), F32),
             pltpu.VMEM((fields, nx, nz), F32),
         ],
+        scratch_shapes=[pltpu.SemaphoreType.DMA((orbs + 4,))],
         compiler_params=params,
         name="pack",
-    )(block, hop_seed)
+    )(stay(block), stay(hop_seed), stay(levels), stay(hops), stay(onsite))
     xlow = shifted(xup, "gx", 1)
     ylow = shifted(yup, "gy", 1)
     xhigh = shifted(xdown, "gx", -1)
     yhigh = shifted(ydown, "gy", -1)
 
     side = width * ny
-    part, high, low, gram = pl.pallas_call(
+    part, high, low, gram, table = pl.pallas_call(
         interior_kernel,
         out_shape=[
             pltpu.VMEM(block.shape, F32),
             pltpu.VMEM((orbs, nx, 2 * side, nz), BF16),
             pltpu.VMEM((orbs, nx, 2 * side, nz), BF16),
             pltpu.VMEM((2 * side, 2 * side), F32),
+            pltpu.VMEM((table_rows, LANES), F32),
         ],
         compiler_params=params,
         cost_estimate=pl.CostEstimate(flops=10**8, bytes_accessed=4 * 10**6, transcendentals=0),
         name="interior",
-    )(prev_block, block, hop_seed, levels, table)
+    )(prev_block, block_here, seed_here, levels_here, hops_here, onsite_here)
 
     phigh, plow, sums = pl.pallas_call(
         halo_kernel,
@@ -337,7 +395,7 @@
         scratch_shapes=[pltpu.VMEM(block.shape, F32), pltpu.VMEM((3 * side, 2 * side), F32)],
         compiler_params=params,
         name="halo",
-    )(part, hop_seed, table, xlow, xhigh, ylow, yhigh, high, low, gram)
+    )(part, seed_here, table, xlow, xhigh, ylow, yhigh, high, low, gram)
 
     sums = lax.all_to_all(sums, ("gx", "gy"), 0, 0)
 

time: 35 us -> 30.2 us (0.86)
  local copies, waits for them, and re-layouts: 3.91 us -> 0.01 us
  blocking collectives: 13.4 us -> 11 us
  Pallas kernels: 9.89 us -> 11.1 us
  starting transfers between devices: 6.71 us -> 7.28 us
    unnamed x14 -> x2, local copies, waits for them, and re-layouts: 3.16 us -> 0.01 us
    all_to_all x1, blocking collectives: 13.4 us -> 11 us  [per_device(): sums = lax.all_to_all(sums, ('gx', 'gy'), 0, 0)]
    pallas_call x1, Pallas kernels: 0.12 us -> 1.3 us  [per_device(): pl.pallas_call(pack_kernel, in_specs=[outside] * 5, out_shape=[pltpu.VMEM...]
    reshape x1 -> x0, local copies, waits for them, and re-layouts: 0.74 us -> none  [per_device(): jnp.transpose(hop_table, (0, 2, 3, 1)).reshape(-1, hop_table.shape[1])]
    ppermute x4, starting transfers between devices: 6.71 us -> 7.28 us  [shifted(): lax.ppermute(value, axis, [(i, (i + steps) % count) for i in range(count)])]
  transfers between devices with their start and end apart: 4 -> 4, of which waited for: 1 -> 0; matrix products, arithmetic and copies ran while one was open for 2% -> 0% of each run, Pallas kernels for 11% -> 13%
where the time goes in v2:
time: 30.2 us; the launch traced here: 30 us
  Pallas kernels  11.1 us (37%)
  blocking collectives  11 us (36%)
  starting transfers between devices  7.28 us (24%)
  between operations  0.7 us (2%)
    all_to_all x1, blocking collectives, per_device(): sums = lax.all_to_all(sums, ('gx', 'gy'), 0, 0)  11 us
    ppermute x4, starting transfers between devices, shifted(): lax.ppermute(value, axis, [(i, (i + steps) % count) for i in range(count)])  7.28 us
    pallas_call x1, Pallas kernels, per_device(): pl.pallas_call(lambda *refs: final_kernel(count, *refs), out_shape=[jax.S...  3.9 us
    pallas_call x1, Pallas kernels, per_device(): pl.pallas_call(interior_kernel, out_shape=[pltpu.VMEM(block.shape, F32),...  3.78 us
    pallas_call x1, Pallas kernels, per_device(): pl.pallas_call(halo_kernel, out_shape=[pltpu.VMEM((orbs, nx, side, nz), B...  2.08 us
    pallas_call x1, Pallas kernels, per_device(): pl.pallas_call(pack_kernel, in_specs=[outside] * 5, out_shape=[pltpu.VMEM...  1.3 us
  transfers between devices with their start and end apart: 4, of which 0 were waited for; matrix products, arithmetic and copies ran while one was open for 0% of the time, Pallas kernels for 13%

profile of v2, /device:TPU:0, one launch (start us, length us, event | category | flops | bytes accessed | tf_op | source)
XLA Modules:
  0.0 30.0 jit_solution(10168985379523110007)
XLA Ops:
  0.6 0.0 copy-start
  0.6 1.3 %pack.1 = (f32[3,8,8,8,128]{4,3,2,1,0:T(8,128)S(1)}, s32[3,8,8,128]{3,2,1,0:T(8,128)S(1)}, s32[8,8,128]{2,1,0:T(8,128)S(1)}, f32[3,3,3,16]{3,2,1,0:T(4,128)S(1)}...) custom-call(f32[3,8,8,8,128]{4,3,2,1,0:T(8,128)} %block_in.1, ...), custom_call_target="tpu_custom_call" | custom-call | tf_op jit(solution)/shard_map/pack/pallas_call | solution.py:350
  1.9 3.0 %collective-permute-start = (f32[25,8,128]{2,1,0:T(8,128)S(1)}, f32[25,8,128]{2,1,0:T(8,128)S(1)}, u32[]{:S(2)}, u32[]{:S(2)}) collective-permute-start(f32[25,8,128]{2,1,0:T(8,128)S(1)} %get-tuple-element.27), channel_id=1, source_target_pairs={{0,8},{8,16},{16,24},{24,0},{1,9},{9,17},{17,25},{25,1},{2,10},{10... | collective-permute-start | bytes 307208 | tf_op jit(solution)/shard_map/ppermute | solution.py:332
  4.9 0.0 collective-permute-start.2
  4.9 1.1 %collective-permute-start.1 = (f32[24,8,128]{2,1,0:T(8,128)S(1)}, f32[24,8,128]{2,1,0:T(8,128)S(1)}, u32[]{:S(2)}, u32[]{:S(2)}) collective-permute-start(f32[24,8,128]{2,1,0:T(8,128)S(1)} %get-tuple-element.28), channel_id=1, source_target_pairs={{0,24},{8,0},{16,8},{24,16},{1,25},{9,1},{17,9},{25,17},{2,26},{10... | collective-permute-start | bytes 294920 | tf_op jit(solution)/shard_map/ppermute | solution.py:332
  6.0 3.2 %collective-permute-start.3 = (f32[24,8,128]{2,1,0:T(8,128)S(1)}, f32[24,8,128]{2,1,0:T(8,128)S(1)}, u32[]{:S(2)}, u32[]{:S(2)}) collective-permute-start(f32[24,8,128]{2,1,0:T(8,128)S(1)} %get-tuple-element.30), channel_id=1, source_target_pairs={{0,7},{1,0},{2,1},{3,2},{4,3},{5,4},{6,5},{7,6},{8,15},{9,8},{10,9... | collective-permute-start | bytes 294920 | tf_op jit(solution)/shard_map/ppermute | solution.py:332
  9.2 0.0 copy-done
  9.2 3.8 %interior.1 = (f32[3,8,8,8,128]{4,3,2,1,0:T(8,128)S(1)}, bf16[3,8,128,128]{3,2,1,0:T(8,128)(2,1)S(1)}, bf16[3,8,128,128]{3,2,1,0:T(8,128)(2,1)S(1)}, f32[128,128]{1,0:T(8,128)S(1)}, f32[35,128]{1,0:T(8,128)S(1)}) custom-call(f32[3,8,8,8,128]{4,3,2,1,0:T(8,128)S(1)} %copy-done, f32[3,8,8,8,128]{4,3,2,1,0:T(8,128)S(1)} %get-tuple-element.20.block_ref, ...), custom_call_target="tpu_custom_call" | custom-call | flops 100000000 | bytes 4000000 | tf_op jit(solution)/shard_map/interior/pallas_call | solution.py:374
  13.0 0.0 collective-permute-done.1.xhigh_ref
  13.0 0.0 collective-permute-done.3.yhigh_ref
  13.0 0.0 collective-permute-done.xlow_ref
  13.0 0.0 collective-permute-done.2.ylow_ref
  13.1 2.1 %halo.1 = (bf16[3,8,64,128]{3,2,1,0:T(8,128)(2,1)S(1)}, bf16[3,8,64,128]{3,2,1,0:T(8,128)(2,1)S(1)}, f32[32,4,128]{2,1,0:T(4,128)S(1)}) custom-call(f32[3,8,8,8,128]{4,3,2,1,0:T(8,128)S(1)} %get-tuple-element.25.part_ref, s32[3,8,8,128]{3,2,1,0:T(8,128)S(1)} %get-tuple-element.21.seed_ref, f32[35,128]{1,0:T(8,128)S(1)} %get-tuple-element.26.table_ref, ...), custom_call_target="tpu_custom_call" | custom-call | tf_op jit(solution)/shard_map/halo/pallas_call | solution.py:388
  15.1 11.0 %all_to_all.5.refs_0_ = f32[32,4,128]{2,1,0:T(4,128)S(1)} all-to-all(f32[32,4,128]{2,1,0:T(4,128)S(1)} %get-tuple-element.34), channel_id=1, replica_groups=mesh['gx'=4,'gy'=8] {'gx','gy'}, dimensions={0} | all-to-all | bytes 131072 | tf_op jit(solution)/shard_map/all_to_all | solution.py:400
  26.1 3.9 %final.1 = (f32[3,8,8,8,128]{4,3,2,1,0:T(8,128)}, f32[8,8]{1,0:T(8,128)}, f32[8,8]{1,0:T(8,128)}) custom-call(f32[32,4,128]{2,1,0:T(4,128)S(1)} %all_to_all.5.refs_0_, bf16[3,8,128,128]{3,2,1,0:T(8,128)(2,1)S(1)} %get-tuple-element.31.high_ref.refs_1_, bf16[3,8,128,128]{3,2,1,0:T(8,128)(2,1)S(1)} %get-tuple-element.32.low_ref.refs_2_, ...), custom_call_target="tpu_custom_call" | custom-call | tf_op jit(solution)/shard_map/final/pallas_call | solution.py:402
Async XLA Ops:
  0.6 8.6 %copy-start = (f32[3,8,8,8,128]{4,3,2,1,0:T(8,128)S(1)}, f32[3,8,8,8,128]{4,3,2,1,0:T(8,128)}, u32[]{:S(2)}) copy-start(f32[3,8,8,8,128]{4,3,2,1,0:T(8,128)} %prev_ref.1) | copy-start | bytes 2359300
  1.9 11.1 %collective-permute-start = (f32[25,8,128]{2,1,0:T(8,128)S(1)}, f32[25,8,128]{2,1,0:T(8,128)S(1)}, u32[]{:S(2)}, u32[]{:S(2)}) collective-permute-start(f32[25,8,128]{2,1,0:T(8,128)S(1)} %get-tuple-element.27), channel_id=1, source_target_pairs={{0,8},{8,16},{16,24},{24,0},{1,9},{9,17},{17,25},{25,1},{2,10},{10... | collective-permute-start | bytes 307208 | tf_op jit(solution)/shard_map/ppermute | solution.py:332
  4.9 8.1 %collective-permute-start.2 = (f32[25,8,128]{2,1,0:T(8,128)S(1)}, f32[25,8,128]{2,1,0:T(8,128)S(1)}, u32[]{:S(2)}, u32[]{:S(2)}) collective-permute-start(f32[25,8,128]{2,1,0:T(8,128)S(1)} %get-tuple-element.29), channel_id=1, source_target_pairs={{0,1},{1,2},{2,3},{3,4},{4,5},{5,6},{6,7},{7,0},{8,9},{9,10},{10,1... | collective-permute-start | bytes 307208 | tf_op jit(solution)/shard_map/ppermute | solution.py:332
  4.9 8.1 %collective-permute-start.1 = (f32[24,8,128]{2,1,0:T(8,128)S(1)}, f32[24,8,128]{2,1,0:T(8,128)S(1)}, u32[]{:S(2)}, u32[]{:S(2)}) collective-permute-start(f32[24,8,128]{2,1,0:T(8,128)S(1)} %get-tuple-element.28), channel_id=1, source_target_pairs={{0,24},{8,0},{16,8},{24,16},{1,25},{9,1},{17,9},{25,17},{2,26},{10... | collective-permute-start | bytes 294920 | tf_op jit(solution)/shard_map/ppermute | solution.py:332
  6.0 7.0 %collective-permute-start.3 = (f32[24,8,128]{2,1,0:T(8,128)S(1)}, f32[24,8,128]{2,1,0:T(8,128)S(1)}, u32[]{:S(2)}, u32[]{:S(2)}) collective-permute-start(f32[24,8,128]{2,1,0:T(8,128)S(1)} %get-tuple-element.30), channel_id=1, source_target_pairs={{0,7},{1,0},{2,1},{3,2},{4,3},{5,4},{6,5},{7,6},{8,15},{9,8},{10,9... | collective-permute-start | bytes 294920 | tf_op jit(solution)/shard_map/ppermute | solution.py:332

commit v3 on v2

--- a/solution.py
+++ b/solution.py
@@ -97,11 +97,19 @@
         load.wait()
 
 
-def small_sums(total, copies):
+def kept_sums(total):
     rows, columns = total.shape
     same = (iota((rows, columns), 0) % ROWS) == (iota((rows, columns), 1) % ROWS)
     kept = jnp.where(same, total, 0.0)
     return kept.reshape(rows // ROWS, ROWS, columns).sum(axis=1)
+
+
+def gathered(value, spots):
+    high, low = split(value)
+    last = (value - high.astype(F32) - low.astype(F32)).astype(BF16)
+    pieces = dot(jnp.concatenate([high, low, last], 0), spots.astype(BF16), ((1,), (0,)))
+    rows = value.shape[0]
+    return pieces[:rows] + pieces[rows : 2 * rows] + pieces[2 * rows :]
 
 
 def interior_kernel(
@@ -114,23 +122,31 @@
     part_ref,
     high_ref,
     low_ref,
+    metric_ref,
+    table_ref,
     gram_ref,
-    table_ref,
 ):
     orbs, width, nx, ny, nz = block_ref.shape
     fill_table(table_ref, hop_ref, onsite_ref)
     row = iota((ny, nz), 0)
     side = width * ny
-    gram_ref[...] = jnp.zeros(gram_ref.shape, F32)
-
-    def onsite(x, carry):
-        index = [seed_ref[d, x] for d in range(3)]
+
+    def stencil(x, carry):
+        before = jnp.maximum(x - 1, 0)
+        inside = jnp.where(x > 0, 1.0, 0.0)
         energy = [pick(table_ref, 3 * orbs * orbs + o, level_ref[x]) for o in range(orbs)]
-        bond_y = bonds_of(table_ref, 1, index[1], orbs)
-        bond_z = bonds_of(table_ref, 2, index[2], orbs)
+        bond_x = bonds_of(table_ref, 0, seed_ref[0, before], orbs)
+        bond_x = [[inside * value for value in line] for line in bond_x]
+        bond_y = bonds_of(table_ref, 1, seed_ref[1, x], orbs)
+        bond_z = bonds_of(table_ref, 2, seed_ref[2, x], orbs)
         for n in range(width):
             here = [block_ref[o, n, x] for o in range(orbs)]
+            behind = [block_ref[o, n, before] for o in range(orbs)]
+            forward = times(bond_x, here)
+            for o in range(orbs):
+                part_ref[o, n, before] += forward[o]
             image = [energy[o] * here[o] for o in range(orbs)]
+            image = [a + b for a, b in zip(image, times_transposed(bond_x, behind))]
             ahead = [jnp.where(row == ny - 1, 0.0, pltpu.roll(v, ny - 1, 0)) for v in here]
             image = [a + b for a, b in zip(image, times(bond_y, ahead))]
             carried = times_transposed(bond_y, here)
@@ -145,21 +161,8 @@
                 part_ref[o, n, x] = image[o]
         return carry
 
-    lax.fori_loop(0, nx, onsite, 0)
-
-    def along_x(x, carry):
-        bonds = bonds_of(table_ref, 0, seed_ref[0, x], orbs)
-        for n in range(width):
-            here = [block_ref[o, n, x] for o in range(orbs)]
-            ahead = [block_ref[o, n, x + 1] for o in range(orbs)]
-            forward = times(bonds, ahead)
-            back = times_transposed(bonds, here)
-            for o in range(orbs):
-                part_ref[o, n, x] += forward[o]
-                part_ref[o, n, x + 1] += back[o]
-        return carry
-
-    lax.fori_loop(0, nx - 1, along_x, 0)
+    lax.fori_loop(0, nx, stencil, 0)
+    gram_ref[...] = jnp.zeros(gram_ref.shape, F32)
 
     def products(pair, carry):
         for o in range(orbs):
@@ -176,18 +179,21 @@
                 lows.append(low)
             high = jnp.concatenate(highs, 1)
             low = jnp.concatenate(lows, 1)
-            gram_ref[...] += (
-                dot(high, high, ((1,), (1,)))
-                + dot(high, low, ((1,), (1,)))
-                + dot(low, high, ((1,), (1,)))
-            )
+            gram_ref[...] += dot(high, jnp.concatenate([high, low], 0), ((1,), (1,)))
         return carry
 
     lax.fori_loop(0, nx // 2, products, 0)
+    crossed = gram_ref[:, 2 * side :]
+    sums = kept_sums(gram_ref[:, : 2 * side] + crossed + crossed.T)
+    spots = iota((LANES, LANES), 0) // ny
+    lanes = iota((LANES, LANES), 1) % (LANES // 2)
+    maps = [jnp.where(lanes == width * (3 + 2 * i) + spots, 1.0, 0.0) for i in range(2)]
+    parts = [sums[i * width : (i + 1) * width] for i in range(2)]
+    metric_ref[...] = gathered(jnp.concatenate(parts, 1), jnp.concatenate(maps, 0))
 
 
 def halo_kernel(
-    part_ref,
+    part_in,
     seed_ref,
     table_ref,
     xlow_ref,
@@ -196,17 +202,16 @@
     yhigh_ref,
     high_ref,
     low_ref,
-    gram_ref,
+    metric_ref,
     phigh_ref,
     plow_ref,
     sums_ref,
-    image_ref,
+    part_ref,
     total_ref,
 ):
     orbs, width, nx, ny, nz = part_ref.shape
     side = width * ny
     last = orbs * width
-    image_ref[...] = part_ref[...]
 
     bond_x = bonds_of(table_ref, 0, seed_ref[0, nx - 1], orbs)
     bond_xlow = bonds_of(table_ref, 0, xlow_ref[last].astype(jnp.int32), orbs)
@@ -214,16 +219,16 @@
         forward = times(bond_x, [xhigh_ref[o * width + n] for o in range(orbs)])
         back = times_transposed(bond_xlow, [xlow_ref[o * width + n] for o in range(orbs)])
         for o in range(orbs):
-            image_ref[o, n, nx - 1] += forward[o]
-            image_ref[o, n, 0] += back[o]
+            part_ref[o, n, nx - 1] += forward[o]
+            part_ref[o, n, 0] += back[o]
     bond_y = bonds_of(table_ref, 1, seed_ref[1, :, ny - 1, :], orbs)
     bond_ylow = bonds_of(table_ref, 1, ylow_ref[last].astype(jnp.int32), orbs)
     for n in range(width):
         forward = times(bond_y, [yhigh_ref[o * width + n] for o in range(orbs)])
         back = times_transposed(bond_ylow, [ylow_ref[o * width + n] for o in range(orbs)])
         for o in range(orbs):
-            image_ref[o, n, :, ny - 1, :] += forward[o]
-            image_ref[o, n, :, 0, :] += back[o]
+            part_ref[o, n, :, ny - 1, :] += forward[o]
+            part_ref[o, n, :, 0, :] += back[o]
 
     total_ref[...] = jnp.zeros(total_ref.shape, F32)
 
@@ -232,99 +237,140 @@
             ins = [[], [], [], []]
             for half in range(2):
                 x = 2 * pair + half
-                high, low = split(image_ref[o, :, x].reshape(side, nz))
+                high, low = split(part_ref[o, :, x].reshape(side, nz))
                 phigh_ref[o, x] = high
                 plow_ref[o, x] = low
                 for group, value in zip(ins, (high, low, high_ref[o, x], low_ref[o, x])):
                     group.append(value)
             high, low, bhigh, blow = (jnp.concatenate(group, 1) for group in ins)
-            both = jnp.concatenate([high, low], 0)
-            total_ref[...] += dot(jnp.concatenate([bhigh, high], 0), both, ((1,), (1,))) + dot(
-                jnp.concatenate([blow, low], 0), both, ((1,), (1,))
+            total_ref[...] += dot(
+                jnp.concatenate([bhigh, high, blow, low], 0),
+                jnp.concatenate([high, low], 0),
+                ((1,), (1,)),
             )
         return carry
 
     lax.fori_loop(0, nx // 2, products, 0)
 
-    first = small_sums(total_ref[...], 3)
-    second = small_sums(gram_ref[...], 2)
-    parts = [first[i * width : (i + 1) * width] for i in range(3)]
-    parts += [second[i * width : (i + 1) * width] for i in range(2)]
-    stacked = jnp.concatenate(parts, 1)
-    spots = iota((LANES, LANES), 0)
-    lanes = iota((LANES, LANES), 1)
-    maps = []
+    sums = kept_sums(total_ref[: 3 * side] + total_ref[3 * side :])
+    spots = (iota((LANES, LANES), 0) // ny) % width
+    sums = gathered(sums, jnp.where(iota((LANES, LANES), 1) % width == spots, 1.0, 0.0))
+    lanes = iota((width, LANES), 1)
+    place = (lanes % (LANES // 2)) // width
+    packed = metric_ref[...]
     for i in range(3):
-        maps.append(jnp.where(lanes == width * i + (spots // ny) % width, 1.0, 0.0))
-    for i in range(2):
-        maps.append(jnp.where(lanes == width * (3 + 2 * i) + spots // ny, 1.0, 0.0))
-    sums = dot(stacked, jnp.concatenate(maps, 0), ((1,), (0,)), HIGH)
+        packed = jnp.where(place == i, sums[i * width : (i + 1) * width], packed)
     half = width // 2
-    folded = sums[:half] + pltpu.roll(sums, LANES // 2, 1)[half:]
+    folded = jnp.where(lanes[:half] < LANES // 2, packed[:half], packed[half:])
     sums_ref[...] = jnp.broadcast_to(folded[None], sums_ref.shape)
 
 
-def final_kernel(count, sums_ref, high_ref, low_ref, phigh_ref, plow_ref, next_ref, alpha_ref, beta_ref):
+def column(value, spot):
+    return jnp.broadcast_to(value[:, spot : spot + 1], value.shape)
+
+
+def line(value, spot):
+    return jnp.broadcast_to(value[spot : spot + 1, :], value.shape)
+
+
+def added(terms):
+    while len(terms) > 1:
+        terms = [sum(terms[i : i + 2][1:], terms[i]) for i in range(0, len(terms), 2)]
+    return terms[0]
+
+
+def final_kernel(
+    count, sums_ref, high_ref, low_ref, phigh_ref, plow_ref, next_ref, alpha_ref, beta_ref, out_ref, sems
+):
     orbs, nx, side, nz = phigh_ref.shape
     width = side // ROWS
+    shape = (width, LANES)
+    rows, lanes = iota(shape, 0), iota(shape, 1)
     folded = jnp.sum(sums_ref[...], axis=0) / count
     sums = jnp.concatenate([folded, pltpu.roll(folded, LANES // 2, 1)], 0)
-    first = jnp.concatenate([sums[:, 0:width], sums[:, width : 2 * width]], 0)
-    norms = sums[:, 2 * width : 3 * width]
-    metric = jnp.concatenate([sums[:, 3 * width : 5 * width], sums[:, 5 * width : 7 * width]], 0)
-    alpha_ref[...] = first[width:]
-    eye = jnp.where(iota((width, width), 0) == iota((width, width), 1), 1.0, 0.0)
-    turned = dot(eye, first, ((1,), (1,)), HIGH)
-    coeffs = 2.0 * turned - dot(turned, metric, ((1,), (0,)), HIGH)
-    rest = turned - dot(coeffs, metric, ((1,), (0,)), HIGH)
-    gram = norms - dot(
-        jnp.concatenate([turned, coeffs], 1),
-        jnp.concatenate([coeffs, rest], 1),
-        ((1,), (1,)),
-        HIGH,
-    )
-    pad = jnp.zeros((width, LANES - 4 * width), F32)
-    table = jnp.concatenate([gram, eye, -coeffs, pad], 1)
-    rows = iota((width, LANES), 0)
-    scale = jnp.ones((width, LANES), F32)
+
+    def moved(start, length):
+        value = sums if start == 0 else pltpu.roll(sums, LANES - start, 1)
+        return jnp.where(lanes < length, value, 0.0)
+
+    first = [moved(0, width), moved(width, width)]
+    norms = moved(2 * width, width)
+    metric = [moved(3 * width, 2 * width), moved(5 * width, 2 * width)]
+    alpha_ref[...] = first[1][:, :width]
+    ones = [jnp.where(lanes == rows + i * width, 1.0, 0.0) for i in range(2)]
+    lack = [one - value for one, value in zip(ones, metric)]
+    lack_columns = [[column(value, k) for k in range(2 * width)] for value in lack]
+
+    def lacking(pair):
+        lines = [line(value, k) for value in pair for k in range(width)]
+        return [added([a * b for a, b in zip(columns, lines)]) for columns in lack_columns]
+
+    one = lacking(first)
+    two = lacking(one)
+    three = lacking(two)
+    weighed = [added(list(terms)) for terms in zip(first, one, two, three)]
+    turned = jnp.concatenate(first, 0).T[:width]
+    turned_columns = [
+        jnp.broadcast_to(turned[:, k : k + 1], shape) for k in range(2 * width)
+    ]
+    weighed_lines = [line(value, k) for value in weighed for k in range(width)]
+    gram = norms - added([a * b for a, b in zip(turned_columns, weighed_lines)])
+    twice = [a + b for a, b in zip(ones, lack)]
+    twice_lines = [line(value, k) for value in twice for k in range(width)]
+    coeffs = added([a * b for a, b in zip(turned_columns, twice_lines)])
+    table = gram + jnp.where(lanes == rows + width, 1.0, 0.0) - pltpu.roll(coeffs, 2 * width, 1)
+
+    entry = {}
     for k in range(width):
-        pivot = jnp.broadcast_to(table[k : k + 1, k : k + 1], (width, LANES))
-        column = jnp.broadcast_to(table[:, k : k + 1], (width, LANES))
-        line = jnp.broadcast_to(table[k : k + 1, :], (width, LANES))
-        table = jnp.where(rows > k, table - column / pivot * line, table)
-        scale = jnp.where(rows == k, lax.rsqrt(pivot), scale)
-    table = table * scale
-    keep = iota((width, width), 0) <= iota((width, width), 1)
-    beta_ref[...] = jnp.where(keep, table[:, :width], 0.0)
-    lanes = iota((width, LANES), 1)
-    basis_part = jnp.take_along_axis(table, 2 * width + lanes // ROWS, axis=1)
-    product_part = jnp.take_along_axis(table, width + (lanes // ROWS) % width, axis=1)
-
-    def spread(value, columns):
-        grown = jnp.broadcast_to(value[:, None, :], (width, ROWS, LANES)).reshape(side, LANES)
-        same = iota((side, LANES), 0) % ROWS == iota((side, LANES), 1) % ROWS
-        return jnp.where(same, grown, 0.0)[:, :columns]
-
-    mixed = jnp.concatenate([spread(basis_part, LANES), spread(product_part, side)], 1)
-    mixed_high, mixed_low = split(mixed)
-
-    def combine(pair, carry):
-        for o in range(orbs):
+        spread = column(gram, k)
+        for j in range(k, width):
+            entry[j, k] = line(spread, j)
+    lines = [line(table, k) for k in range(width)]
+    for k in range(width):
+        inverse = 1.0 / entry[k, k]
+        for j in range(k + 1, width):
+            ratio = entry[j, k] * inverse
+            for i in range(k + 1, j + 1):
+                entry[j, i] = entry[j, i] - ratio * entry[i, k]
+            lines[j] = lines[j] - ratio * lines[k]
+    lines = [value * lax.rsqrt(entry[k, k]) for k, value in enumerate(lines)]
+    upper = jnp.zeros(shape, F32)
+    for k in range(width):
+        upper = jnp.where((rows == k) & (lanes >= k), lines[k], upper)
+    beta_ref[...] = upper[:, :width]
+
+    same = rows == lanes % ROWS
+    spots = [2 * width + lanes // ROWS, width + (lanes // ROWS) % width]
+    grown = [
+        jnp.concatenate(
+            [jnp.where(same, jnp.take_along_axis(value, spot, axis=1), 0.0) for value in lines], 0
+        )
+        for spot in spots
+    ]
+    mixed_high, mixed_low = split(jnp.concatenate([grown[0], grown[1][:, :side]], 1))
+    mixed = jnp.concatenate([mixed_high, mixed_low], 0)
+    dims = ((1,), (0,))
+    stores = []
+    for o in range(orbs):
+
+        def combine(pair, carry):
             highs, lows = [], []
             for half in range(2):
                 x = 2 * pair + half
                 highs.append(jnp.concatenate([high_ref[o, x], phigh_ref[o, x]], 0))
                 lows.append(jnp.concatenate([low_ref[o, x], plow_ref[o, x]], 0))
-            high = jnp.concatenate(highs, 1)
-            low = jnp.concatenate(lows, 1)
-            dims = ((1,), (0,))
-            out = dot(mixed_high, high, dims) + dot(mixed_low, high, dims) + dot(mixed_high, low, dims)
+            both = dot(mixed, jnp.concatenate(highs, 1), dims)
+            out = both[:side] + both[side:] + dot(mixed_high, jnp.concatenate(lows, 1), dims)
             for half in range(2):
                 x = 2 * pair + half
-                next_ref[o, :, x] = out[:, half * nz : (half + 1) * nz].reshape(width, ROWS, nz)
-        return carry
-
-    lax.fori_loop(0, nx // 2, combine, 0)
+                out_ref[o, :, x] = out[:, half * nz : (half + 1) * nz].reshape(width, ROWS, nz)
+            return carry
+
+        lax.fori_loop(0, nx // 2, combine, 0)
+        stores.append(pltpu.make_async_copy(out_ref.at[o], next_ref.at[o], sems.at[o]))
+        stores[-1].start()
+    for store in stores:
+        store.wait()
 
 
 def shifted(value, axis, steps):
@@ -371,31 +417,34 @@
     yhigh = shifted(ydown, "gy", -1)
 
     side = width * ny
-    part, high, low, gram, table = pl.pallas_call(
+    part, high, low, metric, table = pl.pallas_call(
         interior_kernel,
         out_shape=[
             pltpu.VMEM(block.shape, F32),
             pltpu.VMEM((orbs, nx, 2 * side, nz), BF16),
             pltpu.VMEM((orbs, nx, 2 * side, nz), BF16),
-            pltpu.VMEM((2 * side, 2 * side), F32),
+            pltpu.VMEM((width, LANES), F32),
             pltpu.VMEM((table_rows, LANES), F32),
         ],
+        scratch_shapes=[pltpu.VMEM((2 * side, 4 * side), F32)],
         compiler_params=params,
         cost_estimate=pl.CostEstimate(flops=10**8, bytes_accessed=4 * 10**6, transcendentals=0),
         name="interior",
     )(prev_block, block_here, seed_here, levels_here, hops_here, onsite_here)
 
-    phigh, plow, sums = pl.pallas_call(
+    phigh, plow, sums, _ = pl.pallas_call(
         halo_kernel,
         out_shape=[
             pltpu.VMEM((orbs, nx, side, nz), BF16),
             pltpu.VMEM((orbs, nx, side, nz), BF16),
             pltpu.VMEM((devices, width // 2, LANES), F32),
+            pltpu.VMEM(block.shape, F32),
         ],
-        scratch_shapes=[pltpu.VMEM(block.shape, F32), pltpu.VMEM((3 * side, 2 * side), F32)],
+        input_output_aliases={0: 3},
+        scratch_shapes=[pltpu.VMEM((6 * side, 2 * side), F32)],
         compiler_params=params,
         name="halo",
-    )(part, seed_here, table, xlow, xhigh, ylow, yhigh, high, low, gram)
+    )(part, seed_here, table, xlow, xhigh, ylow, yhigh, high, low, metric)
 
     sums = lax.all_to_all(sums, ("gx", "gy"), 0, 0)
 
@@ -406,6 +455,8 @@
             jax.ShapeDtypeStruct((width, width), F32),
             jax.ShapeDtypeStruct((width, width), F32),
         ],
+        out_specs=[outside, pl.BlockSpec(memory_space=pltpu.VMEM), pl.BlockSpec(memory_space=pltpu.VMEM)],
+        scratch_shapes=[pltpu.VMEM(block.shape, F32), pltpu.SemaphoreType.DMA((orbs,))],
         compiler_params=params,
         name="final",
     )(sums, high, low, phigh, plow)

time: 30.2 us -> 30.3 us (level)
  Pallas kernels: 11.1 us -> 10.5 us
  blocking collectives: 11 us -> 11.6 us
    all_to_all x1, blocking collectives: 11 us -> 11.6 us  [per_device(): sums = lax.all_to_all(sums, ('gx', 'gy'), 0, 0)]
    pallas_call x1, Pallas kernels: 3.78 us -> 3.19 us  [per_device(): pl.pallas_call(interior_kernel, out_shape=[pltpu.VMEM(block.shape, F32),...]
  transfers between devices with their start and end apart: 4 -> 4, of which waited for: 0 -> 0; matrix products, arithmetic and copies ran while one was open for 0% -> 0% of each run, Pallas kernels for 13% -> 11%
where the time goes in v3:
time: 30.3 us; the launch traced here: 30.1 us
  blocking collectives  11.6 us (38%)
  Pallas kernels  10.5 us (35%)
  starting transfers between devices  7.28 us (24%)
  between operations  0.68 us (2%)
    all_to_all x1, blocking collectives, per_device(): sums = lax.all_to_all(sums, ('gx', 'gy'), 0, 0)  11.6 us
    ppermute x4, starting transfers between devices, shifted(): lax.ppermute(value, axis, [(i, (i + steps) % count) for i in range(count)])  7.28 us
    pallas_call x1, Pallas kernels, per_device(): pl.pallas_call(lambda *refs: final_kernel(count, *refs), out_shape=[jax.S...  4.17 us
    pallas_call x1, Pallas kernels, per_device(): pl.pallas_call(interior_kernel, out_shape=[pltpu.VMEM(block.shape, F32),...  3.19 us
    pallas_call x1, Pallas kernels, per_device(): pl.pallas_call(halo_kernel, out_shape=[pltpu.VMEM((orbs, nx, side, nz), B...  1.88 us
    pallas_call x1, Pallas kernels, per_device(): pl.pallas_call(pack_kernel, in_specs=[outside] * 5, out_shape=[pltpu.VMEM...  1.3 us
  transfers between devices with their start and end apart: 4, of which 0 were waited for; matrix products, arithmetic and copies ran while one was open for 0% of the time, Pallas kernels for 11%

profile of v3, /device:TPU:0, one launch (start us, length us, event | category | flops | bytes accessed | tf_op | source)
XLA Modules:
  0.0 30.1 jit_solution(16683161615020845102)
XLA Ops:
  0.6 0.0 copy-start
  0.6 1.3 %pack.1 = (f32[3,8,8,8,128]{4,3,2,1,0:T(8,128)S(1)}, s32[3,8,8,128]{3,2,1,0:T(8,128)S(1)}, s32[8,8,128]{2,1,0:T(8,128)S(1)}, f32[3,3,3,16]{3,2,1,0:T(4,128)S(1)}...) custom-call(f32[3,8,8,8,128]{4,3,2,1,0:T(8,128)} %block_in.1, ...), custom_call_target="tpu_custom_call" | custom-call | tf_op jit(solution)/shard_map/pack/pallas_call | solution.py:396
  1.9 3.0 %collective-permute-start = (f32[25,8,128]{2,1,0:T(8,128)S(1)}, f32[25,8,128]{2,1,0:T(8,128)S(1)}, u32[]{:S(2)}, u32[]{:S(2)}) collective-permute-start(f32[25,8,128]{2,1,0:T(8,128)S(1)} %get-tuple-element.27), channel_id=1, source_target_pairs={{0,8},{8,16},{16,24},{24,0},{1,9},{9,17},{17,25},{25,1},{2,10},{10... | collective-permute-start | bytes 307208 | tf_op jit(solution)/shard_map/ppermute | solution.py:378
  4.9 0.0 collective-permute-start.2
  4.9 1.1 %collective-permute-start.1 = (f32[24,8,128]{2,1,0:T(8,128)S(1)}, f32[24,8,128]{2,1,0:T(8,128)S(1)}, u32[]{:S(2)}, u32[]{:S(2)}) collective-permute-start(f32[24,8,128]{2,1,0:T(8,128)S(1)} %get-tuple-element.28), channel_id=1, source_target_pairs={{0,24},{8,0},{16,8},{24,16},{1,25},{9,1},{17,9},{25,17},{2,26},{10... | collective-permute-start | bytes 294920 | tf_op jit(solution)/shard_map/ppermute | solution.py:378
  6.0 3.2 %collective-permute-start.3 = (f32[24,8,128]{2,1,0:T(8,128)S(1)}, f32[24,8,128]{2,1,0:T(8,128)S(1)}, u32[]{:S(2)}, u32[]{:S(2)}) collective-permute-start(f32[24,8,128]{2,1,0:T(8,128)S(1)} %get-tuple-element.30), channel_id=1, source_target_pairs={{0,7},{1,0},{2,1},{3,2},{4,3},{5,4},{6,5},{7,6},{8,15},{9,8},{10,9... | collective-permute-start | bytes 294920 | tf_op jit(solution)/shard_map/ppermute | solution.py:378
  9.2 0.0 copy-done
  9.2 3.2 %interior.1 = (f32[3,8,8,8,128]{4,3,2,1,0:T(8,128)S(1)}, bf16[3,8,128,128]{3,2,1,0:T(8,128)(2,1)S(1)}, bf16[3,8,128,128]{3,2,1,0:T(8,128)(2,1)S(1)}, f32[8,128]{1,0:T(8,128)S(1)}, f32[35,128]{1,0:T(8,128)S(1)}) custom-call(f32[3,8,8,8,128]{4,3,2,1,0:T(8,128)S(1)} %copy-done, f32[3,8,8,8,128]{4,3,2,1,0:T(8,128)S(1)} %get-tuple-element.20.block_ref, ...), custom_call_target="tpu_custom_call" | custom-call | flops 100000000 | bytes 4000000 | tf_op jit(solution)/shard_map/interior/pallas_call | solution.py:420
  12.4 0.0 collective-permute-done.1.xhigh_ref
  12.4 0.0 collective-permute-done.3.yhigh_ref
  12.4 0.0 collective-permute-done.xlow_ref
  12.4 0.0 collective-permute-done.2.ylow_ref
  12.5 1.9 %halo.1 = (bf16[3,8,64,128]{3,2,1,0:T(8,128)(2,1)S(1)}, bf16[3,8,64,128]{3,2,1,0:T(8,128)(2,1)S(1)}, f32[32,4,128]{2,1,0:T(4,128)S(1)}, f32[3,8,8,8,128]{4,3,2,1,0:T(8,128)S(1)}) custom-call(f32[3,8,8,8,128]{4,3,2,1,0:T(8,128)S(1)} %get-tuple-element.25.part_in, s32[3,8,8,128]{3,2,1,0:T(8,128)S(1)} %get-tuple-element.21.seed_ref, ...), custom_call_target="tpu_custom_call", output_to_operand_aliasing={{3}: (0, {})} | custom-call | tf_op jit(solution)/shard_map/halo/pallas_call | solution.py:435
  14.3 11.6 %all_to_all.5.refs_0_ = f32[32,4,128]{2,1,0:T(4,128)S(1)} all-to-all(f32[32,4,128]{2,1,0:T(4,128)S(1)} %get-tuple-element.34), channel_id=1, replica_groups=mesh['gx'=4,'gy'=8] {'gx','gy'}, dimensions={0} | all-to-all | bytes 131072 | tf_op jit(solution)/shard_map/all_to_all | solution.py:449
  25.9 4.2 %final.1 = (f32[3,8,8,8,128]{4,3,2,1,0:T(8,128)}, f32[8,8]{1,0:T(8,128)}, f32[8,8]{1,0:T(8,128)}) custom-call(f32[32,4,128]{2,1,0:T(4,128)S(1)} %all_to_all.5.refs_0_, bf16[3,8,128,128]{3,2,1,0:T(8,128)(2,1)S(1)} %get-tuple-element.31.high_ref.refs_1_, bf16[3,8,128,128]{3,2,1,0:T(8,128)(2,1)S(1)} %get-tuple-element.32.low_ref.refs_2_, ...), custom_call_target="tpu_custom_call" | custom-call | tf_op jit(solution)/shard_map/final/pallas_call | solution.py:451
Async XLA Ops:
  0.6 8.6 %copy-start = (f32[3,8,8,8,128]{4,3,2,1,0:T(8,128)S(1)}, f32[3,8,8,8,128]{4,3,2,1,0:T(8,128)}, u32[]{:S(2)}) copy-start(f32[3,8,8,8,128]{4,3,2,1,0:T(8,128)} %prev_ref.1) | copy-start | bytes 2359300
  1.9 10.5 %collective-permute-start = (f32[25,8,128]{2,1,0:T(8,128)S(1)}, f32[25,8,128]{2,1,0:T(8,128)S(1)}, u32[]{:S(2)}, u32[]{:S(2)}) collective-permute-start(f32[25,8,128]{2,1,0:T(8,128)S(1)} %get-tuple-element.27), channel_id=1, source_target_pairs={{0,8},{8,16},{16,24},{24,0},{1,9},{9,17},{17,25},{25,1},{2,10},{10... | collective-permute-start | bytes 307208 | tf_op jit(solution)/shard_map/ppermute | solution.py:378
  4.9 7.5 %collective-permute-start.2 = (f32[25,8,128]{2,1,0:T(8,128)S(1)}, f32[25,8,128]{2,1,0:T(8,128)S(1)}, u32[]{:S(2)}, u32[]{:S(2)}) collective-permute-start(f32[25,8,128]{2,1,0:T(8,128)S(1)} %get-tuple-element.29), channel_id=1, source_target_pairs={{0,1},{1,2},{2,3},{3,4},{4,5},{5,6},{6,7},{7,0},{8,9},{9,10},{10,1... | collective-permute-start | bytes 307208 | tf_op jit(solution)/shard_map/ppermute | solution.py:378
  4.9 7.5 %collective-permute-start.1 = (f32[24,8,128]{2,1,0:T(8,128)S(1)}, f32[24,8,128]{2,1,0:T(8,128)S(1)}, u32[]{:S(2)}, u32[]{:S(2)}) collective-permute-start(f32[24,8,128]{2,1,0:T(8,128)S(1)} %get-tuple-element.28), channel_id=1, source_target_pairs={{0,24},{8,0},{16,8},{24,16},{1,25},{9,1},{17,9},{25,17},{2,26},{10... | collective-permute-start | bytes 294920 | tf_op jit(solution)/shard_map/ppermute | solution.py:378
  6.0 6.4 %collective-permute-start.3 = (f32[24,8,128]{2,1,0:T(8,128)S(1)}, f32[24,8,128]{2,1,0:T(8,128)S(1)}, u32[]{:S(2)}, u32[]{:S(2)}) collective-permute-start(f32[24,8,128]{2,1,0:T(8,128)S(1)} %get-tuple-element.30), channel_id=1, source_target_pairs={{0,7},{1,0},{2,1},{3,2},{4,3},{5,4},{6,5},{7,6},{8,15},{9,8},{10,9... | collective-permute-start | bytes 294920 | tf_op jit(solution)/shard_map/ppermute | solution.py:378

commit v4 on v3

--- a/solution.py
+++ b/solution.py
@@ -164,7 +164,7 @@
     lax.fori_loop(0, nx, stencil, 0)
     gram_ref[...] = jnp.zeros(gram_ref.shape, F32)
 
-    def products(pair, carry):
+    def products(pair):
         for o in range(orbs):
             highs, lows = [], []
             for half in range(2):
@@ -180,9 +180,9 @@
             high = jnp.concatenate(highs, 1)
             low = jnp.concatenate(lows, 1)
             gram_ref[...] += dot(high, jnp.concatenate([high, low], 0), ((1,), (1,)))
-        return carry
-
-    lax.fori_loop(0, nx // 2, products, 0)
+
+    for pair in range(nx // 2):
+        products(pair)
     crossed = gram_ref[:, 2 * side :]
     sums = kept_sums(gram_ref[:, : 2 * side] + crossed + crossed.T)
     spots = iota((LANES, LANES), 0) // ny
@@ -232,7 +232,7 @@
 
     total_ref[...] = jnp.zeros(total_ref.shape, F32)
 
-    def products(pair, carry):
+    def products(pair):
         for o in range(orbs):
             ins = [[], [], [], []]
             for half in range(2):
@@ -248,9 +248,9 @@
                 jnp.concatenate([high, low], 0),
                 ((1,), (1,)),
             )
-        return carry
-
-    lax.fori_loop(0, nx // 2, products, 0)
+
+    for pair in range(nx // 2):
+        products(pair)
 
     sums = kept_sums(total_ref[: 3 * side] + total_ref[3 * side :])
     spots = (iota((LANES, LANES), 0) // ny) % width
@@ -280,7 +280,19 @@
 
 
 def final_kernel(
-    count, sums_ref, high_ref, low_ref, phigh_ref, plow_ref, next_ref, alpha_ref, beta_ref, out_ref, sems
+    count,
+    sums_ref,
+    high_ref,
+    low_ref,
+    phigh_ref,
+    plow_ref,
+    next_ref,
+    alpha_out,
+    beta_out,
+    out_ref,
+    alpha_ref,
+    beta_ref,
+    sems,
 ):
     orbs, nx, side, nz = phigh_ref.shape
     width = side // ROWS
@@ -297,6 +309,8 @@
     norms = moved(2 * width, width)
     metric = [moved(3 * width, 2 * width), moved(5 * width, 2 * width)]
     alpha_ref[...] = first[1][:, :width]
+    stores = [pltpu.make_async_copy(alpha_ref, alpha_out, sems.at[orbs])]
+    stores[-1].start()
     ones = [jnp.where(lanes == rows + i * width, 1.0, 0.0) for i in range(2)]
     lack = [one - value for one, value in zip(ones, metric)]
     lack_columns = [[column(value, k) for k in range(2 * width)] for value in lack]
@@ -338,6 +352,8 @@
     for k in range(width):
         upper = jnp.where((rows == k) & (lanes >= k), lines[k], upper)
     beta_ref[...] = upper[:, :width]
+    stores.append(pltpu.make_async_copy(beta_ref, beta_out, sems.at[orbs + 1]))
+    stores[-1].start()
 
     same = rows == lanes % ROWS
     spots = [2 * width + lanes // ROWS, width + (lanes // ROWS) % width]
@@ -350,23 +366,22 @@
     mixed_high, mixed_low = split(jnp.concatenate([grown[0], grown[1][:, :side]], 1))
     mixed = jnp.concatenate([mixed_high, mixed_low], 0)
     dims = ((1,), (0,))
-    stores = []
+
+    def chunk(o, pair):
+        highs, lows = [], []
+        for half in range(2):
+            x = 2 * pair + half
+            highs.append(jnp.concatenate([high_ref[o, x], phigh_ref[o, x]], 0))
+            lows.append(jnp.concatenate([low_ref[o, x], plow_ref[o, x]], 0))
+        both = dot(mixed, jnp.concatenate(highs, 1), dims)
+        out = both[:side] + both[side:] + dot(mixed_high, jnp.concatenate(lows, 1), dims)
+        for half in range(2):
+            x = 2 * pair + half
+            out_ref[o, :, x] = out[:, half * nz : (half + 1) * nz].reshape(width, ROWS, nz)
+
     for o in range(orbs):
-
-        def combine(pair, carry):
-            highs, lows = [], []
-            for half in range(2):
-                x = 2 * pair + half
-                highs.append(jnp.concatenate([high_ref[o, x], phigh_ref[o, x]], 0))
-                lows.append(jnp.concatenate([low_ref[o, x], plow_ref[o, x]], 0))
-            both = dot(mixed, jnp.concatenate(highs, 1), dims)
-            out = both[:side] + both[side:] + dot(mixed_high, jnp.concatenate(lows, 1), dims)
-            for half in range(2):
-                x = 2 * pair + half
-                out_ref[o, :, x] = out[:, half * nz : (half + 1) * nz].reshape(width, ROWS, nz)
-            return carry
-
-        lax.fori_loop(0, nx // 2, combine, 0)
+        for pair in range(nx // 2):
+            chunk(o, pair)
         stores.append(pltpu.make_async_copy(out_ref.at[o], next_ref.at[o], sems.at[o]))
         stores[-1].start()
     for store in stores:
@@ -455,8 +470,13 @@
             jax.ShapeDtypeStruct((width, width), F32),
             jax.ShapeDtypeStruct((width, width), F32),
         ],
-        out_specs=[outside, pl.BlockSpec(memory_space=pltpu.VMEM), pl.BlockSpec(memory_space=pltpu.VMEM)],
-        scratch_shapes=[pltpu.VMEM(block.shape, F32), pltpu.SemaphoreType.DMA((orbs,))],
+        out_specs=[outside] * 3,
+        scratch_shapes=[
+            pltpu.VMEM(block.shape, F32),
+            pltpu.VMEM((width, width), F32),
+            pltpu.VMEM((width, width), F32),
+            pltpu.SemaphoreType.DMA((orbs + 2,)),
+        ],
         compiler_params=params,
         name="final",
     )(sums, high, low, phigh, plow)

time: 30.3 us -> 27.4 us (0.904)
  Pallas kernels: 10.5 us -> 7.14 us
  blocking collectives: 11.6 us -> 12.1 us
    pallas_call x1, Pallas kernels: 4.17 us -> 1.92 us  [per_device(): pl.pallas_call(lambda *refs: final_kernel(count, *refs), out_shape=[jax.S...]
    pallas_call x1, Pallas kernels: 1.88 us -> 1.29 us  [per_device(): pl.pallas_call(halo_kernel, out_shape=[pltpu.VMEM((orbs, nx, side, nz), B...]
    pallas_call x1, Pallas kernels: 3.19 us -> 2.62 us  [per_device(): pl.pallas_call(interior_kernel, out_shape=[pltpu.VMEM(block.shape, F32),...]
    all_to_all x1, blocking collectives: 11.6 us -> 12.1 us  [per_device(): sums = lax.all_to_all(sums, ('gx', 'gy'), 0, 0)]
  transfers between devices with their start and end apart: 4 -> 4, of which waited for: 0 -> 0; matrix products, arithmetic and copies ran while one was open for 0% -> 0% of each run, Pallas kernels for 11% -> 10%
where the time goes in v4:
time: 27.4 us; the launch traced here: 27.3 us
  blocking collectives  12.1 us (44%)
  starting transfers between devices  7.28 us (27%)
  Pallas kernels  7.14 us (26%)
  between operations  0.68 us (2%)
    all_to_all x1, blocking collectives, per_device(): sums = lax.all_to_all(sums, ('gx', 'gy'), 0, 0)  12.1 us
    ppermute x4, starting transfers between devices, shifted(): lax.ppermute(value, axis, [(i, (i + steps) % count) for i in range(count)])  7.28 us
    pallas_call x1, Pallas kernels, per_device(): pl.pallas_call(interior_kernel, out_shape=[pltpu.VMEM(block.shape, F32),...  2.62 us
    pallas_call x1, Pallas kernels, per_device(): pl.pallas_call(lambda *refs: final_kernel(count, *refs), out_shape=[jax.S...  1.92 us
    pallas_call x1, Pallas kernels, per_device(): pl.pallas_call(pack_kernel, in_specs=[outside] * 5, out_shape=[pltpu.VMEM...  1.3 us
    pallas_call x1, Pallas kernels, per_device(): pl.pallas_call(halo_kernel, out_shape=[pltpu.VMEM((orbs, nx, side, nz), B...  1.29 us
  transfers between devices with their start and end apart: 4, of which 0 were waited for; matrix products, arithmetic and copies ran while one was open for 0% of the time, Pallas kernels for 10%

profile of v4, /device:TPU:0, one launch (start us, length us, event | category | flops | bytes accessed | tf_op | source)
XLA Modules:
  0.0 27.3 jit_solution(11571674640399855727)
XLA Ops:
  0.6 0.0 copy-start
  0.6 1.3 %pack.1 = (f32[3,8,8,8,128]{4,3,2,1,0:T(8,128)S(1)}, s32[3,8,8,128]{3,2,1,0:T(8,128)S(1)}, s32[8,8,128]{2,1,0:T(8,128)S(1)}, f32[3,3,3,16]{3,2,1,0:T(4,128)S(1)}...) custom-call(f32[3,8,8,8,128]{4,3,2,1,0:T(8,128)} %block_in.1, ...), custom_call_target="tpu_custom_call" | custom-call | tf_op jit(solution)/shard_map/pack/pallas_call | solution.py:411
  1.9 3.0 %collective-permute-start = (f32[25,8,128]{2,1,0:T(8,128)S(1)}, f32[25,8,128]{2,1,0:T(8,128)S(1)}, u32[]{:S(2)}, u32[]{:S(2)}) collective-permute-start(f32[25,8,128]{2,1,0:T(8,128)S(1)} %get-tuple-element.27), channel_id=1, source_target_pairs={{0,8},{8,16},{16,24},{24,0},{1,9},{9,17},{17,25},{25,1},{2,10},{10... | collective-permute-start | bytes 307208 | tf_op jit(solution)/shard_map/ppermute | solution.py:393
  4.9 0.0 collective-permute-start.2
  4.9 1.1 %collective-permute-start.1 = (f32[24,8,128]{2,1,0:T(8,128)S(1)}, f32[24,8,128]{2,1,0:T(8,128)S(1)}, u32[]{:S(2)}, u32[]{:S(2)}) collective-permute-start(f32[24,8,128]{2,1,0:T(8,128)S(1)} %get-tuple-element.28), channel_id=1, source_target_pairs={{0,24},{8,0},{16,8},{24,16},{1,25},{9,1},{17,9},{25,17},{2,26},{10... | collective-permute-start | bytes 294920 | tf_op jit(solution)/shard_map/ppermute | solution.py:393
  6.0 3.2 %collective-permute-start.3 = (f32[24,8,128]{2,1,0:T(8,128)S(1)}, f32[24,8,128]{2,1,0:T(8,128)S(1)}, u32[]{:S(2)}, u32[]{:S(2)}) collective-permute-start(f32[24,8,128]{2,1,0:T(8,128)S(1)} %get-tuple-element.30), channel_id=1, source_target_pairs={{0,7},{1,0},{2,1},{3,2},{4,3},{5,4},{6,5},{7,6},{8,15},{9,8},{10,9... | collective-permute-start | bytes 294920 | tf_op jit(solution)/shard_map/ppermute | solution.py:393
  9.2 0.0 copy-done
  9.2 2.6 %interior.1 = (f32[3,8,8,8,128]{4,3,2,1,0:T(8,128)S(1)}, bf16[3,8,128,128]{3,2,1,0:T(8,128)(2,1)S(1)}, bf16[3,8,128,128]{3,2,1,0:T(8,128)(2,1)S(1)}, f32[8,128]{1,0:T(8,128)S(1)}, f32[35,128]{1,0:T(8,128)S(1)}) custom-call(f32[3,8,8,8,128]{4,3,2,1,0:T(8,128)S(1)} %copy-done, f32[3,8,8,8,128]{4,3,2,1,0:T(8,128)S(1)} %get-tuple-element.20.block_ref, ...), custom_call_target="tpu_custom_call" | custom-call | flops 100000000 | bytes 4000000 | tf_op jit(solution)/shard_map/interior/pallas_call | solution.py:435
  11.9 0.0 collective-permute-done.1.xhigh_ref
  11.9 0.0 collective-permute-done.3.yhigh_ref
  11.9 0.0 collective-permute-done.xlow_ref
  11.9 0.0 collective-permute-done.2.ylow_ref
  11.9 1.3 %halo.1 = (bf16[3,8,64,128]{3,2,1,0:T(8,128)(2,1)S(1)}, bf16[3,8,64,128]{3,2,1,0:T(8,128)(2,1)S(1)}, f32[32,4,128]{2,1,0:T(4,128)S(1)}, f32[3,8,8,8,128]{4,3,2,1,0:T(8,128)S(1)}) custom-call(f32[3,8,8,8,128]{4,3,2,1,0:T(8,128)S(1)} %get-tuple-element.25.part_in, s32[3,8,8,128]{3,2,1,0:T(8,128)S(1)} %get-tuple-element.21.seed_ref, ...), custom_call_target="tpu_custom_call", output_to_operand_aliasing={{3}: (0, {})} | custom-call | tf_op jit(solution)/shard_map/halo/pallas_call | solution.py:450
  13.2 12.1 %all_to_all.5.refs_0_ = f32[32,4,128]{2,1,0:T(4,128)S(1)} all-to-all(f32[32,4,128]{2,1,0:T(4,128)S(1)} %get-tuple-element.34), channel_id=1, replica_groups=mesh['gx'=4,'gy'=8] {'gx','gy'}, dimensions={0} | all-to-all | bytes 131072 | tf_op jit(solution)/shard_map/all_to_all | solution.py:464
  25.3 1.9 %final.1 = (f32[3,8,8,8,128]{4,3,2,1,0:T(8,128)}, f32[8,8]{1,0:T(8,128)}, f32[8,8]{1,0:T(8,128)}) custom-call(f32[32,4,128]{2,1,0:T(4,128)S(1)} %all_to_all.5.refs_0_, bf16[3,8,128,128]{3,2,1,0:T(8,128)(2,1)S(1)} %get-tuple-element.31.high_ref.refs_1_, bf16[3,8,128,128]{3,2,1,0:T(8,128)(2,1)S(1)} %get-tuple-element.32.low_ref.refs_2_, ...), custom_call_target="tpu_custom_call" | custom-call | tf_op jit(solution)/shard_map/final/pallas_call | solution.py:466
Async XLA Ops:
  0.6 8.6 %copy-start = (f32[3,8,8,8,128]{4,3,2,1,0:T(8,128)S(1)}, f32[3,8,8,8,128]{4,3,2,1,0:T(8,128)}, u32[]{:S(2)}) copy-start(f32[3,8,8,8,128]{4,3,2,1,0:T(8,128)} %prev_ref.1) | copy-start | bytes 2359300
  1.9 9.9 %collective-permute-start = (f32[25,8,128]{2,1,0:T(8,128)S(1)}, f32[25,8,128]{2,1,0:T(8,128)S(1)}, u32[]{:S(2)}, u32[]{:S(2)}) collective-permute-start(f32[25,8,128]{2,1,0:T(8,128)S(1)} %get-tuple-element.27), channel_id=1, source_target_pairs={{0,8},{8,16},{16,24},{24,0},{1,9},{9,17},{17,25},{25,1},{2,10},{10... | collective-permute-start | bytes 307208 | tf_op jit(solution)/shard_map/ppermute | solution.py:393
  4.9 6.9 %collective-permute-start.2 = (f32[25,8,128]{2,1,0:T(8,128)S(1)}, f32[25,8,128]{2,1,0:T(8,128)S(1)}, u32[]{:S(2)}, u32[]{:S(2)}) collective-permute-start(f32[25,8,128]{2,1,0:T(8,128)S(1)} %get-tuple-element.29), channel_id=1, source_target_pairs={{0,1},{1,2},{2,3},{3,4},{4,5},{5,6},{6,7},{7,0},{8,9},{9,10},{10,1... | collective-permute-start | bytes 307208 | tf_op jit(solution)/shard_map/ppermute | solution.py:393
  4.9 6.9 %collective-permute-start.1 = (f32[24,8,128]{2,1,0:T(8,128)S(1)}, f32[24,8,128]{2,1,0:T(8,128)S(1)}, u32[]{:S(2)}, u32[]{:S(2)}) collective-permute-start(f32[24,8,128]{2,1,0:T(8,128)S(1)} %get-tuple-element.28), channel_id=1, source_target_pairs={{0,24},{8,0},{16,8},{24,16},{1,25},{9,1},{17,9},{25,17},{2,26},{10... | collective-permute-start | bytes 294920 | tf_op jit(solution)/shard_map/ppermute | solution.py:393
  6.0 5.8 %collective-permute-start.3 = (f32[24,8,128]{2,1,0:T(8,128)S(1)}, f32[24,8,128]{2,1,0:T(8,128)S(1)}, u32[]{:S(2)}, u32[]{:S(2)}) collective-permute-start(f32[24,8,128]{2,1,0:T(8,128)S(1)} %get-tuple-element.30), channel_id=1, source_target_pairs={{0,7},{1,0},{2,1},{3,2},{4,3},{5,4},{6,5},{7,6},{8,15},{9,8},{10,9... | collective-permute-start | bytes 294920 | tf_op jit(solution)/shard_map/ppermute | solution.py:393

commit v5 on v4

--- a/solution.py
+++ b/solution.py
@@ -70,13 +70,15 @@
     level_ref,
     hop_ref,
     onsite_ref,
-    xup_ref,
-    xdown_ref,
-    yup_ref,
-    ydown_ref,
+    xnear_ref,
+    yfar_ref,
+    ynear_ref,
+    xfar_ref,
     sems,
 ):
     orbs, width, nx, ny, _ = block_ref.shape
+    yeven = lax.axis_index("gy") % 2 == 0
+    near = nx - 1
     pairs = [(block_in.at[o], block_ref.at[o]) for o in range(orbs)]
     pairs += [(seed_in, seed_ref), (level_in, level_ref), (hop_in, hop_ref), (onsite_in, onsite_ref)]
     loads = [pltpu.make_async_copy(*pair, sems.at[i]) for i, pair in enumerate(pairs)]
@@ -86,13 +88,16 @@
         loads[o].wait()
         for n in range(width):
             spot = o * width + n
-            xup_ref[spot] = block_ref[o, n, nx - 1]
-            xdown_ref[spot] = block_ref[o, n, 0]
-            yup_ref[spot] = block_ref[o, n, :, ny - 1, :]
-            ydown_ref[spot] = block_ref[o, n, :, 0, :]
+            xnear_ref[spot] = block_ref[o, n, near]
+            xfar_ref[spot] = block_ref[o, n, nx - 1 - near]
+            top, bottom = block_ref[o, n, :, ny - 1, :], block_ref[o, n, :, 0, :]
+            ynear_ref[spot] = jnp.where(yeven, top, bottom)
+            yfar_ref[spot] = jnp.where(yeven, bottom, top)
     loads[orbs].wait()
-    xup_ref[orbs * width] = seed_ref[0, nx - 1].astype(F32)
-    yup_ref[orbs * width] = seed_ref[1, :, ny - 1, :].astype(F32)
+    for ref in (xnear_ref, xfar_ref):
+        ref[orbs * width] = seed_ref[0, nx - 1].astype(F32)
+    for ref in (ynear_ref, yfar_ref):
+        ref[orbs * width] = seed_ref[1, :, ny - 1, :].astype(F32)
     for load in loads[orbs + 1 :]:
         load.wait()
 
@@ -196,10 +201,10 @@
     part_in,
     seed_ref,
     table_ref,
-    xlow_ref,
-    xhigh_ref,
-    ylow_ref,
-    yhigh_ref,
+    xnear_ref,
+    yfar_ref,
+    ynear_ref,
+    xfar_ref,
     high_ref,
     low_ref,
     metric_ref,
@@ -213,22 +218,30 @@
     side = width * ny
     last = orbs * width
 
-    bond_x = bonds_of(table_ref, 0, seed_ref[0, nx - 1], orbs)
-    bond_xlow = bonds_of(table_ref, 0, xlow_ref[last].astype(jnp.int32), orbs)
-    for n in range(width):
-        forward = times(bond_x, [xhigh_ref[o * width + n] for o in range(orbs)])
-        back = times_transposed(bond_xlow, [xlow_ref[o * width + n] for o in range(orbs)])
-        for o in range(orbs):
-            part_ref[o, n, nx - 1] += forward[o]
-            part_ref[o, n, 0] += back[o]
-    bond_y = bonds_of(table_ref, 1, seed_ref[1, :, ny - 1, :], orbs)
-    bond_ylow = bonds_of(table_ref, 1, ylow_ref[last].astype(jnp.int32), orbs)
-    for n in range(width):
-        forward = times(bond_y, [yhigh_ref[o * width + n] for o in range(orbs)])
-        back = times_transposed(bond_ylow, [ylow_ref[o * width + n] for o in range(orbs)])
-        for o in range(orbs):
-            part_ref[o, n, :, ny - 1, :] += forward[o]
-            part_ref[o, n, :, 0, :] += back[o]
+    def add_x(low_ref, high_ref):
+        bond = bonds_of(table_ref, 0, seed_ref[0, nx - 1], orbs)
+        bond_low = bonds_of(table_ref, 0, low_ref[last].astype(jnp.int32), orbs)
+        for n in range(width):
+            forward = times(bond, [high_ref[o * width + n] for o in range(orbs)])
+            back = times_transposed(bond_low, [low_ref[o * width + n] for o in range(orbs)])
+            for o in range(orbs):
+                part_ref[o, n, nx - 1] += forward[o]
+                part_ref[o, n, 0] += back[o]
+
+    def add_y(low_ref, high_ref):
+        bond = bonds_of(table_ref, 1, seed_ref[1, :, ny - 1, :], orbs)
+        bond_low = bonds_of(table_ref, 1, low_ref[last].astype(jnp.int32), orbs)
+        for n in range(width):
+            forward = times(bond, [high_ref[o * width + n] for o in range(orbs)])
+            back = times_transposed(bond_low, [low_ref[o * width + n] for o in range(orbs)])
+            for o in range(orbs):
+                part_ref[o, n, :, ny - 1, :] += forward[o]
+                part_ref[o, n, :, 0, :] += back[o]
+
+    yeven = lax.axis_index("gy") % 2 == 0
+    add_x(xnear_ref, xfar_ref)
+    pl.when(yeven)(lambda: add_y(yfar_ref, ynear_ref))
+    pl.when(jnp.logical_not(yeven))(lambda: add_y(ynear_ref, yfar_ref))
 
     total_ref[...] = jnp.zeros(total_ref.shape, F32)
 
@@ -393,6 +406,13 @@
     return lax.ppermute(value, axis, [(i, (i + steps) % count) for i in range(count)])
 
 
+def swapped(value, axis, far):
+    count = lax.axis_size(axis)
+    return lax.ppermute(
+        value, axis, [(i, (i + (1 if i % 2 == far else -1)) % count) for i in range(count)]
+    )
+
+
 def per_device(prev_block, block, hop_seed, levels, hop_table, onsite_table):
     orbs, width, nx, ny, nz = block.shape
     devices = lax.axis_size("gx") * lax.axis_size("gy")
@@ -408,7 +428,7 @@
 
     params = pltpu.CompilerParams(**PARAMS)
 
-    block_here, seed_here, levels_here, hops_here, onsite_here, xup, xdown, yup, ydown = pl.pallas_call(
+    block_here, seed_here, levels_here, hops_here, onsite_here, xnear, yfar, ynear, xfar = pl.pallas_call(
         pack_kernel,
         in_specs=[outside] * 5,
         out_shape=[
@@ -418,18 +438,18 @@
             pltpu.VMEM(hops.shape, F32),
             pltpu.VMEM(onsite.shape, F32),
             pltpu.VMEM((fields + 1, ny, nz), F32),
-            pltpu.VMEM((fields, ny, nz), F32),
             pltpu.VMEM((fields + 1, nx, nz), F32),
-            pltpu.VMEM((fields, nx, nz), F32),
+            pltpu.VMEM((fields + 1, nx, nz), F32),
+            pltpu.VMEM((fields + 1, ny, nz), F32),
         ],
         scratch_shapes=[pltpu.SemaphoreType.DMA((orbs + 4,))],
         compiler_params=params,
         name="pack",
     )(stay(block), stay(hop_seed), stay(levels), stay(hops), stay(onsite))
-    xlow = shifted(xup, "gx", 1)
-    ylow = shifted(yup, "gy", 1)
-    xhigh = shifted(xdown, "gx", -1)
-    yhigh = shifted(ydown, "gy", -1)
+    xnear = shifted(xnear, "gx", 1)
+    yfar = swapped(yfar, "gy", 1)
+    ynear = swapped(ynear, "gy", 0)
+    xfar = shifted(xfar, "gx", -1)
 
     side = width * ny
     part, high, low, metric, table = pl.pallas_call(
@@ -459,7 +479,7 @@
         scratch_shapes=[pltpu.VMEM((6 * side, 2 * side), F32)],
         compiler_params=params,
         name="halo",
-    )(part, seed_here, table, xlow, xhigh, ylow, yhigh, high, low, metric)
+    )(part, seed_here, table, xnear, yfar, ynear, xfar, high, low, metric)
 
     sums = lax.all_to_all(sums, ("gx", "gy"), 0, 0)
 

time: 27.4 us -> 26.9 us (0.982)
  blocking collectives: 12.1 us -> 10.4 us
  waiting for transfers between devices: 0.01 us -> 1.22 us
    ppermute x4 -> x2, starting transfers between devices: 7.28 us -> 4.42 us  [shifted(): lax.ppermute(value, axis, [(i, (i + steps) % count) for i in range(count)])]
    ppermute x0 -> x2, starting transfers between devices: none -> 2.76 us  [swapped(): lax.ppermute(value, axis, [(i, (i + (1 if i % 2 == far else -1)) % count)...]
    all_to_all x1, blocking collectives: 12.1 us -> 10.4 us  [per_device(): sums = lax.all_to_all(sums, ('gx', 'gy'), 0, 0)]
    ppermute x4 -> x2, waiting for transfers between devices: 0.01 us -> 1.21 us  [shifted(): lax.ppermute(value, axis, [(i, (i + steps) % count) for i in range(count)])]
  transfers between devices with their start and end apart: 4 -> 4, of which waited for: 0 -> 1; matrix products, arithmetic and copies ran while one was open for 0% -> 0% of each run, Pallas kernels for 10% -> 10%
where the time goes in v5:
time: 26.9 us; the launch traced here: 26.7 us
  blocking collectives  10.4 us (39%)
  Pallas kernels  7.22 us (27%)
  starting transfers between devices  7.19 us (27%)
  waiting for transfers between devices  1.22 us (5%)
  between operations  0.68 us (3%)
    all_to_all x1, blocking collectives, per_device(): sums = lax.all_to_all(sums, ('gx', 'gy'), 0, 0)  10.4 us
    ppermute x2, starting transfers between devices, shifted(): lax.ppermute(value, axis, [(i, (i + steps) % count) for i in range(count)])  4.42 us
    ppermute x2, starting transfers between devices, swapped(): lax.ppermute(value, axis, [(i, (i + (1 if i % 2 == far else -1)) % count)...  2.76 us
    pallas_call x1, Pallas kernels, per_device(): pl.pallas_call(interior_kernel, out_shape=[pltpu.VMEM(block.shape, F32),...  2.62 us
    pallas_call x1, Pallas kernels, per_device(): pl.pallas_call(lambda *refs: final_kernel(count, *refs), out_shape=[jax.S...  1.93 us
    pallas_call x1, Pallas kernels, per_device(): pl.pallas_call(halo_kernel, out_shape=[pltpu.VMEM((orbs, nx, side, nz), B...  1.36 us
    pallas_call x1, Pallas kernels, per_device(): pl.pallas_call(pack_kernel, in_specs=[outside] * 5, out_shape=[pltpu.VMEM...  1.31 us
    ppermute x2, waiting for transfers between devices, shifted(): lax.ppermute(value, axis, [(i, (i + steps) % count) for i in range(count)])  1.21 us
  transfers between devices with their start and end apart: 4, of which 1 were waited for; matrix products, arithmetic and copies ran while one was open for 0% of the time, Pallas kernels for 10%

profile of v5, /device:TPU:0, one launch (start us, length us, event | category | flops | bytes accessed | tf_op | source)
XLA Modules:
  0.0 26.7 jit_solution(11703060790066534024)
XLA Ops:
  0.6 0.0 copy-start
  0.6 1.3 %pack.1 = (f32[3,8,8,8,128]{4,3,2,1,0:T(8,128)S(1)}, s32[3,8,8,128]{3,2,1,0:T(8,128)S(1)}, s32[8,8,128]{2,1,0:T(8,128)S(1)}, f32[3,3,3,16]{3,2,1,0:T(4,128)S(1)}...) custom-call(f32[3,8,8,8,128]{4,3,2,1,0:T(8,128)} %block_in.1, ...), custom_call_target="tpu_custom_call" | custom-call | tf_op jit(solution)/shard_map/pack/pallas_call | solution.py:431
  2.0 3.0 %collective-permute-start = (f32[25,8,128]{2,1,0:T(8,128)S(1)}, f32[25,8,128]{2,1,0:T(8,128)S(1)}, u32[]{:S(2)}, u32[]{:S(2)}) collective-permute-start(f32[25,8,128]{2,1,0:T(8,128)S(1)} %get-tuple-element.27), channel_id=1, source_target_pairs={{0,8},{8,16},{16,24},{24,0},{1,9},{9,17},{17,25},{25,1},{2,10},{10... | collective-permute-start | bytes 307208 | tf_op jit(solution)/shard_map/ppermute | solution.py:406
  5.0 2.8 %collective-permute-start.1 = (f32[25,8,128]{2,1,0:T(8,128)S(1)}, f32[25,8,128]{2,1,0:T(8,128)S(1)}, u32[]{:S(2)}, u32[]{:S(2)}) collective-permute-start(f32[25,8,128]{2,1,0:T(8,128)S(1)} %get-tuple-element.28), channel_id=1, source_target_pairs={{0,7},{1,2},{2,1},{3,4},{4,3},{5,6},{6,5},{7,0},{8,15},{9,10},{10,... | collective-permute-start | bytes 307208 | tf_op jit(solution)/shard_map/ppermute | solution.py:411
  7.7 0.0 collective-permute-start.2
  7.7 1.4 %collective-permute-start.3 = (f32[25,8,128]{2,1,0:T(8,128)S(1)}, f32[25,8,128]{2,1,0:T(8,128)S(1)}, u32[]{:S(2)}, u32[]{:S(2)}) collective-permute-start(f32[25,8,128]{2,1,0:T(8,128)S(1)} %get-tuple-element.30), channel_id=1, source_target_pairs={{0,24},{8,0},{16,8},{24,16},{1,25},{9,1},{17,9},{25,17},{2,26},{10... | collective-permute-start | bytes 307208 | tf_op jit(solution)/shard_map/ppermute | solution.py:406
  9.1 0.0 copy-done
  9.2 2.6 %interior.1 = (f32[3,8,8,8,128]{4,3,2,1,0:T(8,128)S(1)}, bf16[3,8,128,128]{3,2,1,0:T(8,128)(2,1)S(1)}, bf16[3,8,128,128]{3,2,1,0:T(8,128)(2,1)S(1)}, f32[8,128]{1,0:T(8,128)S(1)}, f32[35,128]{1,0:T(8,128)S(1)}) custom-call(f32[3,8,8,8,128]{4,3,2,1,0:T(8,128)S(1)} %copy-done, f32[3,8,8,8,128]{4,3,2,1,0:T(8,128)S(1)} %get-tuple-element.20.block_ref, ...), custom_call_target="tpu_custom_call" | custom-call | flops 100000000 | bytes 4000000 | tf_op jit(solution)/shard_map/interior/pallas_call | solution.py:455
  11.8 0.0 collective-permute-done.xnear_ref
  11.8 0.0 collective-permute-done.1.yfar_ref
  11.8 0.0 collective-permute-done.2.ynear_ref
  11.8 1.2 %collective-permute-done.3.xfar_ref = f32[25,8,128]{2,1,0:T(8,128)S(1)} collective-permute-done((f32[25,8,128]{2,1,0:T(8,128)S(1)}, f32[25,8,128]{2,1,0:T(8,128)S(1)}, u32[]{:S(2)}, u32[]{:S(2)}) %collective-permute-start.3) | collective-permute-done | bytes 102432 | tf_op jit(solution)/shard_map/ppermute | solution.py:406
  13.0 1.4 %halo.1 = (bf16[3,8,64,128]{3,2,1,0:T(8,128)(2,1)S(1)}, bf16[3,8,64,128]{3,2,1,0:T(8,128)(2,1)S(1)}, f32[32,4,128]{2,1,0:T(4,128)S(1)}, f32[3,8,8,8,128]{4,3,2,1,0:T(8,128)S(1)}) custom-call(f32[3,8,8,8,128]{4,3,2,1,0:T(8,128)S(1)} %get-tuple-element.25.part_in, s32[3,8,8,128]{3,2,1,0:T(8,128)S(1)} %get-tuple-element.21.seed_ref, ...), custom_call_target="tpu_custom_call", output_to_operand_aliasing={{3}: (0, {})} | custom-call | tf_op jit(solution)/shard_map/halo/pallas_call | solution.py:470
  14.4 10.4 %all_to_all.5.refs_0_ = f32[32,4,128]{2,1,0:T(4,128)S(1)} all-to-all(f32[32,4,128]{2,1,0:T(4,128)S(1)} %get-tuple-element.34), channel_id=1, replica_groups=mesh['gx'=4,'gy'=8] {'gx','gy'}, dimensions={0} | all-to-all | bytes 131072 | tf_op jit(solution)/shard_map/all_to_all | solution.py:484
  24.8 1.9 %final.1 = (f32[3,8,8,8,128]{4,3,2,1,0:T(8,128)}, f32[8,8]{1,0:T(8,128)}, f32[8,8]{1,0:T(8,128)}) custom-call(f32[32,4,128]{2,1,0:T(4,128)S(1)} %all_to_all.5.refs_0_, bf16[3,8,128,128]{3,2,1,0:T(8,128)(2,1)S(1)} %get-tuple-element.31.high_ref.refs_1_, bf16[3,8,128,128]{3,2,1,0:T(8,128)(2,1)S(1)} %get-tuple-element.32.low_ref.refs_2_, ...), custom_call_target="tpu_custom_call" | custom-call | tf_op jit(solution)/shard_map/final/pallas_call | solution.py:486
Async XLA Ops:
  0.6 8.5 %copy-start = (f32[3,8,8,8,128]{4,3,2,1,0:T(8,128)S(1)}, f32[3,8,8,8,128]{4,3,2,1,0:T(8,128)}, u32[]{:S(2)}) copy-start(f32[3,8,8,8,128]{4,3,2,1,0:T(8,128)} %prev_ref.1) | copy-start | bytes 2359300
  2.0 9.8 %collective-permute-start = (f32[25,8,128]{2,1,0:T(8,128)S(1)}, f32[25,8,128]{2,1,0:T(8,128)S(1)}, u32[]{:S(2)}, u32[]{:S(2)}) collective-permute-start(f32[25,8,128]{2,1,0:T(8,128)S(1)} %get-tuple-element.27), channel_id=1, source_target_pairs={{0,8},{8,16},{16,24},{24,0},{1,9},{9,17},{17,25},{25,1},{2,10},{10... | collective-permute-start | bytes 307208 | tf_op jit(solution)/shard_map/ppermute | solution.py:406
  5.0 6.8 %collective-permute-start.1 = (f32[25,8,128]{2,1,0:T(8,128)S(1)}, f32[25,8,128]{2,1,0:T(8,128)S(1)}, u32[]{:S(2)}, u32[]{:S(2)}) collective-permute-start(f32[25,8,128]{2,1,0:T(8,128)S(1)} %get-tuple-element.28), channel_id=1, source_target_pairs={{0,7},{1,2},{2,1},{3,4},{4,3},{5,6},{6,5},{7,0},{8,15},{9,10},{10,... | collective-permute-start | bytes 307208 | tf_op jit(solution)/shard_map/ppermute | solution.py:411
  7.7 4.1 %collective-permute-start.2 = (f32[25,8,128]{2,1,0:T(8,128)S(1)}, f32[25,8,128]{2,1,0:T(8,128)S(1)}, u32[]{:S(2)}, u32[]{:S(2)}) collective-permute-start(f32[25,8,128]{2,1,0:T(8,128)S(1)} %get-tuple-element.29), channel_id=1, source_target_pairs={{0,1},{1,0},{2,3},{3,2},{4,5},{5,4},{6,7},{7,6},{8,9},{9,8},{10,11... | collective-permute-start | bytes 307208 | tf_op jit(solution)/shard_map/ppermute | solution.py:411
  7.7 5.3 %collective-permute-start.3 = (f32[25,8,128]{2,1,0:T(8,128)S(1)}, f32[25,8,128]{2,1,0:T(8,128)S(1)}, u32[]{:S(2)}, u32[]{:S(2)}) collective-permute-start(f32[25,8,128]{2,1,0:T(8,128)S(1)} %get-tuple-element.30), channel_id=1, source_target_pairs={{0,24},{8,0},{16,8},{24,16},{1,25},{9,1},{17,9},{25,17},{2,26},{10... | collective-permute-start | bytes 307208 | tf_op jit(solution)/shard_map/ppermute | solution.py:406

commit v6 on v5

--- a/solution.py
+++ b/solution.py
@@ -70,15 +70,14 @@
     level_ref,
     hop_ref,
     onsite_ref,
-    xnear_ref,
+    xup_ref,
     yfar_ref,
     ynear_ref,
-    xfar_ref,
+    xdown_ref,
     sems,
 ):
     orbs, width, nx, ny, _ = block_ref.shape
     yeven = lax.axis_index("gy") % 2 == 0
-    near = nx - 1
     pairs = [(block_in.at[o], block_ref.at[o]) for o in range(orbs)]
     pairs += [(seed_in, seed_ref), (level_in, level_ref), (hop_in, hop_ref), (onsite_in, onsite_ref)]
     loads = [pltpu.make_async_copy(*pair, sems.at[i]) for i, pair in enumerate(pairs)]
@@ -88,14 +87,13 @@
         loads[o].wait()
         for n in range(width):
             spot = o * width + n
-            xnear_ref[spot] = block_ref[o, n, near]
-            xfar_ref[spot] = block_ref[o, n, nx - 1 - near]
+            xup_ref[spot] = block_ref[o, n, nx - 1]
+            xdown_ref[spot] = block_ref[o, n, 0]
             top, bottom = block_ref[o, n, :, ny - 1, :], block_ref[o, n, :, 0, :]
             ynear_ref[spot] = jnp.where(yeven, top, bottom)
             yfar_ref[spot] = jnp.where(yeven, bottom, top)
     loads[orbs].wait()
-    for ref in (xnear_ref, xfar_ref):
-        ref[orbs * width] = seed_ref[0, nx - 1].astype(F32)
+    xup_ref[orbs * width] = seed_ref[0, nx - 1].astype(F32)
     for ref in (ynear_ref, yfar_ref):
         ref[orbs * width] = seed_ref[1, :, ny - 1, :].astype(F32)
     for load in loads[orbs + 1 :]:
@@ -118,7 +116,7 @@
 
 
 def interior_kernel(
-    prev_ref,
+    prev_in,
     block_ref,
     seed_ref,
     level_ref,
@@ -130,8 +128,12 @@
     metric_ref,
     table_ref,
     gram_ref,
+    prev_ref,
+    sem,
 ):
     orbs, width, nx, ny, nz = block_ref.shape
+    load = pltpu.make_async_copy(prev_in, prev_ref, sem)
+    load.start()
     fill_table(table_ref, hop_ref, onsite_ref)
     row = iota((ny, nz), 0)
     side = width * ny
@@ -167,6 +169,7 @@
         return carry
 
     lax.fori_loop(0, nx, stencil, 0)
+    load.wait()
     gram_ref[...] = jnp.zeros(gram_ref.shape, F32)
 
     def products(pair):
@@ -197,20 +200,38 @@
     metric_ref[...] = gathered(jnp.concatenate(parts, 1), jnp.concatenate(maps, 0))
 
 
-def halo_kernel(
+def placed(total, base):
+    width = base.shape[0]
+    sums = kept_sums(total)
+    spots = (iota((LANES, LANES), 0) // ROWS) % width
+    sums = gathered(sums, jnp.where(iota((LANES, LANES), 1) % width == spots, 1.0, 0.0))
+    place = (iota(base.shape, 1) % (LANES // 2)) // width
+    for i in range(3):
+        base = base + jnp.where(place == i, sums[i * width : (i + 1) * width], 0.0)
+    return base
+
+
+def product_sums(bhigh, blow, high, low):
+    both = dot(
+        jnp.concatenate([bhigh, high, blow, low], 0), jnp.concatenate([high, low], 0), ((1,), (1,))
+    )
+    half = both.shape[0] // 2
+    return both[:half] + both[half:]
+
+
+def y_kernel(
     part_in,
     seed_ref,
     table_ref,
-    xnear_ref,
-    yfar_ref,
-    ynear_ref,
-    xfar_ref,
+    up_ref,
+    far_ref,
+    near_ref,
     high_ref,
     low_ref,
     metric_ref,
     phigh_ref,
     plow_ref,
-    sums_ref,
+    packed_ref,
     part_ref,
     total_ref,
 ):
@@ -218,63 +239,76 @@
     side = width * ny
     last = orbs * width
 
-    def add_x(low_ref, high_ref):
-        bond = bonds_of(table_ref, 0, seed_ref[0, nx - 1], orbs)
-        bond_low = bonds_of(table_ref, 0, low_ref[last].astype(jnp.int32), orbs)
+    bond_low = bonds_of(table_ref, 0, up_ref[last].astype(jnp.int32), orbs)
+    for n in range(width):
+        back = times_transposed(bond_low, [up_ref[o * width + n] for o in range(orbs)])
+        for o in range(orbs):
+            part_ref[o, n, 0] += back[o]
+
+    def add_faces(low_face, high_face):
+        bond = bonds_of(table_ref, 1, seed_ref[1, :, ny - 1, :], orbs)
+        bond_low = bonds_of(table_ref, 1, low_face[last].astype(jnp.int32), orbs)
         for n in range(width):
-            forward = times(bond, [high_ref[o * width + n] for o in range(orbs)])
-            back = times_transposed(bond_low, [low_ref[o * width + n] for o in range(orbs)])
-            for o in range(orbs):
-                part_ref[o, n, nx - 1] += forward[o]
-                part_ref[o, n, 0] += back[o]
-
-    def add_y(low_ref, high_ref):
-        bond = bonds_of(table_ref, 1, seed_ref[1, :, ny - 1, :], orbs)
-        bond_low = bonds_of(table_ref, 1, low_ref[last].astype(jnp.int32), orbs)
-        for n in range(width):
-            forward = times(bond, [high_ref[o * width + n] for o in range(orbs)])
-            back = times_transposed(bond_low, [low_ref[o * width + n] for o in range(orbs)])
+            forward = times(bond, [high_face[o * width + n] for o in range(orbs)])
+            back = times_transposed(bond_low, [low_face[o * width + n] for o in range(orbs)])
             for o in range(orbs):
                 part_ref[o, n, :, ny - 1, :] += forward[o]
                 part_ref[o, n, :, 0, :] += back[o]
 
-    yeven = lax.axis_index("gy") % 2 == 0
-    add_x(xnear_ref, xfar_ref)
-    pl.when(yeven)(lambda: add_y(yfar_ref, ynear_ref))
-    pl.when(jnp.logical_not(yeven))(lambda: add_y(ynear_ref, yfar_ref))
+    even = lax.axis_index("gy") % 2 == 0
+    pl.when(even)(lambda: add_faces(far_ref, near_ref))
+    pl.when(jnp.logical_not(even))(lambda: add_faces(near_ref, far_ref))
 
     total_ref[...] = jnp.zeros(total_ref.shape, F32)
-
-    def products(pair):
+    for first in range(1, nx - 1, 2):
         for o in range(orbs):
             ins = [[], [], [], []]
-            for half in range(2):
-                x = 2 * pair + half
+            for x in (first, first + 1):
                 high, low = split(part_ref[o, :, x].reshape(side, nz))
                 phigh_ref[o, x] = high
                 plow_ref[o, x] = low
-                for group, value in zip(ins, (high, low, high_ref[o, x], low_ref[o, x])):
+                for group, value in zip(ins, (high_ref[o, x], low_ref[o, x], high, low)):
                     group.append(value)
-            high, low, bhigh, blow = (jnp.concatenate(group, 1) for group in ins)
-            total_ref[...] += dot(
-                jnp.concatenate([bhigh, high, blow, low], 0),
-                jnp.concatenate([high, low], 0),
-                ((1,), (1,)),
-            )
-
-    for pair in range(nx // 2):
-        products(pair)
-
-    sums = kept_sums(total_ref[: 3 * side] + total_ref[3 * side :])
-    spots = (iota((LANES, LANES), 0) // ny) % width
-    sums = gathered(sums, jnp.where(iota((LANES, LANES), 1) % width == spots, 1.0, 0.0))
-    lanes = iota((width, LANES), 1)
-    place = (lanes % (LANES // 2)) // width
-    packed = metric_ref[...]
-    for i in range(3):
-        packed = jnp.where(place == i, sums[i * width : (i + 1) * width], packed)
+            total_ref[...] += product_sums(*(jnp.concatenate(group, 1) for group in ins))
+    packed_ref[...] = placed(total_ref[...], metric_ref[...])
+
+
+def x_kernel(
+    part_ref,
+    seed_ref,
+    table_ref,
+    down_ref,
+    high_ref,
+    low_ref,
+    packed_ref,
+    phigh_in,
+    plow_in,
+    phigh_ref,
+    plow_ref,
+    sums_ref,
+    face_ref,
+):
+    orbs, width, nx, ny, nz = part_ref.shape
+    bond = bonds_of(table_ref, 0, seed_ref[0, nx - 1], orbs)
+    for n in range(width):
+        forward = times(bond, [down_ref[o * width + n] for o in range(orbs)])
+        for o in range(orbs):
+            face_ref[o, n * ny : (n + 1) * ny, :nz] = part_ref[o, n, 0]
+            face_ref[o, n * ny : (n + 1) * ny, nz:] = part_ref[o, n, nx - 1] + forward[o]
+    total = 0.0
+    for o in range(orbs):
+        high, low = split(face_ref[o])
+        for i, x in enumerate((0, nx - 1)):
+            phigh_ref[o, x] = high[:, i * nz : (i + 1) * nz]
+            plow_ref[o, x] = low[:, i * nz : (i + 1) * nz]
+        bhigh, blow = (
+            jnp.concatenate([ref[o, 0], ref[o, nx - 1]], 1) for ref in (high_ref, low_ref)
+        )
+        total = total + product_sums(bhigh, blow, high, low)
+    packed = placed(total, packed_ref[...])
     half = width // 2
-    folded = jnp.where(lanes[:half] < LANES // 2, packed[:half], packed[half:])
+    lanes = iota((half, LANES), 1)
+    folded = jnp.where(lanes < LANES // 2, packed[:half], packed[half:])
     sums_ref[...] = jnp.broadcast_to(folded[None], sums_ref.shape)
 
 
@@ -428,7 +462,7 @@
 
     params = pltpu.CompilerParams(**PARAMS)
 
-    block_here, seed_here, levels_here, hops_here, onsite_here, xnear, yfar, ynear, xfar = pl.pallas_call(
+    block_here, seed_here, levels_here, hops_here, onsite_here, xup, yfar, ynear, xdown = pl.pallas_call(
         pack_kernel,
         in_specs=[outside] * 5,
         out_shape=[
@@ -440,16 +474,16 @@
             pltpu.VMEM((fields + 1, ny, nz), F32),
             pltpu.VMEM((fields + 1, nx, nz), F32),
             pltpu.VMEM((fields + 1, nx, nz), F32),
-            pltpu.VMEM((fields + 1, ny, nz), F32),
+            pltpu.VMEM((fields, ny, nz), F32),
         ],
         scratch_shapes=[pltpu.SemaphoreType.DMA((orbs + 4,))],
         compiler_params=params,
         name="pack",
     )(stay(block), stay(hop_seed), stay(levels), stay(hops), stay(onsite))
-    xnear = shifted(xnear, "gx", 1)
+    xup = shifted(xup, "gx", 1)
     yfar = swapped(yfar, "gy", 1)
     ynear = swapped(ynear, "gy", 0)
-    xfar = shifted(xfar, "gx", -1)
+    xdown = shifted(xdown, "gx", -1)
 
     side = width * ny
     part, high, low, metric, table = pl.pallas_call(
@@ -461,25 +495,37 @@
             pltpu.VMEM((width, LANES), F32),
             pltpu.VMEM((table_rows, LANES), F32),
         ],
-        scratch_shapes=[pltpu.VMEM((2 * side, 4 * side), F32)],
+        in_specs=[outside] + [pl.BlockSpec(memory_space=pltpu.VMEM)] * 5,
+        scratch_shapes=[
+            pltpu.VMEM((2 * side, 4 * side), F32),
+            pltpu.VMEM(block.shape, F32),
+            pltpu.SemaphoreType.DMA(()),
+        ],
         compiler_params=params,
         cost_estimate=pl.CostEstimate(flops=10**8, bytes_accessed=4 * 10**6, transcendentals=0),
         name="interior",
-    )(prev_block, block_here, seed_here, levels_here, hops_here, onsite_here)
-
-    phigh, plow, sums, _ = pl.pallas_call(
-        halo_kernel,
-        out_shape=[
-            pltpu.VMEM((orbs, nx, side, nz), BF16),
-            pltpu.VMEM((orbs, nx, side, nz), BF16),
-            pltpu.VMEM((devices, width // 2, LANES), F32),
-            pltpu.VMEM(block.shape, F32),
-        ],
+    )(stay(prev_block), block_here, seed_here, levels_here, hops_here, onsite_here)
+
+    product_halves = [pltpu.VMEM((orbs, nx, side, nz), BF16)] * 2
+    phigh, plow, packed, part = pl.pallas_call(
+        y_kernel,
+        out_shape=product_halves
+        + [pltpu.VMEM((width, LANES), F32), pltpu.VMEM(block.shape, F32)],
         input_output_aliases={0: 3},
-        scratch_shapes=[pltpu.VMEM((6 * side, 2 * side), F32)],
+        scratch_shapes=[pltpu.VMEM((3 * side, 2 * side), F32)],
         compiler_params=params,
-        name="halo",
-    )(part, seed_here, table, xnear, yfar, ynear, xfar, high, low, metric)
+        cost_estimate=pl.CostEstimate(flops=10**8, bytes_accessed=4 * 10**6, transcendentals=0),
+        name="y_faces",
+    )(part, seed_here, table, xup, yfar, ynear, high, low, metric)
+
+    phigh, plow, sums = pl.pallas_call(
+        x_kernel,
+        out_shape=product_halves + [pltpu.VMEM((devices, width // 2, LANES), F32)],
+        input_output_aliases={7: 0, 8: 1},
+        scratch_shapes=[pltpu.VMEM((orbs, side, 2 * nz), F32)],
+        compiler_params=params,
+        name="x_faces",
+    )(part, seed_here, table, xdown, high, low, packed, phigh, plow)
 
     sums = lax.all_to_all(sums, ("gx", "gy"), 0, 0)
 

time: 26.9 us -> 25.9 us (0.963)
  waiting for transfers between devices: 1.22 us -> 0.01 us
  Pallas kernels: 7.22 us -> 7.56 us
    ppermute x2, waiting for transfers between devices: 1.21 us -> 0.01 us  [shifted(): lax.ppermute(value, axis, [(i, (i + steps) % count) for i in range(count)])]
    pallas_call x1 -> x2, Pallas kernels: 1.36 us -> 1.75 us  [the longest x1 1.17 us: per_device(): pl.pallas_call(y_kernel, out_shape=product_halves + [pltpu.VMEM((width, L...]
  transfers between devices with their start and end apart: 4 -> 4, of which waited for: 1 -> 0; matrix products, arithmetic and copies ran while one was open for 0% -> 0% of each run, Pallas kernels for 10% -> 15%
where the time goes in v6:
time: 25.9 us; the launch traced here: 25.8 us
  blocking collectives  10.3 us (40%)
  Pallas kernels  7.56 us (29%)
  starting transfers between devices  7.19 us (28%)
  between operations  0.7 us (3%)
    all_to_all x1, blocking collectives, per_device(): sums = lax.all_to_all(sums, ('gx', 'gy'), 0, 0)  10.3 us
    ppermute x2, starting transfers between devices, shifted(): lax.ppermute(value, axis, [(i, (i + steps) % count) for i in range(count)])  4.42 us
    ppermute x2, starting transfers between devices, swapped(): lax.ppermute(value, axis, [(i, (i + (1 if i % 2 == far else -1)) % count)...  2.76 us
    pallas_call x1, Pallas kernels, per_device(): pl.pallas_call(interior_kernel, out_shape=[pltpu.VMEM(block.shape, F32),...  2.65 us
    pallas_call x1, Pallas kernels, per_device(): pl.pallas_call(lambda *refs: final_kernel(count, *refs), out_shape=[jax.S...  1.93 us
    pallas_call x1, Pallas kernels, per_device(): pl.pallas_call(pack_kernel, in_specs=[outside] * 5, out_shape=[pltpu.VMEM...  1.24 us
    pallas_call x1, Pallas kernels, per_device(): pl.pallas_call(y_kernel, out_shape=product_halves + [pltpu.VMEM((width, L...  1.17 us
    pallas_call x1, Pallas kernels, per_device(): pl.pallas_call(x_kernel, out_shape=product_halves + [pltpu.VMEM((devices,...  0.58 us
  transfers between devices with their start and end apart: 4, of which 0 were waited for; matrix products, arithmetic and copies ran while one was open for 0% of the time, Pallas kernels for 15%

profile of v6, /device:TPU:0, one launch (start us, length us, event | category | flops | bytes accessed | tf_op | source)
XLA Modules:
  0.0 25.8 jit_solution(10222315430959439369)
XLA Ops:
  0.6 1.2 %pack.1 = (f32[3,8,8,8,128]{4,3,2,1,0:T(8,128)S(1)}, s32[3,8,8,128]{3,2,1,0:T(8,128)S(1)}, s32[8,8,128]{2,1,0:T(8,128)S(1)}, f32[3,3,3,16]{3,2,1,0:T(4,128)S(1)}...) custom-call(f32[3,8,8,8,128]{4,3,2,1,0:T(8,128)} %block_in.1, ...), custom_call_target="tpu_custom_call" | custom-call | tf_op jit(solution)/shard_map/pack/pallas_call | solution.py:465
  1.9 3.0 %collective-permute-start = (f32[25,8,128]{2,1,0:T(8,128)S(1)}, f32[25,8,128]{2,1,0:T(8,128)S(1)}, u32[]{:S(2)}, u32[]{:S(2)}) collective-permute-start(f32[25,8,128]{2,1,0:T(8,128)S(1)} %get-tuple-element.31), channel_id=1, source_target_pairs={{0,8},{8,16},{16,24},{24,0},{1,9},{9,17},{17,25},{25,1},{2,10},{10... | collective-permute-start | bytes 307208 | tf_op jit(solution)/shard_map/ppermute | solution.py:440
  4.9 2.8 %collective-permute-start.1 = (f32[25,8,128]{2,1,0:T(8,128)S(1)}, f32[25,8,128]{2,1,0:T(8,128)S(1)}, u32[]{:S(2)}, u32[]{:S(2)}) collective-permute-start(f32[25,8,128]{2,1,0:T(8,128)S(1)} %get-tuple-element.32), channel_id=1, source_target_pairs={{0,7},{1,2},{2,1},{3,4},{4,3},{5,6},{6,5},{7,0},{8,15},{9,10},{10,... | collective-permute-start | bytes 307208 | tf_op jit(solution)/shard_map/ppermute | solution.py:445
  7.6 0.0 collective-permute-start.2
  7.6 1.4 %collective-permute-start.3 = (f32[24,8,128]{2,1,0:T(8,128)S(1)}, f32[24,8,128]{2,1,0:T(8,128)S(1)}, u32[]{:S(2)}, u32[]{:S(2)}) collective-permute-start(f32[24,8,128]{2,1,0:T(8,128)S(1)} %get-tuple-element.38), channel_id=1, source_target_pairs={{0,24},{8,0},{16,8},{24,16},{1,25},{9,1},{17,9},{25,17},{2,26},{10... | collective-permute-start | bytes 294920 | tf_op jit(solution)/shard_map/ppermute | solution.py:440
  9.1 2.6 %interior.1 = (f32[3,8,8,8,128]{4,3,2,1,0:T(8,128)S(1)}, bf16[3,8,128,128]{3,2,1,0:T(8,128)(2,1)S(1)}, bf16[3,8,128,128]{3,2,1,0:T(8,128)(2,1)S(1)}, f32[8,128]{1,0:T(8,128)S(1)}, f32[35,128]{1,0:T(8,128)S(1)}) custom-call(f32[3,8,8,8,128]{4,3,2,1,0:T(8,128)} %prev_in.1, f32[3,8,8,8,128]{4,3,2,1,0:T(8,128)S(1)} %get-tuple-element.24.block_ref, ...), custom_call_target="tpu_custom_call" | custom-call | flops 100000000 | bytes 4000000 | tf_op jit(solution)/shard_map/interior/pallas_call | solution.py:489
  11.7 0.0 collective-permute-done.up_ref
  11.7 0.0 collective-permute-done.1.far_ref
  11.7 0.0 collective-permute-done.2.near_ref
  11.8 1.2 %y_faces.1 = (bf16[3,8,64,128]{3,2,1,0:T(8,128)(2,1)S(1)}, bf16[3,8,64,128]{3,2,1,0:T(8,128)(2,1)S(1)}, f32[8,128]{1,0:T(8,128)S(1)}, f32[3,8,8,8,128]{4,3,2,1,0:T(8,128)S(1)}) custom-call(f32[3,8,8,8,128]{4,3,2,1,0:T(8,128)S(1)} %get-tuple-element.29.part_in, s32[3,8,8,128]{3,2,1,0:T(8,128)S(1)} %get-tuple-element.25.seed_ref, ...), custom_call_target="tpu_custom_call", output_to_operand_aliasing={{3}: (0, {})} | custom-call | flops 100000000 | bytes 4000000 | tf_op jit(solution)/shard_map/y_faces/pallas_call | solution.py:510
  12.9 0.0 collective-permute-done.3.down_ref
  12.9 0.6 %x_faces.1 = (bf16[3,8,64,128]{3,2,1,0:T(8,128)(2,1)S(1)}, bf16[3,8,64,128]{3,2,1,0:T(8,128)(2,1)S(1)}, f32[32,4,128]{2,1,0:T(4,128)S(1)}) custom-call(f32[3,8,8,8,128]{4,3,2,1,0:T(8,128)S(1)} %get-tuple-element.37.part_ref, s32[3,8,8,128]{3,2,1,0:T(8,128)S(1)} %get-tuple-element.25.seed_ref, ...), custom_call_target="tpu_custom_call", output_to_operand_aliasing={{0}: (7, {}), {1}: (8, {})} | custom-call | tf_op jit(solution)/shard_map/x_faces/pallas_call | solution.py:521
  13.5 10.3 %all_to_all.5.refs_0_ = f32[32,4,128]{2,1,0:T(4,128)S(1)} all-to-all(f32[32,4,128]{2,1,0:T(4,128)S(1)} %get-tuple-element.42), channel_id=1, replica_groups=mesh['gx'=4,'gy'=8] {'gx','gy'}, dimensions={0} | all-to-all | bytes 131072 | tf_op jit(solution)/shard_map/all_to_all | solution.py:530
  23.8 1.9 %final.1 = (f32[3,8,8,8,128]{4,3,2,1,0:T(8,128)}, f32[8,8]{1,0:T(8,128)}, f32[8,8]{1,0:T(8,128)}) custom-call(f32[32,4,128]{2,1,0:T(4,128)S(1)} %all_to_all.5.refs_0_, bf16[3,8,128,128]{3,2,1,0:T(8,128)(2,1)S(1)} %get-tuple-element.34.high_ref.refs_1_, bf16[3,8,128,128]{3,2,1,0:T(8,128)(2,1)S(1)} %get-tuple-element.35.low_ref.refs_2_, ...), custom_call_target="tpu_custom_call" | custom-call | tf_op jit(solution)/shard_map/final/pallas_call | solution.py:532
Async XLA Ops:
  1.9 9.8 %collective-permute-start = (f32[25,8,128]{2,1,0:T(8,128)S(1)}, f32[25,8,128]{2,1,0:T(8,128)S(1)}, u32[]{:S(2)}, u32[]{:S(2)}) collective-permute-start(f32[25,8,128]{2,1,0:T(8,128)S(1)} %get-tuple-element.31), channel_id=1, source_target_pairs={{0,8},{8,16},{16,24},{24,0},{1,9},{9,17},{17,25},{25,1},{2,10},{10... | collective-permute-start | bytes 307208 | tf_op jit(solution)/shard_map/ppermute | solution.py:440
  4.9 6.9 %collective-permute-start.1 = (f32[25,8,128]{2,1,0:T(8,128)S(1)}, f32[25,8,128]{2,1,0:T(8,128)S(1)}, u32[]{:S(2)}, u32[]{:S(2)}) collective-permute-start(f32[25,8,128]{2,1,0:T(8,128)S(1)} %get-tuple-element.32), channel_id=1, source_target_pairs={{0,7},{1,2},{2,1},{3,4},{4,3},{5,6},{6,5},{7,0},{8,15},{9,10},{10,... | collective-permute-start | bytes 307208 | tf_op jit(solution)/shard_map/ppermute | solution.py:445
  7.6 4.1 %collective-permute-start.2 = (f32[25,8,128]{2,1,0:T(8,128)S(1)}, f32[25,8,128]{2,1,0:T(8,128)S(1)}, u32[]{:S(2)}, u32[]{:S(2)}) collective-permute-start(f32[25,8,128]{2,1,0:T(8,128)S(1)} %get-tuple-element.33), channel_id=1, source_target_pairs={{0,1},{1,0},{2,3},{3,2},{4,5},{5,4},{6,7},{7,6},{8,9},{9,8},{10,11... | collective-permute-start | bytes 307208 | tf_op jit(solution)/shard_map/ppermute | solution.py:445
  7.6 5.3 %collective-permute-start.3 = (f32[24,8,128]{2,1,0:T(8,128)S(1)}, f32[24,8,128]{2,1,0:T(8,128)S(1)}, u32[]{:S(2)}, u32[]{:S(2)}) collective-permute-start(f32[24,8,128]{2,1,0:T(8,128)S(1)} %get-tuple-element.38), channel_id=1, source_target_pairs={{0,24},{8,0},{16,8},{24,16},{1,25},{9,1},{17,9},{25,17},{2,26},{10... | collective-permute-start | bytes 294920 | tf_op jit(solution)/shard_map/ppermute | solution.py:440

commit v7 on v6

--- a/solution.py
+++ b/solution.py
@@ -39,6 +39,11 @@
     return [
         [pick(table_ref, base + a * orbs + b, index) for b in range(orbs)] for a in range(orbs)
     ]
+
+
+def kept_bonds(edge_ref, direction, orbs):
+    base = direction * orbs * orbs
+    return [[edge_ref[base + a * orbs + b] for b in range(orbs)] for a in range(orbs)]
 
 
 def fill_table(table_ref, hop_ref, onsite_ref):
@@ -127,6 +132,7 @@
     low_ref,
     metric_ref,
     table_ref,
+    edge_ref,
     gram_ref,
     prev_ref,
     sem,
@@ -169,6 +175,9 @@
         return carry
 
     lax.fori_loop(0, nx, stencil, 0)
+    for d, index in enumerate((seed_ref[0, nx - 1], seed_ref[1, :, ny - 1, :])):
+        for i, bond in enumerate(sum(bonds_of(table_ref, d, index, orbs), [])):
+            edge_ref[d * orbs * orbs + i] = bond
     load.wait()
     gram_ref[...] = jnp.zeros(gram_ref.shape, F32)
 
@@ -221,19 +230,17 @@
 
 def y_kernel(
     part_in,
-    seed_ref,
+    edge_ref,
     table_ref,
     up_ref,
     far_ref,
     near_ref,
     high_ref,
     low_ref,
-    metric_ref,
     phigh_ref,
     plow_ref,
-    packed_ref,
+    total_ref,
     part_ref,
-    total_ref,
 ):
     orbs, width, nx, ny, nz = part_ref.shape
     side = width * ny
@@ -246,7 +253,7 @@
             part_ref[o, n, 0] += back[o]
 
     def add_faces(low_face, high_face):
-        bond = bonds_of(table_ref, 1, seed_ref[1, :, ny - 1, :], orbs)
+        bond = kept_bonds(edge_ref, 1, orbs)
         bond_low = bonds_of(table_ref, 1, low_face[last].astype(jnp.int32), orbs)
         for n in range(width):
             forward = times(bond, [high_face[o * width + n] for o in range(orbs)])
@@ -270,17 +277,16 @@
                 for group, value in zip(ins, (high_ref[o, x], low_ref[o, x], high, low)):
                     group.append(value)
             total_ref[...] += product_sums(*(jnp.concatenate(group, 1) for group in ins))
-    packed_ref[...] = placed(total_ref[...], metric_ref[...])
 
 
 def x_kernel(
     part_ref,
-    seed_ref,
-    table_ref,
+    edge_ref,
     down_ref,
     high_ref,
     low_ref,
-    packed_ref,
+    total_ref,
+    metric_ref,
     phigh_in,
     plow_in,
     phigh_ref,
@@ -289,13 +295,13 @@
     face_ref,
 ):
     orbs, width, nx, ny, nz = part_ref.shape
-    bond = bonds_of(table_ref, 0, seed_ref[0, nx - 1], orbs)
+    bond = kept_bonds(edge_ref, 0, orbs)
     for n in range(width):
         forward = times(bond, [down_ref[o * width + n] for o in range(orbs)])
         for o in range(orbs):
             face_ref[o, n * ny : (n + 1) * ny, :nz] = part_ref[o, n, 0]
             face_ref[o, n * ny : (n + 1) * ny, nz:] = part_ref[o, n, nx - 1] + forward[o]
-    total = 0.0
+    total = total_ref[...]
     for o in range(orbs):
         high, low = split(face_ref[o])
         for i, x in enumerate((0, nx - 1)):
@@ -305,7 +311,7 @@
             jnp.concatenate([ref[o, 0], ref[o, nx - 1]], 1) for ref in (high_ref, low_ref)
         )
         total = total + product_sums(bhigh, blow, high, low)
-    packed = placed(total, packed_ref[...])
+    packed = placed(total, metric_ref[...])
     half = width // 2
     lanes = iota((half, LANES), 1)
     folded = jnp.where(lanes < LANES // 2, packed[:half], packed[half:])
@@ -356,7 +362,7 @@
     norms = moved(2 * width, width)
     metric = [moved(3 * width, 2 * width), moved(5 * width, 2 * width)]
     alpha_ref[...] = first[1][:, :width]
-    stores = [pltpu.make_async_copy(alpha_ref, alpha_out, sems.at[orbs])]
+    stores = [pltpu.make_async_copy(alpha_ref, alpha_out, sems.at[2 * orbs])]
     stores[-1].start()
     ones = [jnp.where(lanes == rows + i * width, 1.0, 0.0) for i in range(2)]
     lack = [one - value for one, value in zip(ones, metric)]
@@ -399,7 +405,7 @@
     for k in range(width):
         upper = jnp.where((rows == k) & (lanes >= k), lines[k], upper)
     beta_ref[...] = upper[:, :width]
-    stores.append(pltpu.make_async_copy(beta_ref, beta_out, sems.at[orbs + 1]))
+    stores.append(pltpu.make_async_copy(beta_ref, beta_out, sems.at[2 * orbs + 1]))
     stores[-1].start()
 
     same = rows == lanes % ROWS
@@ -429,8 +435,13 @@
     for o in range(orbs):
         for pair in range(nx // 2):
             chunk(o, pair)
-        stores.append(pltpu.make_async_copy(out_ref.at[o], next_ref.at[o], sems.at[o]))
-        stores[-1].start()
+            if pair % 2:
+                spot = pl.ds(2 * pair - 2, 4)
+                place = 2 * o + pair // 2
+                stores.append(
+                    pltpu.make_async_copy(out_ref.at[o, :, spot], next_ref.at[o, :, spot], sems.at[place])
+                )
+                stores[-1].start()
     for store in stores:
         store.wait()
 
@@ -486,7 +497,7 @@
     xdown = shifted(xdown, "gx", -1)
 
     side = width * ny
-    part, high, low, metric, table = pl.pallas_call(
+    part, high, low, metric, table, edges = pl.pallas_call(
         interior_kernel,
         out_shape=[
             pltpu.VMEM(block.shape, F32),
@@ -494,6 +505,7 @@
             pltpu.VMEM((orbs, nx, 2 * side, nz), BF16),
             pltpu.VMEM((width, LANES), F32),
             pltpu.VMEM((table_rows, LANES), F32),
+            pltpu.VMEM((2 * orbs * orbs, ny, nz), F32),
         ],
         in_specs=[outside] + [pl.BlockSpec(memory_space=pltpu.VMEM)] * 5,
         scratch_shapes=[
@@ -507,16 +519,15 @@
     )(stay(prev_block), block_here, seed_here, levels_here, hops_here, onsite_here)
 
     product_halves = [pltpu.VMEM((orbs, nx, side, nz), BF16)] * 2
-    phigh, plow, packed, part = pl.pallas_call(
+    phigh, plow, total, part = pl.pallas_call(
         y_kernel,
         out_shape=product_halves
-        + [pltpu.VMEM((width, LANES), F32), pltpu.VMEM(block.shape, F32)],
+        + [pltpu.VMEM((3 * side, 2 * side), F32), pltpu.VMEM(block.shape, F32)],
         input_output_aliases={0: 3},
-        scratch_shapes=[pltpu.VMEM((3 * side, 2 * side), F32)],
         compiler_params=params,
         cost_estimate=pl.CostEstimate(flops=10**8, bytes_accessed=4 * 10**6, transcendentals=0),
         name="y_faces",
-    )(part, seed_here, table, xup, yfar, ynear, high, low, metric)
+    )(part, edges, table, xup, yfar, ynear, high, low)
 
     phigh, plow, sums = pl.pallas_call(
         x_kernel,
@@ -525,7 +536,7 @@
         scratch_shapes=[pltpu.VMEM((orbs, side, 2 * nz), F32)],
         compiler_params=params,
         name="x_faces",
-    )(part, seed_here, table, xdown, high, low, packed, phigh, plow)
+    )(part, edges, xdown, high, low, total, metric, phigh, plow)
 
     sums = lax.all_to_all(sums, ("gx", "gy"), 0, 0)
 
@@ -541,7 +552,7 @@
             pltpu.VMEM(block.shape, F32),
             pltpu.VMEM((width, width), F32),
             pltpu.VMEM((width, width), F32),
-            pltpu.SemaphoreType.DMA((orbs + 2,)),
+            pltpu.SemaphoreType.DMA((2 * orbs + 2,)),
         ],
         compiler_params=params,
         name="final",

time: 25.9 us -> 25.8 us (level)
  transfers between devices with their start and end apart: 4 -> 4, of which waited for: 0 -> 0; matrix products, arithmetic and copies ran while one was open for 0% -> 0% of each run, Pallas kernels for 15% -> 14%
where the time goes in v7:
time: 25.8 us; the launch traced here: 25.7 us
  blocking collectives  10.4 us (40%)
  Pallas kernels  7.35 us (28%)
  starting transfers between devices  7.19 us (28%)
  between operations  0.69 us (3%)
    all_to_all x1, blocking collectives, per_device(): sums = lax.all_to_all(sums, ('gx', 'gy'), 0, 0)  10.4 us
    ppermute x2, starting transfers between devices, shifted(): lax.ppermute(value, axis, [(i, (i + steps) % count) for i in range(count)])  4.42 us
    ppermute x2, starting transfers between devices, swapped(): lax.ppermute(value, axis, [(i, (i + (1 if i % 2 == far else -1)) % count)...  2.76 us
    pallas_call x1, Pallas kernels, per_device(): pl.pallas_call(interior_kernel, out_shape=[pltpu.VMEM(block.shape, F32),...  2.73 us
    pallas_call x1, Pallas kernels, per_device(): pl.pallas_call(lambda *refs: final_kernel(count, *refs), out_shape=[jax.S...  1.91 us
    pallas_call x1, Pallas kernels, per_device(): pl.pallas_call(pack_kernel, in_specs=[outside] * 5, out_shape=[pltpu.VMEM...  1.24 us
    pallas_call x1, Pallas kernels, per_device(): pl.pallas_call(y_kernel, out_shape=product_halves + [pltpu.VMEM((3 * side...  0.97 us
  transfers between devices with their start and end apart: 4, of which 0 were waited for; matrix products, arithmetic and copies ran while one was open for 0% of the time, Pallas kernels for 14%

profile of v7, /device:TPU:0, one launch (start us, length us, event | category | flops | bytes accessed | tf_op | source)
XLA Modules:
  0.0 25.7 jit_solution(152317269451064661)
XLA Ops:
  0.6 1.2 %pack.1 = (f32[3,8,8,8,128]{4,3,2,1,0:T(8,128)S(1)}, s32[3,8,8,128]{3,2,1,0:T(8,128)S(1)}, s32[8,8,128]{2,1,0:T(8,128)S(1)}, f32[3,3,3,16]{3,2,1,0:T(4,128)S(1)}...) custom-call(f32[3,8,8,8,128]{4,3,2,1,0:T(8,128)} %block_in.1, ...), custom_call_target="tpu_custom_call" | custom-call | tf_op jit(solution)/shard_map/pack/pallas_call | solution.py:476
  1.9 3.0 %collective-permute-start = (f32[25,8,128]{2,1,0:T(8,128)S(1)}, f32[25,8,128]{2,1,0:T(8,128)S(1)}, u32[]{:S(2)}, u32[]{:S(2)}) collective-permute-start(f32[25,8,128]{2,1,0:T(8,128)S(1)} %get-tuple-element.33), channel_id=1, source_target_pairs={{0,8},{8,16},{16,24},{24,0},{1,9},{9,17},{17,25},{25,1},{2,10},{10... | collective-permute-start | bytes 307208 | tf_op jit(solution)/shard_map/ppermute | solution.py:451
  4.9 2.8 %collective-permute-start.1 = (f32[25,8,128]{2,1,0:T(8,128)S(1)}, f32[25,8,128]{2,1,0:T(8,128)S(1)}, u32[]{:S(2)}, u32[]{:S(2)}) collective-permute-start(f32[25,8,128]{2,1,0:T(8,128)S(1)} %get-tuple-element.34), channel_id=1, source_target_pairs={{0,7},{1,2},{2,1},{3,4},{4,3},{5,6},{6,5},{7,0},{8,15},{9,10},{10,... | collective-permute-start | bytes 307208 | tf_op jit(solution)/shard_map/ppermute | solution.py:456
  7.6 0.0 collective-permute-start.2
  7.6 1.4 %collective-permute-start.3 = (f32[24,8,128]{2,1,0:T(8,128)S(1)}, f32[24,8,128]{2,1,0:T(8,128)S(1)}, u32[]{:S(2)}, u32[]{:S(2)}) collective-permute-start(f32[24,8,128]{2,1,0:T(8,128)S(1)} %get-tuple-element.39), channel_id=1, source_target_pairs={{0,24},{8,0},{16,8},{24,16},{1,25},{9,1},{17,9},{25,17},{2,26},{10... | collective-permute-start | bytes 294920 | tf_op jit(solution)/shard_map/ppermute | solution.py:451
  9.1 2.7 %interior.1 = (f32[3,8,8,8,128]{4,3,2,1,0:T(8,128)S(1)}, bf16[3,8,128,128]{3,2,1,0:T(8,128)(2,1)S(1)}, bf16[3,8,128,128]{3,2,1,0:T(8,128)(2,1)S(1)}, f32[8,128]{...) custom-call(f32[3,8,8,8,128]{4,3,2,1,0:T(8,128)} %prev_in.1, ...), custom_call_target="tpu_custom_call" | custom-call | flops 100000000 | bytes 4000000 | tf_op jit(solution)/shard_map/interior/pallas_call | solution.py:500
  11.8 0.0 collective-permute-done.up_ref
  11.8 0.0 collective-permute-done.1.far_ref
  11.8 0.0 collective-permute-done.2.near_ref
  11.8 1.0 %y_faces.1 = (bf16[3,8,64,128]{3,2,1,0:T(8,128)(2,1)S(1)}, bf16[3,8,64,128]{3,2,1,0:T(8,128)(2,1)S(1)}, f32[192,128]{1,0:T(8,128)S(1)}, f32[3,8,8,8,128]{4,3,2,1,0:T(8,128)S(1)}) custom-call(f32[3,8,8,8,128]{4,3,2,1,0:T(8,128)S(1)} %get-tuple-element.30.part_in, f32[18,8,128]{2,1,0:T(8,128)S(1)} %get-tuple-element.31.edge_ref, ...), custom_call_target="tpu_custom_call", output_to_operand_aliasing={{3}: (0, {})} | custom-call | flops 100000000 | bytes 4000000 | tf_op jit(solution)/shard_map/y_faces/pallas_call | solution.py:522
  12.8 0.0 collective-permute-done.3.down_ref
  12.8 0.5 %x_faces.1 = (bf16[3,8,64,128]{3,2,1,0:T(8,128)(2,1)S(1)}, bf16[3,8,64,128]{3,2,1,0:T(8,128)(2,1)S(1)}, f32[32,4,128]{2,1,0:T(4,128)S(1)}) custom-call(f32[3,8,8,8,128]{4,3,2,1,0:T(8,128)S(1)} %get-tuple-element.38.part_ref, f32[18,8,128]{2,1,0:T(8,128)S(1)} %get-tuple-element.31.edge_ref, ...), custom_call_target="tpu_custom_call", output_to_operand_aliasing={{0}: (7, {}), {1}: (8, {})} | custom-call | tf_op jit(solution)/shard_map/x_faces/pallas_call | solution.py:532
  13.4 10.4 %all_to_all.5.refs_0_ = f32[32,4,128]{2,1,0:T(4,128)S(1)} all-to-all(f32[32,4,128]{2,1,0:T(4,128)S(1)} %get-tuple-element.44), channel_id=1, replica_groups=mesh['gx'=4,'gy'=8] {'gx','gy'}, dimensions={0} | all-to-all | bytes 131072 | tf_op jit(solution)/shard_map/all_to_all | solution.py:541
  23.7 1.9 %final.1 = (f32[3,8,8,8,128]{4,3,2,1,0:T(8,128)}, f32[8,8]{1,0:T(8,128)}, f32[8,8]{1,0:T(8,128)}) custom-call(f32[32,4,128]{2,1,0:T(4,128)S(1)} %all_to_all.5.refs_0_, bf16[3,8,128,128]{3,2,1,0:T(8,128)(2,1)S(1)} %get-tuple-element.36.high_ref.refs_1_, bf16[3,8,128,128]{3,2,1,0:T(8,128)(2,1)S(1)} %get-tuple-element.37.low_ref.refs_2_, ...), custom_call_target="tpu_custom_call" | custom-call | tf_op jit(solution)/shard_map/final/pallas_call | solution.py:543
Async XLA Ops:
  1.9 9.9 %collective-permute-start = (f32[25,8,128]{2,1,0:T(8,128)S(1)}, f32[25,8,128]{2,1,0:T(8,128)S(1)}, u32[]{:S(2)}, u32[]{:S(2)}) collective-permute-start(f32[25,8,128]{2,1,0:T(8,128)S(1)} %get-tuple-element.33), channel_id=1, source_target_pairs={{0,8},{8,16},{16,24},{24,0},{1,9},{9,17},{17,25},{25,1},{2,10},{10... | collective-permute-start | bytes 307208 | tf_op jit(solution)/shard_map/ppermute | solution.py:451
  4.9 7.0 %collective-permute-start.1 = (f32[25,8,128]{2,1,0:T(8,128)S(1)}, f32[25,8,128]{2,1,0:T(8,128)S(1)}, u32[]{:S(2)}, u32[]{:S(2)}) collective-permute-start(f32[25,8,128]{2,1,0:T(8,128)S(1)} %get-tuple-element.34), channel_id=1, source_target_pairs={{0,7},{1,2},{2,1},{3,4},{4,3},{5,6},{6,5},{7,0},{8,15},{9,10},{10,... | collective-permute-start | bytes 307208 | tf_op jit(solution)/shard_map/ppermute | solution.py:456
  7.6 4.2 %collective-permute-start.2 = (f32[25,8,128]{2,1,0:T(8,128)S(1)}, f32[25,8,128]{2,1,0:T(8,128)S(1)}, u32[]{:S(2)}, u32[]{:S(2)}) collective-permute-start(f32[25,8,128]{2,1,0:T(8,128)S(1)} %get-tuple-element.35), channel_id=1, source_target_pairs={{0,1},{1,0},{2,3},{3,2},{4,5},{5,4},{6,7},{7,6},{8,9},{9,8},{10,11... | collective-permute-start | bytes 307208 | tf_op jit(solution)/shard_map/ppermute | solution.py:456
  7.6 5.2 %collective-permute-start.3 = (f32[24,8,128]{2,1,0:T(8,128)S(1)}, f32[24,8,128]{2,1,0:T(8,128)S(1)}, u32[]{:S(2)}, u32[]{:S(2)}) collective-permute-start(f32[24,8,128]{2,1,0:T(8,128)S(1)} %get-tuple-element.39), channel_id=1, source_target_pairs={{0,24},{8,0},{16,8},{24,16},{1,25},{9,1},{17,9},{25,17},{2,26},{10... | collective-permute-start | bytes 294920 | tf_op jit(solution)/shard_map/ppermute | solution.py:451

commit v8 on v7

--- a/solution.py
+++ b/solution.py
@@ -174,7 +174,7 @@
                 part_ref[o, n, x] = image[o]
         return carry
 
-    lax.fori_loop(0, nx, stencil, 0)
+    lax.fori_loop(0, nx, stencil, 0, unroll=2)
     for d, index in enumerate((seed_ref[0, nx - 1], seed_ref[1, :, ny - 1, :])):
         for i, bond in enumerate(sum(bonds_of(table_ref, d, index, orbs), [])):
             edge_ref[d * orbs * orbs + i] = bond
@@ -345,6 +345,7 @@
     out_ref,
     alpha_ref,
     beta_ref,
+    row_ref,
     sems,
 ):
     orbs, nx, side, nz = phigh_ref.shape
@@ -368,8 +369,18 @@
     lack = [one - value for one, value in zip(ones, metric)]
     lack_columns = [[column(value, k) for k in range(2 * width)] for value in lack]
 
+    slots = iter(range(row_ref.shape[0]))
+
+    def lines_of(values):
+        lines = []
+        for value in values:
+            slot = next(slots)
+            row_ref[slot] = value
+            lines += [jnp.broadcast_to(row_ref[slot, k : k + 1, :], shape) for k in range(width)]
+        return lines
+
     def lacking(pair):
-        lines = [line(value, k) for value in pair for k in range(width)]
+        lines = lines_of(pair)
         return [added([a * b for a, b in zip(columns, lines)]) for columns in lack_columns]
 
     one = lacking(first)
@@ -380,19 +391,19 @@
     turned_columns = [
         jnp.broadcast_to(turned[:, k : k + 1], shape) for k in range(2 * width)
     ]
-    weighed_lines = [line(value, k) for value in weighed for k in range(width)]
+    weighed_lines = lines_of(weighed)
     gram = norms - added([a * b for a, b in zip(turned_columns, weighed_lines)])
     twice = [a + b for a, b in zip(ones, lack)]
-    twice_lines = [line(value, k) for value in twice for k in range(width)]
+    twice_lines = lines_of(twice)
     coeffs = added([a * b for a, b in zip(turned_columns, twice_lines)])
     table = gram + jnp.where(lanes == rows + width, 1.0, 0.0) - pltpu.roll(coeffs, 2 * width, 1)
 
     entry = {}
     for k in range(width):
-        spread = column(gram, k)
+        spread = lines_of([column(gram, k)])
         for j in range(k, width):
-            entry[j, k] = line(spread, j)
-    lines = [line(table, k) for k in range(width)]
+            entry[j, k] = spread[j]
+    lines = lines_of([table])
     for k in range(width):
         inverse = 1.0 / entry[k, k]
         for j in range(k + 1, width):
@@ -552,6 +563,7 @@
             pltpu.VMEM(block.shape, F32),
             pltpu.VMEM((width, width), F32),
             pltpu.VMEM((width, width), F32),
+            pltpu.VMEM((2 * width + 4, width, LANES), F32),
             pltpu.SemaphoreType.DMA((2 * orbs + 2,)),
         ],
         compiler_params=params,

time: 25.8 us -> 25.8 us (level)
  transfers between devices with their start and end apart: 4 -> 4, of which waited for: 0 -> 1; matrix products, arithmetic and copies ran while one was open for 0% -> 0% of each run, Pallas kernels for 14% -> 14%
where the time goes in v8:
time: 25.8 us; the launch traced here: 25.6 us
  blocking collectives  10.4 us (40%)
  starting transfers between devices  7.19 us (28%)
  Pallas kernels  7.13 us (28%)
  between operations  0.69 us (3%)
    all_to_all x1, blocking collectives, per_device(): sums = lax.all_to_all(sums, ('gx', 'gy'), 0, 0)  10.4 us
    ppermute x2, starting transfers between devices, shifted(): lax.ppermute(value, axis, [(i, (i + steps) % count) for i in range(count)])  4.42 us
    ppermute x2, starting transfers between devices, swapped(): lax.ppermute(value, axis, [(i, (i + (1 if i % 2 == far else -1)) % count)...  2.76 us
    pallas_call x1, Pallas kernels, per_device(): pl.pallas_call(interior_kernel, out_shape=[pltpu.VMEM(block.shape, F32),...  2.53 us
    pallas_call x1, Pallas kernels, per_device(): pl.pallas_call(lambda *refs: final_kernel(count, *refs), out_shape=[jax.S...  1.89 us
    pallas_call x1, Pallas kernels, per_device(): pl.pallas_call(pack_kernel, in_specs=[outside] * 5, out_shape=[pltpu.VMEM...  1.24 us
    pallas_call x1, Pallas kernels, per_device(): pl.pallas_call(y_kernel, out_shape=product_halves + [pltpu.VMEM((3 * side...  0.97 us
  transfers between devices with their start and end apart: 4, of which 1 were waited for; matrix products, arithmetic and copies ran while one was open for 0% of the time, Pallas kernels for 14%

profile of v8, /device:TPU:0, one launch (start us, length us, event | category | flops | bytes accessed | tf_op | source)
XLA Modules:
  0.0 25.6 jit_solution(9881658271413280675)
XLA Ops:
  0.6 1.2 %pack.1 = (f32[3,8,8,8,128]{4,3,2,1,0:T(8,128)S(1)}, s32[3,8,8,128]{3,2,1,0:T(8,128)S(1)}, s32[8,8,128]{2,1,0:T(8,128)S(1)}, f32[3,3,3,16]{3,2,1,0:T(4,128)S(1)}...) custom-call(f32[3,8,8,8,128]{4,3,2,1,0:T(8,128)} %block_in.1, ...), custom_call_target="tpu_custom_call" | custom-call | tf_op jit(solution)/shard_map/pack/pallas_call | solution.py:487
  1.9 3.0 %collective-permute-start = (f32[25,8,128]{2,1,0:T(8,128)S(1)}, f32[25,8,128]{2,1,0:T(8,128)S(1)}, u32[]{:S(2)}, u32[]{:S(2)}) collective-permute-start(f32[25,8,128]{2,1,0:T(8,128)S(1)} %get-tuple-element.33), channel_id=1, source_target_pairs={{0,8},{8,16},{16,24},{24,0},{1,9},{9,17},{17,25},{25,1},{2,10},{10... | collective-permute-start | bytes 307208 | tf_op jit(solution)/shard_map/ppermute | solution.py:462
  4.9 2.8 %collective-permute-start.1 = (f32[25,8,128]{2,1,0:T(8,128)S(1)}, f32[25,8,128]{2,1,0:T(8,128)S(1)}, u32[]{:S(2)}, u32[]{:S(2)}) collective-permute-start(f32[25,8,128]{2,1,0:T(8,128)S(1)} %get-tuple-element.34), channel_id=1, source_target_pairs={{0,7},{1,2},{2,1},{3,4},{4,3},{5,6},{6,5},{7,0},{8,15},{9,10},{10,... | collective-permute-start | bytes 307208 | tf_op jit(solution)/shard_map/ppermute | solution.py:467
  7.6 0.0 collective-permute-start.2
  7.6 1.4 %collective-permute-start.3 = (f32[24,8,128]{2,1,0:T(8,128)S(1)}, f32[24,8,128]{2,1,0:T(8,128)S(1)}, u32[]{:S(2)}, u32[]{:S(2)}) collective-permute-start(f32[24,8,128]{2,1,0:T(8,128)S(1)} %get-tuple-element.39), channel_id=1, source_target_pairs={{0,24},{8,0},{16,8},{24,16},{1,25},{9,1},{17,9},{25,17},{2,26},{10... | collective-permute-start | bytes 294920 | tf_op jit(solution)/shard_map/ppermute | solution.py:462
  9.1 2.5 %interior.1 = (f32[3,8,8,8,128]{4,3,2,1,0:T(8,128)S(1)}, bf16[3,8,128,128]{3,2,1,0:T(8,128)(2,1)S(1)}, bf16[3,8,128,128]{3,2,1,0:T(8,128)(2,1)S(1)}, f32[8,128]{...) custom-call(f32[3,8,8,8,128]{4,3,2,1,0:T(8,128)} %prev_in.1, ...), custom_call_target="tpu_custom_call" | custom-call | flops 100000000 | bytes 4000000 | tf_op jit(solution)/shard_map/interior/pallas_call | solution.py:511
  11.6 0.0 collective-permute-done.up_ref
  11.6 0.0 collective-permute-done.1.far_ref
  11.6 0.0 collective-permute-done.2.near_ref
  11.6 1.0 %y_faces.1 = (bf16[3,8,64,128]{3,2,1,0:T(8,128)(2,1)S(1)}, bf16[3,8,64,128]{3,2,1,0:T(8,128)(2,1)S(1)}, f32[192,128]{1,0:T(8,128)S(1)}, f32[3,8,8,8,128]{4,3,2,1,0:T(8,128)S(1)}) custom-call(f32[3,8,8,8,128]{4,3,2,1,0:T(8,128)S(1)} %get-tuple-element.30.part_in, f32[18,8,128]{2,1,0:T(8,128)S(1)} %get-tuple-element.31.edge_ref, ...), custom_call_target="tpu_custom_call", output_to_operand_aliasing={{3}: (0, {})} | custom-call | flops 100000000 | bytes 4000000 | tf_op jit(solution)/shard_map/y_faces/pallas_call | solution.py:533
  12.6 0.2 collective-permute-done.3.down_ref
  12.8 0.5 %x_faces.1 = (bf16[3,8,64,128]{3,2,1,0:T(8,128)(2,1)S(1)}, bf16[3,8,64,128]{3,2,1,0:T(8,128)(2,1)S(1)}, f32[32,4,128]{2,1,0:T(4,128)S(1)}) custom-call(f32[3,8,8,8,128]{4,3,2,1,0:T(8,128)S(1)} %get-tuple-element.38.part_ref, f32[18,8,128]{2,1,0:T(8,128)S(1)} %get-tuple-element.31.edge_ref, ...), custom_call_target="tpu_custom_call", output_to_operand_aliasing={{0}: (7, {}), {1}: (8, {})} | custom-call | tf_op jit(solution)/shard_map/x_faces/pallas_call | solution.py:543
  13.4 10.4 %all_to_all.5.refs_0_ = f32[32,4,128]{2,1,0:T(4,128)S(1)} all-to-all(f32[32,4,128]{2,1,0:T(4,128)S(1)} %get-tuple-element.44), channel_id=1, replica_groups=mesh['gx'=4,'gy'=8] {'gx','gy'}, dimensions={0} | all-to-all | bytes 131072 | tf_op jit(solution)/shard_map/all_to_all | solution.py:552
  23.7 1.9 %final.1 = (f32[3,8,8,8,128]{4,3,2,1,0:T(8,128)}, f32[8,8]{1,0:T(8,128)}, f32[8,8]{1,0:T(8,128)}) custom-call(f32[32,4,128]{2,1,0:T(4,128)S(1)} %all_to_all.5.refs_0_, bf16[3,8,128,128]{3,2,1,0:T(8,128)(2,1)S(1)} %get-tuple-element.36.high_ref.refs_1_, bf16[3,8,128,128]{3,2,1,0:T(8,128)(2,1)S(1)} %get-tuple-element.37.low_ref.refs_2_, ...), custom_call_target="tpu_custom_call" | custom-call | tf_op jit(solution)/shard_map/final/pallas_call | solution.py:554
Async XLA Ops:
  1.9 9.7 %collective-permute-start = (f32[25,8,128]{2,1,0:T(8,128)S(1)}, f32[25,8,128]{2,1,0:T(8,128)S(1)}, u32[]{:S(2)}, u32[]{:S(2)}) collective-permute-start(f32[25,8,128]{2,1,0:T(8,128)S(1)} %get-tuple-element.33), channel_id=1, source_target_pairs={{0,8},{8,16},{16,24},{24,0},{1,9},{9,17},{17,25},{25,1},{2,10},{10... | collective-permute-start | bytes 307208 | tf_op jit(solution)/shard_map/ppermute | solution.py:462
  4.9 6.8 %collective-permute-start.1 = (f32[25,8,128]{2,1,0:T(8,128)S(1)}, f32[25,8,128]{2,1,0:T(8,128)S(1)}, u32[]{:S(2)}, u32[]{:S(2)}) collective-permute-start(f32[25,8,128]{2,1,0:T(8,128)S(1)} %get-tuple-element.34), channel_id=1, source_target_pairs={{0,7},{1,2},{2,1},{3,4},{4,3},{5,6},{6,5},{7,0},{8,15},{9,10},{10,... | collective-permute-start | bytes 307208 | tf_op jit(solution)/shard_map/ppermute | solution.py:467
  7.6 4.0 %collective-permute-start.2 = (f32[25,8,128]{2,1,0:T(8,128)S(1)}, f32[25,8,128]{2,1,0:T(8,128)S(1)}, u32[]{:S(2)}, u32[]{:S(2)}) collective-permute-start(f32[25,8,128]{2,1,0:T(8,128)S(1)} %get-tuple-element.35), channel_id=1, source_target_pairs={{0,1},{1,0},{2,3},{3,2},{4,5},{5,4},{6,7},{7,6},{8,9},{9,8},{10,11... | collective-permute-start | bytes 307208 | tf_op jit(solution)/shard_map/ppermute | solution.py:467
  7.6 5.2 %collective-permute-start.3 = (f32[24,8,128]{2,1,0:T(8,128)S(1)}, f32[24,8,128]{2,1,0:T(8,128)S(1)}, u32[]{:S(2)}, u32[]{:S(2)}) collective-permute-start(f32[24,8,128]{2,1,0:T(8,128)S(1)} %get-tuple-element.39), channel_id=1, source_target_pairs={{0,24},{8,0},{16,8},{24,16},{1,25},{9,1},{17,9},{25,17},{2,26},{10... | collective-permute-start | bytes 294920 | tf_op jit(solution)/shard_map/ppermute | solution.py:462

commit v9 on v8

--- a/solution.py
+++ b/solution.py
@@ -174,7 +174,7 @@
                 part_ref[o, n, x] = image[o]
         return carry
 
-    lax.fori_loop(0, nx, stencil, 0, unroll=2)
+    lax.fori_loop(0, nx, stencil, 0)
     for d, index in enumerate((seed_ref[0, nx - 1], seed_ref[1, :, ny - 1, :])):
         for i, bond in enumerate(sum(bonds_of(table_ref, d, index, orbs), [])):
             edge_ref[d * orbs * orbs + i] = bond

time: 25.8 us -> 25.8 us (level)
  transfers between devices with their start and end apart: 4 -> 4, of which waited for: 1 -> 0; matrix products, arithmetic and copies ran while one was open for 0% -> 0% of each run, Pallas kernels for 14% -> 14%
where the time goes in v9:
time: 25.8 us; the launch traced here: 25.6 us
  blocking collectives  10.4 us (40%)
  Pallas kernels  7.33 us (28%)
  starting transfers between devices  7.19 us (28%)
  between operations  0.69 us (3%)
    all_to_all x1, blocking collectives, per_device(): sums = lax.all_to_all(sums, ('gx', 'gy'), 0, 0)  10.4 us
    ppermute x2, starting transfers between devices, shifted(): lax.ppermute(value, axis, [(i, (i + steps) % count) for i in range(count)])  4.42 us
    ppermute x2, starting transfers between devices, swapped(): lax.ppermute(value, axis, [(i, (i + (1 if i % 2 == far else -1)) % count)...  2.76 us
    pallas_call x1, Pallas kernels, per_device(): pl.pallas_call(interior_kernel, out_shape=[pltpu.VMEM(block.shape, F32),...  2.73 us
    pallas_call x1, Pallas kernels, per_device(): pl.pallas_call(lambda *refs: final_kernel(count, *refs), out_shape=[jax.S...  1.89 us
    pallas_call x1, Pallas kernels, per_device(): pl.pallas_call(pack_kernel, in_specs=[outside] * 5, out_shape=[pltpu.VMEM...  1.24 us
    pallas_call x1, Pallas kernels, per_device(): pl.pallas_call(y_kernel, out_shape=product_halves + [pltpu.VMEM((3 * side...  0.97 us
  transfers between devices with their start and end apart: 4, of which 0 were waited for; matrix products, arithmetic and copies ran while one was open for 0% of the time, Pallas kernels for 14%

profile of v9, /device:TPU:0, one launch (start us, length us, event | category | flops | bytes accessed | tf_op | source)
XLA Modules:
  0.0 25.6 jit_solution(2217067014112184471)
XLA Ops:
  0.6 1.2 %pack.1 = (f32[3,8,8,8,128]{4,3,2,1,0:T(8,128)S(1)}, s32[3,8,8,128]{3,2,1,0:T(8,128)S(1)}, s32[8,8,128]{2,1,0:T(8,128)S(1)}, f32[3,3,3,16]{3,2,1,0:T(4,128)S(1)}...) custom-call(f32[3,8,8,8,128]{4,3,2,1,0:T(8,128)} %block_in.1, ...), custom_call_target="tpu_custom_call" | custom-call | tf_op jit(solution)/shard_map/pack/pallas_call | solution.py:487
  1.9 3.0 %collective-permute-start = (f32[25,8,128]{2,1,0:T(8,128)S(1)}, f32[25,8,128]{2,1,0:T(8,128)S(1)}, u32[]{:S(2)}, u32[]{:S(2)}) collective-permute-start(f32[25,8,128]{2,1,0:T(8,128)S(1)} %get-tuple-element.33), channel_id=1, source_target_pairs={{0,8},{8,16},{16,24},{24,0},{1,9},{9,17},{17,25},{25,1},{2,10},{10... | collective-permute-start | bytes 307208 | tf_op jit(solution)/shard_map/ppermute | solution.py:462
  4.9 2.8 %collective-permute-start.1 = (f32[25,8,128]{2,1,0:T(8,128)S(1)}, f32[25,8,128]{2,1,0:T(8,128)S(1)}, u32[]{:S(2)}, u32[]{:S(2)}) collective-permute-start(f32[25,8,128]{2,1,0:T(8,128)S(1)} %get-tuple-element.34), channel_id=1, source_target_pairs={{0,7},{1,2},{2,1},{3,4},{4,3},{5,6},{6,5},{7,0},{8,15},{9,10},{10,... | collective-permute-start | bytes 307208 | tf_op jit(solution)/shard_map/ppermute | solution.py:467
  7.6 0.0 collective-permute-start.2
  7.6 1.4 %collective-permute-start.3 = (f32[24,8,128]{2,1,0:T(8,128)S(1)}, f32[24,8,128]{2,1,0:T(8,128)S(1)}, u32[]{:S(2)}, u32[]{:S(2)}) collective-permute-start(f32[24,8,128]{2,1,0:T(8,128)S(1)} %get-tuple-element.39), channel_id=1, source_target_pairs={{0,24},{8,0},{16,8},{24,16},{1,25},{9,1},{17,9},{25,17},{2,26},{10... | collective-permute-start | bytes 294920 | tf_op jit(solution)/shard_map/ppermute | solution.py:462
  9.1 2.7 %interior.1 = (f32[3,8,8,8,128]{4,3,2,1,0:T(8,128)S(1)}, bf16[3,8,128,128]{3,2,1,0:T(8,128)(2,1)S(1)}, bf16[3,8,128,128]{3,2,1,0:T(8,128)(2,1)S(1)}, f32[8,128]{...) custom-call(f32[3,8,8,8,128]{4,3,2,1,0:T(8,128)} %prev_in.1, ...), custom_call_target="tpu_custom_call" | custom-call | flops 100000000 | bytes 4000000 | tf_op jit(solution)/shard_map/interior/pallas_call | solution.py:511
  11.8 0.0 collective-permute-done.up_ref
  11.8 0.0 collective-permute-done.1.far_ref
  11.8 0.0 collective-permute-done.2.near_ref
  11.8 1.0 %y_faces.1 = (bf16[3,8,64,128]{3,2,1,0:T(8,128)(2,1)S(1)}, bf16[3,8,64,128]{3,2,1,0:T(8,128)(2,1)S(1)}, f32[192,128]{1,0:T(8,128)S(1)}, f32[3,8,8,8,128]{4,3,2,1,0:T(8,128)S(1)}) custom-call(f32[3,8,8,8,128]{4,3,2,1,0:T(8,128)S(1)} %get-tuple-element.30.part_in, f32[18,8,128]{2,1,0:T(8,128)S(1)} %get-tuple-element.31.edge_ref, ...), custom_call_target="tpu_custom_call", output_to_operand_aliasing={{3}: (0, {})} | custom-call | flops 100000000 | bytes 4000000 | tf_op jit(solution)/shard_map/y_faces/pallas_call | solution.py:533
  12.8 0.0 collective-permute-done.3.down_ref
  12.8 0.5 %x_faces.1 = (bf16[3,8,64,128]{3,2,1,0:T(8,128)(2,1)S(1)}, bf16[3,8,64,128]{3,2,1,0:T(8,128)(2,1)S(1)}, f32[32,4,128]{2,1,0:T(4,128)S(1)}) custom-call(f32[3,8,8,8,128]{4,3,2,1,0:T(8,128)S(1)} %get-tuple-element.38.part_ref, f32[18,8,128]{2,1,0:T(8,128)S(1)} %get-tuple-element.31.edge_ref, ...), custom_call_target="tpu_custom_call", output_to_operand_aliasing={{0}: (7, {}), {1}: (8, {})} | custom-call | tf_op jit(solution)/shard_map/x_faces/pallas_call | solution.py:543
  13.4 10.4 %all_to_all.5.refs_0_ = f32[32,4,128]{2,1,0:T(4,128)S(1)} all-to-all(f32[32,4,128]{2,1,0:T(4,128)S(1)} %get-tuple-element.44), channel_id=1, replica_groups=mesh['gx'=4,'gy'=8] {'gx','gy'}, dimensions={0} | all-to-all | bytes 131072 | tf_op jit(solution)/shard_map/all_to_all | solution.py:552
  23.7 1.9 %final.1 = (f32[3,8,8,8,128]{4,3,2,1,0:T(8,128)}, f32[8,8]{1,0:T(8,128)}, f32[8,8]{1,0:T(8,128)}) custom-call(f32[32,4,128]{2,1,0:T(4,128)S(1)} %all_to_all.5.refs_0_, bf16[3,8,128,128]{3,2,1,0:T(8,128)(2,1)S(1)} %get-tuple-element.36.high_ref.refs_1_, bf16[3,8,128,128]{3,2,1,0:T(8,128)(2,1)S(1)} %get-tuple-element.37.low_ref.refs_2_, ...), custom_call_target="tpu_custom_call" | custom-call | tf_op jit(solution)/shard_map/final/pallas_call | solution.py:554
Async XLA Ops:
  1.9 9.9 %collective-permute-start = (f32[25,8,128]{2,1,0:T(8,128)S(1)}, f32[25,8,128]{2,1,0:T(8,128)S(1)}, u32[]{:S(2)}, u32[]{:S(2)}) collective-permute-start(f32[25,8,128]{2,1,0:T(8,128)S(1)} %get-tuple-element.33), channel_id=1, source_target_pairs={{0,8},{8,16},{16,24},{24,0},{1,9},{9,17},{17,25},{25,1},{2,10},{10... | collective-permute-start | bytes 307208 | tf_op jit(solution)/shard_map/ppermute | solution.py:462
  4.9 7.0 %collective-permute-start.1 = (f32[25,8,128]{2,1,0:T(8,128)S(1)}, f32[25,8,128]{2,1,0:T(8,128)S(1)}, u32[]{:S(2)}, u32[]{:S(2)}) collective-permute-start(f32[25,8,128]{2,1,0:T(8,128)S(1)} %get-tuple-element.34), channel_id=1, source_target_pairs={{0,7},{1,2},{2,1},{3,4},{4,3},{5,6},{6,5},{7,0},{8,15},{9,10},{10,... | collective-permute-start | bytes 307208 | tf_op jit(solution)/shard_map/ppermute | solution.py:467
  7.6 4.2 %collective-permute-start.2 = (f32[25,8,128]{2,1,0:T(8,128)S(1)}, f32[25,8,128]{2,1,0:T(8,128)S(1)}, u32[]{:S(2)}, u32[]{:S(2)}) collective-permute-start(f32[25,8,128]{2,1,0:T(8,128)S(1)} %get-tuple-element.35), channel_id=1, source_target_pairs={{0,1},{1,0},{2,3},{3,2},{4,5},{5,4},{6,7},{7,6},{8,9},{9,8},{10,11... | collective-permute-start | bytes 307208 | tf_op jit(solution)/shard_map/ppermute | solution.py:467
  7.6 5.2 %collective-permute-start.3 = (f32[24,8,128]{2,1,0:T(8,128)S(1)}, f32[24,8,128]{2,1,0:T(8,128)S(1)}, u32[]{:S(2)}, u32[]{:S(2)}) collective-permute-start(f32[24,8,128]{2,1,0:T(8,128)S(1)} %get-tuple-element.39), channel_id=1, source_target_pairs={{0,24},{8,0},{16,8},{24,16},{1,25},{9,1},{17,9},{25,17},{2,26},{10... | collective-permute-start | bytes 294920 | tf_op jit(solution)/shard_map/ppermute | solution.py:462

commit v10 on v7

--- a/solution.py
+++ b/solution.py
@@ -86,7 +86,7 @@
     pairs = [(block_in.at[o], block_ref.at[o]) for o in range(orbs)]
     pairs += [(seed_in, seed_ref), (level_in, level_ref), (hop_in, hop_ref), (onsite_in, onsite_ref)]
     loads = [pltpu.make_async_copy(*pair, sems.at[i]) for i, pair in enumerate(pairs)]
-    for load in loads:
+    for load in loads[orbs:] + loads[:orbs]:
         load.start()
     for o in range(orbs):
         loads[o].wait()

time: 25.8 us -> 25.9 us (level)
  no operation moved by 1% of the time
where the time goes in v10:
time: 25.9 us; the launch traced here: 25.8 us
  blocking collectives  10.4 us (40%)
  Pallas kernels  7.45 us (29%)
  starting transfers between devices  7.19 us (28%)
  between operations  0.69 us (3%)
    all_to_all x1, blocking collectives, per_device(): sums = lax.all_to_all(sums, ('gx', 'gy'), 0, 0)  10.4 us
    ppermute x2, starting transfers between devices, shifted(): lax.ppermute(value, axis, [(i, (i + steps) % count) for i in range(count)])  4.42 us
    ppermute x2, starting transfers between devices, swapped(): lax.ppermute(value, axis, [(i, (i + (1 if i % 2 == far else -1)) % count)...  2.76 us
    pallas_call x1, Pallas kernels, per_device(): pl.pallas_call(interior_kernel, out_shape=[pltpu.VMEM(block.shape, F32),...  2.73 us
    pallas_call x1, Pallas kernels, per_device(): pl.pallas_call(lambda *refs: final_kernel(count, *refs), out_shape=[jax.S...  1.9 us
    pallas_call x1, Pallas kernels, per_device(): pl.pallas_call(pack_kernel, in_specs=[outside] * 5, out_shape=[pltpu.VMEM...  1.34 us
    pallas_call x1, Pallas kernels, per_device(): pl.pallas_call(y_kernel, out_shape=product_halves + [pltpu.VMEM((3 * side...  0.97 us
  transfers between devices with their start and end apart: 4, of which 0 were waited for; matrix products, arithmetic and copies ran while one was open for 0% of the time, Pallas kernels for 14%

profile of v10, /device:TPU:0, one launch (start us, length us, event | category | flops | bytes accessed | tf_op | source)
XLA Modules:
  0.0 25.8 jit_solution(11042582245971968931)
XLA Ops:
  0.6 1.3 %pack.1 = (f32[3,8,8,8,128]{4,3,2,1,0:T(8,128)S(1)}, s32[3,8,8,128]{3,2,1,0:T(8,128)S(1)}, s32[8,8,128]{2,1,0:T(8,128)S(1)}, f32[3,3,3,16]{3,2,1,0:T(4,128)S(1)}...) custom-call(f32[3,8,8,8,128]{4,3,2,1,0:T(8,128)} %block_in.1, ...), custom_call_target="tpu_custom_call" | custom-call | tf_op jit(solution)/shard_map/pack/pallas_call | solution.py:476
  2.0 3.0 %collective-permute-start = (f32[25,8,128]{2,1,0:T(8,128)S(1)}, f32[25,8,128]{2,1,0:T(8,128)S(1)}, u32[]{:S(2)}, u32[]{:S(2)}) collective-permute-start(f32[25,8,128]{2,1,0:T(8,128)S(1)} %get-tuple-element.33), channel_id=1, source_target_pairs={{0,8},{8,16},{16,24},{24,0},{1,9},{9,17},{17,25},{25,1},{2,10},{10... | collective-permute-start | bytes 307208 | tf_op jit(solution)/shard_map/ppermute | solution.py:451
  5.0 2.8 %collective-permute-start.1 = (f32[25,8,128]{2,1,0:T(8,128)S(1)}, f32[25,8,128]{2,1,0:T(8,128)S(1)}, u32[]{:S(2)}, u32[]{:S(2)}) collective-permute-start(f32[25,8,128]{2,1,0:T(8,128)S(1)} %get-tuple-element.34), channel_id=1, source_target_pairs={{0,7},{1,2},{2,1},{3,4},{4,3},{5,6},{6,5},{7,0},{8,15},{9,10},{10,... | collective-permute-start | bytes 307208 | tf_op jit(solution)/shard_map/ppermute | solution.py:456
  7.7 0.0 collective-permute-start.2
  7.7 1.4 %collective-permute-start.3 = (f32[24,8,128]{2,1,0:T(8,128)S(1)}, f32[24,8,128]{2,1,0:T(8,128)S(1)}, u32[]{:S(2)}, u32[]{:S(2)}) collective-permute-start(f32[24,8,128]{2,1,0:T(8,128)S(1)} %get-tuple-element.39), channel_id=1, source_target_pairs={{0,24},{8,0},{16,8},{24,16},{1,25},{9,1},{17,9},{25,17},{2,26},{10... | collective-permute-start | bytes 294920 | tf_op jit(solution)/shard_map/ppermute | solution.py:451
  9.2 2.7 %interior.1 = (f32[3,8,8,8,128]{4,3,2,1,0:T(8,128)S(1)}, bf16[3,8,128,128]{3,2,1,0:T(8,128)(2,1)S(1)}, bf16[3,8,128,128]{3,2,1,0:T(8,128)(2,1)S(1)}, f32[8,128]{...) custom-call(f32[3,8,8,8,128]{4,3,2,1,0:T(8,128)} %prev_in.1, ...), custom_call_target="tpu_custom_call" | custom-call | flops 100000000 | bytes 4000000 | tf_op jit(solution)/shard_map/interior/pallas_call | solution.py:500
  11.9 0.0 collective-permute-done.up_ref
  11.9 0.0 collective-permute-done.1.far_ref
  11.9 0.0 collective-permute-done.2.near_ref
  11.9 1.0 %y_faces.1 = (bf16[3,8,64,128]{3,2,1,0:T(8,128)(2,1)S(1)}, bf16[3,8,64,128]{3,2,1,0:T(8,128)(2,1)S(1)}, f32[192,128]{1,0:T(8,128)S(1)}, f32[3,8,8,8,128]{4,3,2,1,0:T(8,128)S(1)}) custom-call(f32[3,8,8,8,128]{4,3,2,1,0:T(8,128)S(1)} %get-tuple-element.30.part_in, f32[18,8,128]{2,1,0:T(8,128)S(1)} %get-tuple-element.31.edge_ref, ...), custom_call_target="tpu_custom_call", output_to_operand_aliasing={{3}: (0, {})} | custom-call | flops 100000000 | bytes 4000000 | tf_op jit(solution)/shard_map/y_faces/pallas_call | solution.py:522
  12.9 0.0 collective-permute-done.3.down_ref
  12.9 0.5 %x_faces.1 = (bf16[3,8,64,128]{3,2,1,0:T(8,128)(2,1)S(1)}, bf16[3,8,64,128]{3,2,1,0:T(8,128)(2,1)S(1)}, f32[32,4,128]{2,1,0:T(4,128)S(1)}) custom-call(f32[3,8,8,8,128]{4,3,2,1,0:T(8,128)S(1)} %get-tuple-element.38.part_ref, f32[18,8,128]{2,1,0:T(8,128)S(1)} %get-tuple-element.31.edge_ref, ...), custom_call_target="tpu_custom_call", output_to_operand_aliasing={{0}: (7, {}), {1}: (8, {})} | custom-call | tf_op jit(solution)/shard_map/x_faces/pallas_call | solution.py:532
  13.5 10.4 %all_to_all.5.refs_0_ = f32[32,4,128]{2,1,0:T(4,128)S(1)} all-to-all(f32[32,4,128]{2,1,0:T(4,128)S(1)} %get-tuple-element.44), channel_id=1, replica_groups=mesh['gx'=4,'gy'=8] {'gx','gy'}, dimensions={0} | all-to-all | bytes 131072 | tf_op jit(solution)/shard_map/all_to_all | solution.py:541
  23.9 1.9 %final.1 = (f32[3,8,8,8,128]{4,3,2,1,0:T(8,128)}, f32[8,8]{1,0:T(8,128)}, f32[8,8]{1,0:T(8,128)}) custom-call(f32[32,4,128]{2,1,0:T(4,128)S(1)} %all_to_all.5.refs_0_, bf16[3,8,128,128]{3,2,1,0:T(8,128)(2,1)S(1)} %get-tuple-element.36.high_ref.refs_1_, bf16[3,8,128,128]{3,2,1,0:T(8,128)(2,1)S(1)} %get-tuple-element.37.low_ref.refs_2_, ...), custom_call_target="tpu_custom_call" | custom-call | tf_op jit(solution)/shard_map/final/pallas_call | solution.py:543
Async XLA Ops:
  2.0 9.9 %collective-permute-start = (f32[25,8,128]{2,1,0:T(8,128)S(1)}, f32[25,8,128]{2,1,0:T(8,128)S(1)}, u32[]{:S(2)}, u32[]{:S(2)}) collective-permute-start(f32[25,8,128]{2,1,0:T(8,128)S(1)} %get-tuple-element.33), channel_id=1, source_target_pairs={{0,8},{8,16},{16,24},{24,0},{1,9},{9,17},{17,25},{25,1},{2,10},{10... | collective-permute-start | bytes 307208 | tf_op jit(solution)/shard_map/ppermute | solution.py:451
  5.0 7.0 %collective-permute-start.1 = (f32[25,8,128]{2,1,0:T(8,128)S(1)}, f32[25,8,128]{2,1,0:T(8,128)S(1)}, u32[]{:S(2)}, u32[]{:S(2)}) collective-permute-start(f32[25,8,128]{2,1,0:T(8,128)S(1)} %get-tuple-element.34), channel_id=1, source_target_pairs={{0,7},{1,2},{2,1},{3,4},{4,3},{5,6},{6,5},{7,0},{8,15},{9,10},{10,... | collective-permute-start | bytes 307208 | tf_op jit(solution)/shard_map/ppermute | solution.py:456
  7.7 4.2 %collective-permute-start.2 = (f32[25,8,128]{2,1,0:T(8,128)S(1)}, f32[25,8,128]{2,1,0:T(8,128)S(1)}, u32[]{:S(2)}, u32[]{:S(2)}) collective-permute-start(f32[25,8,128]{2,1,0:T(8,128)S(1)} %get-tuple-element.35), channel_id=1, source_target_pairs={{0,1},{1,0},{2,3},{3,2},{4,5},{5,4},{6,7},{7,6},{8,9},{9,8},{10,11... | collective-permute-start | bytes 307208 | tf_op jit(solution)/shard_map/ppermute | solution.py:456
  7.7 5.2 %collective-permute-start.3 = (f32[24,8,128]{2,1,0:T(8,128)S(1)}, f32[24,8,128]{2,1,0:T(8,128)S(1)}, u32[]{:S(2)}, u32[]{:S(2)}) collective-permute-start(f32[24,8,128]{2,1,0:T(8,128)S(1)} %get-tuple-element.39), channel_id=1, source_target_pairs={{0,24},{8,0},{16,8},{24,16},{1,25},{9,1},{17,9},{25,17},{2,26},{10... | collective-permute-start | bytes 294920 | tf_op jit(solution)/shard_map/ppermute | solution.py:451
